TPU v7x, 32 devices: a whole 2x2x4 slice. The times are simulated.
32 devices in a mesh: parts: 2 (over y), rows: 4 (over z), ex: 4 (over x, core).
Axes of the slice: x: 2, y: 2, z: 4, core: 2. Of those that a mesh axis runs over, the one named last changes fastest.
Arguments:
- hidden_acts: bfloat16 [1024, 512], P(('parts', 'ex'), 'rows'), parts along dimension 0, may hold values from -6 to 6
- cotangent: bfloat16 [1024, 4096], P(('parts', 'ex'), 'rows'), parts along dimension 0, may hold values from -0.796875 to 0.796875
- lengths: int32 [64], P('parts'), parts along dimension 0, may hold values from 1 to 64, 512 in all
- row_signs: int32 [512], P('rows'), may hold values from -1 to 1, as said below
- col_signs: int32 [4096], replicated, may hold values from -1 to 1, as said below
- feat_row: int32 [8192], replicated, may hold values from 0 to 511
- feat_col: int32 [8192], replicated, may hold values from 0 to 4095
- inverse_rows: bfloat16 [8192, 8192], P('rows'), as said below
Outputs:
- scores: bfloat16 [64, 8192], P(('parts', 'ex'), 'rows'), parts along dimension 0
There are 2 independent parts, one for each index of `parts`. A program takes and returns all parts, laid end to end along the dimension named above; an argument that names none is the same for every part. Nothing has to cross between parts.
Inputs may be any that keep to these rules, and one draw needn't show every extreme that they name: `row_signs`: every entry is -1 or +1. `col_signs`: every entry is -1 or +1. `inverse_rows`: the whole matrix equals its transpose. The lengths sum to 512 and the largest equals 64.
All inputs are finite; a program needn't handle non-finite values.
Results may differ from a plain program's by a relative error of at most 0.0049.
Values may be sent and summed in bfloat16 or wider, within the bound.
No kernel may reach another device: no remote copies, remote signals or barrier semaphores. Data moves between devices by JAX's collectives and lax.ppermute only.
A program may use at most 128 MiB of HBM per device.

v0:
```python
import math

import jax
import jax.numpy as jnp
from jax import lax
from jax.sharding import PartitionSpec as P

exact_mode = lax.Precision.HIGHEST


def hadamard(mat_size):
    indices = jnp.arange(mat_size, dtype=jnp.int32)
    common = indices[:, None] & indices[None, :]
    parity = jnp.zeros((mat_size, mat_size), jnp.int32)
    for bit_pos in range(max(mat_size.bit_length() - 1, 0)):
        parity = parity + (common >> bit_pos & 1)
    return (1 - 2 * (parity % 2)).astype(jnp.float32)


def sign_of(first_bits, second_bits, bit_count):
    parity = jnp.zeros_like(first_bits)
    for bit_pos in range(bit_count):
        parity = parity + (first_bits >> bit_pos & second_bits >> bit_pos & 1)
    return (1 - 2 * (parity % 2)).astype(jnp.float32)


def kron_signed(signed, outer_size, inner_size):
    tokens = signed.shape[0]
    shaped = signed.reshape(tokens, outer_size, inner_size)
    shaped = jnp.einsum(
        "tri,ia->tra",
        shaped,
        hadamard(inner_size).astype(jnp.bfloat16),
        preferred_element_type=jnp.float32,
    )
    shaped = jnp.einsum("tra,rh->tha", shaped, hadamard(outer_size), precision=exact_mode)
    return shaped.reshape(tokens, outer_size * inner_size)


def local(hidden_acts, cotangent, lengths, row_signs, col_signs, feat_row, feat_col, inverse_rows):
    row_count = lax.axis_size("rows")
    row_rank = lax.axis_index("rows")
    ex_group = lax.axis_index("ex")
    tok_dev = hidden_acts.shape[0]
    width_dev = hidden_acts.shape[1]
    model_width = col_signs.shape[0]
    feature_count = feat_row.shape[0]
    example_count = lengths.shape[0]
    row_bits = row_count.bit_length() - 1
    norm_scale = 1.0 / math.sqrt(width_dev * row_count * model_width)
    block_rows = min(tok_dev, 128)
    inner_width = min(model_width, 128)
    end_pos = jnp.cumsum(lengths)
    base_pos = ex_group * tok_dev
    example_ids = jnp.arange(example_count, dtype=jnp.int32)
    full_cot = lax.all_gather(cotangent, "rows", axis=1, tiled=True)
    sign_table = hadamard(width_dev) * row_signs.astype(jnp.float32)[:, None]
    left_side = jnp.dot(
        hidden_acts, sign_table.astype(jnp.bfloat16), preferred_element_type=jnp.float32
    )
    signed = full_cot * col_signs.astype(jnp.bfloat16)[None, :]
    right_side = kron_signed(signed, model_width // inner_width, inner_width)
    left_index = feat_row % width_dev
    feature_weight = sign_of(feat_row // width_dev, row_rank, row_bits) * norm_scale

    def one_block(block_id, total):
        products = jnp.take(left_side, left_index, axis=1) * jnp.take(right_side, feat_col, axis=1)
        positions = base_pos + block_id * block_rows + jnp.arange(block_rows, dtype=jnp.int32)
        owner = jnp.sum((positions[:, None] >= end_pos[None, :]).astype(jnp.int32), axis=1)
        member = (example_ids[:, None] == owner[None, :]).astype(jnp.float32)
        return total + jnp.dot(member, products, precision=exact_mode)

    summed = lax.fori_loop(
        0, tok_dev // block_rows, one_block, jnp.zeros((example_count, feature_count), jnp.float32)
    )
    phi_part = summed * feature_weight[None, :]
    by_feature = lax.psum_scatter(phi_part, "rows", scatter_dimension=1, tiled=True)
    phi_own = lax.psum_scatter(by_feature, "ex", scatter_dimension=0, tiled=True)
    phi_low = phi_own.astype(jnp.bfloat16)
    phi_all = lax.all_gather(phi_low, "rows", axis=1, tiled=True)
    scores = lax.dot_general(
        phi_all, inverse_rows, (((1,), (1,)), ((), ())), preferred_element_type=jnp.float32
    )
    return scores.astype(jnp.bfloat16)


def solution(mesh):
    placed = (
        P(("parts", "ex"), "rows"),
        P(("parts", "ex"), "rows"),
        P("parts"),
        P("rows"),
        P(),
        P(),
        P(),
        P("rows", None),
    )
    return jax.shard_map(
        local, mesh=mesh, in_specs=placed, out_specs=P(("parts", "ex"), "rows"), check_vma=False
    )
```

profile of v0, /device:TPU:0, one launch (start us, length us, event | category | flops | bytes accessed | tf_op | source)
XLA Modules:
  0.0 168.2 jit_solution(14677767108908052451)
XLA Ops:
  6.5 0.0 copy-start
  6.5 0.0 all-gather.2.cloned.1.call-start
  6.5 0.7 all-gather.2.cloned.1.call-update
  7.3 0.0 reduce-scatter.3.cloned.1.call-start
  7.3 0.7 convert_element_type.38
  8.0 0.7 convert_element_type.41
  8.7 0.7 copy.13
  9.4 0.1 reduce-window.8
  9.5 0.1 reduce
  9.6 0.8 broadcast_clamp_fusion
  10.4 0.0 copy-done
  10.4 0.3 convolution_bitcast_fusion.1
  10.7 0.0 copy-start.2
  10.7 0.0 copy-start.1
  10.7 27.7 %gather_fusion = f32[8192,128]{1,0:T(8,128)} fusion(f32[128,128]{0,1:T(8,128)S(1)} %convolution_bitcast_fusion.1, s32[8192]{0:T(1024)S(1)} %broadcast_clamp_fusion), kind=kCustom, calls=%fused_computation | custom fusion | bytes 8421376 | tf_op jit(solution)/shard_map/while/body/eval_jaxpr/jit(_take)/gather | solution.py:67
  38.4 0.1 convert_reduce_fusion
  38.5 0.0 copy-done.2
  38.5 0.0 copy-done.1
  38.5 0.1 fusion.14
  38.6 1.0 all-gather.2.cloned.1.call-done
  39.6 1.3 multiply_bitcast_fusion
  40.9 0.2 copy.16
  41.1 0.5 fusion.15
  41.6 3.2 %convolution_bitcast_fusion = f32[128,32,128]{2,1,0:T(8,128)} fusion(f32[128,32,128]{2,1,0:T(8,128)S(1)} %fusion.15), kind=kOutput, calls=%fused_computation.10 | convolution fusion | flops 201356288 | bytes 4194304 | tf_op jit(solution)/shard_map/tra,rh->tha/dot_general | solution.py:36
  44.9 2.0 %copy.15 = f32[128,32,128]{0,2,1:T(8,128)S(1)} copy(f32[128,32,128]{2,1,0:T(8,128)} %convolution_bitcast_fusion) | data formatting | bytes 4194304 | tf_op jit(solution)/shard_map/reshape | solution.py:37
  46.9 27.7 %gather_fusion.1 = f32[8192,128]{1,0:T(8,128)} fusion(f32[128,4096]{0,1:T(8,128)S(1)} %bitcast.20, s32[8192]{0:T(1024)S(1)} %fusion.22), kind=kCustom, calls=%fused_computation.1 | custom fusion | bytes 8421376 | tf_op jit(solution)/shard_map/while/body/eval_jaxpr/jit(_take)/gather | solution.py:67
  74.6 7.2 %convolution_multiply_fusion = f32[32,8192]{1,0:T(8,128)} fusion(f32[8192,128]{1,0:T(8,128)} %gather_fusion.1, f32[8192,128]{1,0:T(8,128)} %gather_fusion, pred[8192]{0:T(1024)(128)(4,1)S(1)} %get-tuple-element.23, pred[8192]{0:T(1024)(128)(4,1)S(1)} %get-tuple-element.24, f32[8192]{0:T(1024)S(1)} %fusion.14, s32[128]{0:T(128)S(1)} %convert_reduce_fusion), kind=kOutput, calls=%fused_computation.2 | convolution fusion | flops 406065152 | bytes 9486848 | tf_op jit(solution)/shard_map/while/body/eval_jaxpr/dot_general | solution.py:71
  81.8 0.0 reduce-scatter.3.cloned.1.call-update
  81.9 0.0 reduce-scatter.5.cloned.1.call-start
  81.9 29.0 %reduce-scatter.3.cloned.1.call-done = f32[32,2048]{1,0:T(8,128)} async-done(((f32[32,8192]{1,0:T(8,128)}), f32[32,2048]{1,0:T(8,128)}) %reduce-scatter.3.cloned.1.call-update) | async-done | bytes 262160 | tf_op jit(solution)/shard_map/reduce_scatter | solution.py:77
  110.9 0.0 reduce-scatter.5.cloned.1.call-update
  110.9 21.3 %reduce-scatter.5.cloned.1.call-done = f32[8,2048]{1,0:T(8,128)} async-done(((f32[32,2048]{1,0:T(8,128)}), f32[8,2048]{1,0:T(8,128)}) %reduce-scatter.5.cloned.1.call-update) | async-done | bytes 65552 | tf_op jit(solution)/shard_map/reduce_scatter | solution.py:78
  132.2 0.8 convert_element_type.44
  133.1 13.5 %all_gather.7 = bf16[8,8192]{1,0:T(8,128)(2,1)S(1)} all-gather(bf16[8,2048]{1,0:T(8,128)(2,1)S(1)} %convert_element_type.44), channel_id=1, replica_groups=mesh['parts'=2,'rows'=4,'ex'=4] {'rows'}, dimensions={1}, use_global_device_ids=true | all-gather | bytes 163840 | tf_op jit(solution)/shard_map/all_gather | solution.py:80
  146.6 15.1 %convolution_convert_fusion = bf16[8,2048]{1,0:T(8,128)(2,1)} fusion(bf16[8,8192]{1,0:T(8,128)(2,1)S(1)} %all_gather.7, bf16[2048,8192]{1,0:T(8,128)(2,1)} %param.15), kind=kOutput, calls=%fused_computation.6 | convolution fusion | flops 268451840 | bytes 33718272 | tf_op jit(solution)/shard_map/dot_general | solution.py:81
  (3 shorter events, 0.1 us)
Async XLA Ops:
  6.5 3.9 %copy-start = (bf16[128,128]{1,0:T(8,128)(2,1)S(1)}, bf16[128,128]{1,0:T(8,128)(2,1)}, u32[]{:S(2)}) copy-start(bf16[128,128]{1,0:T(8,128)(2,1)} %param.8) | copy-start | bytes 98308
  6.5 33.1 %all-gather.2.cloned.1.call-start = ((), (), s32[]{:S(2)}) async-start(), calls=%async_computation.2 | async-start | bytes 1310720 | tf_op jit(solution)/shard_map/all_gather | solution.py:56
  7.3 103.6 %reduce-scatter.3.cloned.1.call-start = ((), (), s32[]{:S(2)}) async-start(), calls=%async_computation.3 | async-start | bytes 1310720 | tf_op jit(solution)/shard_map/reduce_scatter | solution.py:77
  10.7 27.8 %copy-start.2 = (s32[8192]{0:T(1024)S(1)}, s32[8192]{0:T(1024)}, u32[]{:S(2)}) copy-start(s32[8192]{0:T(1024)} %param.14) | copy-start | bytes 98308
  10.7 27.8 %copy-start.1 = (s32[8192]{0:T(1024)S(1)}, s32[8192]{0:T(1024)}, u32[]{:S(2)}) copy-start(s32[8192]{0:T(1024)} %param.13) | copy-start | bytes 98308
  81.9 50.4 %reduce-scatter.5.cloned.1.call-start = ((), (), s32[]{:S(2)}) async-start(), calls=%async_computation.4 | async-start | bytes 327680 | tf_op jit(solution)/shard_map/reduce_scatter | solution.py:78
Sparse Core Ops, SparseCore 0:
  8.9 30.6 all-gather.1
  82.0 28.8 reduce-scatter.2
  113.5 18.6 reduce-scatter.4
where the time goes:
time: 169 us; the launch traced here: 168 us
  local copies, waits for them, and re-layouts  58.4 us (35%)
  waiting for transfers between devices  52 us (31%)
  matrix products  26.3 us (16%)
  blocking collectives  13.5 us (8%)
  between operations  13.2 us (8%)
  other arithmetic  4.68 us (3%)
    reduce_scatter x1, waiting for transfers between devices, local(): lax.psum_scatter(phi_part, 'rows', scatter_dimension=1, tiled=True)  29 us
    gather x1, local copies, waits for them, and re-layouts, one_block(): jnp.take(right_side, feat_col, axis=1)  27.7 us
    gather x1, local copies, waits for them, and re-layouts, one_block(): jnp.take(left_side, left_index, axis=1)  27.7 us
    reduce_scatter x1, waiting for transfers between devices, local(): lax.psum_scatter(by_feature, 'ex', scatter_dimension=0, tiled=True)  21.3 us
    dot_general x1, matrix products, local(): lax.dot_general(phi_all, inverse_rows, (((1,), (1,)), ((), ())), preferre...  15.1 us
    all_gather x1, blocking collectives, local(): phi_all = lax.all_gather(phi_low, 'rows', axis=1, tiled=True)  13.5 us
    dot_general x1, matrix products, one_block(): return total + jnp.dot(member, products, precision=exact_mode)  7.22 us
  transfers between devices with their start and end apart: 3, of which 3 were waited for; matrix products, arithmetic and copies ran while one was open for 19% of the time, Pallas kernels for 0%

commit v1 on v0

v1 whole, which is shorter than its diff:
```python
import functools
import math

import jax
import jax.numpy as jnp
from jax import lax
from jax.experimental import pallas as pl
from jax.experimental.pallas import tpu as pltpu
from jax.sharding import PartitionSpec as P

f32 = jnp.float32
bf16 = jnp.bfloat16
contract_last = (((1,), (1,)), ((), ()))
vmem_bytes = 30 * 2**20


def swap(values, axis, mask):
    size = lax.axis_size(axis)
    return lax.ppermute(values, axis, [(rank, rank ^ mask) for rank in range(size)])


def bit_sign(index, bit_pos):
    return (1 - 2 * (index >> bit_pos & 1)).astype(f32)


def parity_sign(bits, bit_count):
    parity = bits & 1
    for bit_pos in range(1, bit_count):
        parity = parity ^ (bits >> bit_pos & 1)
    return (1 - 2 * parity).astype(f32)


def sign_columns(index, size):
    columns = index.shape[1]
    first = min(size, 16)
    row_id = lax.broadcasted_iota(jnp.int32, (first, columns), 0)
    first_bits = first.bit_length() - 1
    table = parity_sign(row_id & index, first_bits).astype(bf16)
    for bit_pos in range(first_bits, size.bit_length() - 1):
        table = jnp.concatenate([table, table * bit_sign(index, bit_pos).astype(bf16)], axis=0)
    return table


def index_row(ref, start, count):
    rows = [ref[pl.ds(start + step, 1), :] for step in range(count)]
    return jnp.concatenate(rows, axis=1)


def cot_products(values, index, block):
    size = values.shape[1]
    base_size = min(size, block)
    base = sign_columns(index, base_size)
    total = None
    for part in range(size // base_size):
        table = base
        if part > 0:
            sign = parity_sign((index // base_size) & part, (size // base_size).bit_length() - 1)
            table = base * sign.astype(bf16)
        piece = jnp.dot(
            values[:, part * base_size : (part + 1) * base_size], table, preferred_element_type=f32
        )
        total = piece if total is None else total + piece
    return total


def right_kernel(is_own, row_count, cot_ref, sign_ref, col_ref, *refs):
    out_ref = refs[-1]
    rank = lax.axis_index("rows")
    block_id = rank if is_own else rank ^ 1
    width = cot_ref.shape[1]
    model_sign = sign_ref[pl.ds(block_id, 1), :].astype(bf16)
    values = cot_ref[...] * model_sign
    lanes = col_ref.shape[1]
    half_rows = col_ref.shape[0] // 2
    first_row = (rank & 1) * half_rows
    columns = out_ref.shape[2]
    group = min(4, columns // lanes)
    row_bits = row_count.bit_length() - 1
    for step in range(half_rows // group):
        index = index_row(col_ref, first_row + step * group, group)
        local_index = index % width
        part = cot_products(values, local_index, 256)
        part = part * parity_sign((index // width) & block_id, row_bits)
        half = step * group * lanes // columns
        at = step * group * lanes % columns
        if not is_own:
            part = part + refs[0][half, :, at : at + group * lanes]
        out_ref[half, :, at : at + group * lanes] = part


def feature_kernel(flip, row_count, hidden_refs, right_ref, row_ref, len_ref, out_ref):
    rank = lax.axis_index("rows")
    ex_rank = lax.axis_index("ex")
    ex_count = lax.axis_size("ex")
    half = (ex_rank & 1) ^ flip
    tokens = right_ref.shape[1]
    width = hidden_refs[0].shape[1]
    examples = out_ref.shape[0]
    lanes = row_ref.shape[1]
    quarter_rows = row_ref.shape[0] // 4
    first_row = ((rank & 1) * 2 + half) * quarter_rows
    row_bits = row_count.bit_length() - 1
    own = examples // ex_count
    shape = (examples, examples)
    row_id = lax.broadcasted_iota(jnp.int32, shape, 0)
    example = ((row_id // own) ^ (ex_rank & ~1) ^ (ex_count - 2)) * own + row_id % own
    other = lax.broadcasted_iota(jnp.int32, shape, 1)
    counts = jnp.broadcast_to(len_ref[...], shape)
    ends = jnp.sum(jnp.where(other <= example, counts, 0), axis=1, keepdims=True)
    starts = jnp.sum(jnp.where(other < example, counts, 0), axis=1, keepdims=True)
    position = ex_rank * tokens + lax.broadcasted_iota(jnp.int32, (examples, tokens), 1)
    member = jnp.logical_and(position >= starts, position < ends).astype(f32).astype(bf16)
    group = min(4, quarter_rows)
    for step in range(quarter_rows // group):
        index = index_row(row_ref, first_row + step * group, group)
        base = sign_columns(index % width, width)
        high = index // width
        left = None
        offset = 0
        for ref in hidden_refs:
            blocks = ref.shape[0]
            for block in range(blocks):
                block_id = rank ^ (offset + block)
                table = base * parity_sign(high & block_id, row_bits).astype(bf16)
                piece = jnp.dot(ref[block], table, preferred_element_type=f32)
                left = piece if left is None else left + piece
            offset += blocks
        columns = slice(step * group * lanes, (step + 1) * group * lanes)
        product = left * right_ref[half, :, columns]
        high_part = product.astype(bf16)
        low_part = (product - high_part.astype(f32)).astype(bf16)
        out_ref[:, columns] = jnp.dot(member, high_part, preferred_element_type=f32) + jnp.dot(
            member, low_part, preferred_element_type=f32
        )


def score_kernel(is_own, low_ref, matrix_ref, *refs):
    if is_own:
        out_ref, held, sems = refs
    else:
        sum_ref, send_ref, keep_ref, held, sems = refs
    rank = lax.axis_index("rows")
    ex_rank = lax.axis_index("ex")
    depth = low_ref.shape[1]
    half = (rank & 1) if is_own else (rank & 1) ^ 1
    first = pl.multiple_of((half * 2 + (ex_rank & 1)) * depth, depth)
    pieces, rows = held.shape[0], held.shape[1]
    copies = []
    for piece in range(pieces):
        copy = pltpu.make_async_copy(
            matrix_ref.at[pl.ds(piece * rows, rows), pl.ds(first, depth)],
            held.at[piece],
            sems.at[piece],
        )
        copy.start()
        copies.append(copy)
    low = low_ref[...]
    own = low.shape[0] // 2
    for piece in range(pieces):
        copies[piece].wait()
        part = lax.dot_general(low, held[piece], contract_last, preferred_element_type=f32)
        columns = slice(piece * rows, (piece + 1) * rows)
        if is_own:
            out_ref[:, columns] = part
        else:
            part = part + sum_ref[:, columns]
            lower = (ex_rank & 1) == 0
            keep_ref[:, columns] = jnp.where(lower, part[:own], part[own:])
            send_ref[:, columns] = jnp.where(lower, part[own:], part[:own])


def local(hidden_acts, cotangent, lengths, row_signs, col_signs, feat_row, feat_col, inverse_rows):
    row_count = lax.axis_size("rows")
    ex_count = lax.axis_size("ex")
    tokens, width = hidden_acts.shape
    model_width = col_signs.shape[0]
    feature_count = feat_row.shape[0]
    example_count = lengths.shape[0]
    quarter = feature_count // 4
    own_examples = example_count // ex_count
    norm_scale = 1.0 / math.sqrt(width * row_count * model_width)
    whole = pl.BlockSpec(memory_space=pltpu.VMEM)
    params = pltpu.CompilerParams(vmem_limit_bytes=vmem_bytes)

    signed = hidden_acts * row_signs.astype(bf16)[None, :]
    hidden_parts = [signed[None]]
    near = swap(signed[None], "rows", 1)
    near_cot = swap(cotangent, "rows", 1)
    hidden_parts.append(near)
    step = 2
    while step < row_count:
        held = jnp.concatenate(hidden_parts, axis=0)
        hidden_parts = [held, swap(held, "rows", step)]
        step *= 2

    col_table = col_signs.reshape(row_count, model_width // row_count)
    col_index = feat_col.reshape(-1, 128)
    row_index = feat_row.reshape(-1, 128)
    right_shape = jax.ShapeDtypeStruct((2, tokens, quarter), f32)
    right = pl.pallas_call(
        functools.partial(right_kernel, True, row_count),
        out_shape=right_shape,
        in_specs=[whole] * 3,
        out_specs=whole,
        compiler_params=params,
    )(cotangent, col_table, col_index)
    right = pl.pallas_call(
        functools.partial(right_kernel, False, row_count),
        out_shape=right_shape,
        in_specs=[whole] * 4,
        out_specs=whole,
        compiler_params=params,
    )(near_cot, col_table, col_index, right)

    def features(flip):
        def kernel(*refs):
            feature_kernel(flip, row_count, refs[: len(hidden_parts)], *refs[len(hidden_parts) :])

        return pl.pallas_call(
            kernel,
            out_shape=jax.ShapeDtypeStruct((example_count, quarter), f32),
            in_specs=[whole] * (len(hidden_parts) + 3),
            out_specs=whole,
            compiler_params=params,
        )(*hidden_parts, right, row_index, lengths.reshape(1, example_count))

    total = swap(features(1), "ex", 1) + features(0)
    mask = ex_count // 2
    while mask > 1:
        half = total.shape[0] // 2
        total = total[half:] + swap(total[:half].astype(bf16), "ex", mask).astype(f32)
        mask //= 2
    step = 2
    while step < row_count:
        total = total + swap(total.astype(bf16), "rows", step).astype(f32)
        step *= 2
    low = (total * norm_scale).astype(bf16)
    near_low = swap(low, "rows", 1)

    out_rows = inverse_rows.shape[0]
    pieces = max(out_rows // 256, 1)
    scratch = [
        pltpu.VMEM((pieces, out_rows // pieces, quarter), bf16),
        pltpu.SemaphoreType.DMA((pieces,)),
    ]
    anywhere = pl.BlockSpec(memory_space=pl.ANY)
    part = pl.pallas_call(
        functools.partial(score_kernel, True),
        out_shape=jax.ShapeDtypeStruct((2 * own_examples, out_rows), f32),
        in_specs=[whole, anywhere],
        out_specs=whole,
        scratch_shapes=scratch,
        compiler_params=params,
    )(low, inverse_rows)
    own_shape = jax.ShapeDtypeStruct((own_examples, out_rows), f32)
    send, keep = pl.pallas_call(
        functools.partial(score_kernel, False),
        out_shape=(own_shape, own_shape),
        in_specs=[whole, anywhere, whole],
        out_specs=(whole, whole),
        scratch_shapes=scratch,
        compiler_params=params,
    )(near_low, inverse_rows, part)
    return (keep + swap(send, "ex", 1)).astype(bf16)


def solution(mesh):
    placed = (
        P(("parts", "ex"), "rows"),
        P(("parts", "ex"), "rows"),
        P("parts"),
        P("rows"),
        P(),
        P(),
        P(),
        P("rows", None),
    )
    return jax.shard_map(
        local, mesh=mesh, in_specs=placed, out_specs=P(("parts", "ex"), "rows"), check_vma=False
    )
```

time: 169 us -> 48.5 us (0.29)
  local copies, waits for them, and re-layouts: 58.4 us -> 2.46 us
  waiting for transfers between devices: 52 us -> 15.5 us
  matrix products: 26.3 us -> 0 us
  Pallas kernels: 0 us -> 18.9 us
  blocking collectives: 13.5 us -> 0 us
  between operations: 13.2 us -> 0.14 us
  starting transfers between devices: 0.08 us -> 9 us
  other arithmetic: 4.68 us -> 2.15 us
    gather x2 -> x0, local copies, waits for them, and re-layouts: 55.4 us -> none  [the longest x1 27.7 us: one_block(): jnp.take(right_side, feat_col, axis=1)]
    reduce_scatter x2 -> x0, waiting for transfers between devices: 50.3 us -> none  [the longest x1 29 us: local(): lax.psum_scatter(phi_part, 'rows', scatter_dimension=1, tiled=True)]
    dot_general x5 -> x0, matrix products: 26.3 us -> none  [the longest x1 15.1 us: local(): lax.dot_general(phi_all, inverse_rows, (((1,), (1,)), ((), ())), preferre...]
    pallas_call x0 -> x6, Pallas kernels: none -> 18.9 us  [the longest x1 6.58 us: local(): pl.pallas_call(functools.partial(score_kernel, False), out_shape=(own_sha...]
    ppermute x0 -> x8, waiting for transfers between devices: none -> 15.5 us  [swap(): lax.ppermute(values, axis, [(rank, rank ^ mask) for rank in range(size)])]
    all_gather x1 -> x0, blocking collectives: 13.5 us -> none  [local(): phi_all = lax.all_gather(phi_low, 'rows', axis=1, tiled=True)]
    ppermute x0 -> x8, starting transfers between devices: none -> 9 us  [swap(): lax.ppermute(values, axis, [(rank, rank ^ mask) for rank in range(size)])]
  transfers between devices with their start and end apart: 3 -> 8, of which waited for: 3 -> 5; matrix products, arithmetic and copies ran while one was open for 19% -> 4% of each run, Pallas kernels for 0% -> 22%
where the time goes in v1:
time: 48.5 us; the launch traced here: 48.2 us
  Pallas kernels  18.9 us (39%)
  waiting for transfers between devices  15.5 us (32%)
  starting transfers between devices  9 us (19%)
  local copies, waits for them, and re-layouts  2.46 us (5%)
  other arithmetic  2.15 us (4%)
    ppermute x8, waiting for transfers between devices, swap(): lax.ppermute(values, axis, [(rank, rank ^ mask) for rank in range(size)])  15.5 us
    ppermute x8, starting transfers between devices, swap(): lax.ppermute(values, axis, [(rank, rank ^ mask) for rank in range(size)])  9 us
    pallas_call x1, Pallas kernels, local(): pl.pallas_call(functools.partial(score_kernel, False), out_shape=(own_sha...  6.58 us
    pallas_call x1, Pallas kernels, local(): pl.pallas_call(functools.partial(score_kernel, True), out_shape=jax.Shape...  6.56 us
    pallas_call x2, Pallas kernels, features(): pl.pallas_call(kernel, out_shape=jax.ShapeDtypeStruct((example_count, qua...  2.88 us
    unnamed x8, local copies, waits for them, and re-layouts  1.72 us
    pallas_call x1, Pallas kernels, local(): pl.pallas_call(functools.partial(right_kernel, False, row_count), out_sha...  1.47 us
    pallas_call x1, Pallas kernels, local(): pl.pallas_call(functools.partial(right_kernel, True, row_count), out_shap...  1.39 us
  transfers between devices with their start and end apart: 8, of which 5 were waited for; matrix products, arithmetic and copies ran while one was open for 4% of the time, Pallas kernels for 22%

profile of v1, /device:TPU:0, one launch (start us, length us, event | category | flops | bytes accessed | tf_op | source)
XLA Modules:
  0.0 48.2 jit_solution(16525051880063135644)
XLA Ops:
  0.0 3.0 %collective-permute-start.2 = (bf16[128,1024]{1,0:T(8,128)(2,1)}, bf16[128,1024]{1,0:T(8,128)(2,1)S(1)}, u32[]{:S(2)}, u32[]{:S(2)}) collective-permute-start(bf16[128,1024]{1,0:T(8,128)(2,1)} %cot_ref.1), channel_id=1, source_target_pairs={{0,4},{4,0},{8,12},{12,8},{1,5},{5,1},{9,13},{13,9},{2,6},{6,2},{1... | collective-permute-start | bytes 786440 | tf_op jit(solution)/shard_map/ppermute | solution.py:19
  3.0 0.7 %convert_element_type.19 = bf16[128]{0:T(256)(128)(2,1)S(1)} convert(s32[128]{0:T(128)} %param.11) | non-fusion elementwise | flops 128 | bytes 768 | tf_op jit(solution)/shard_map/convert_element_type | solution.py:185
  3.7 0.8 %multiply_bitcast_fusion = bf16[1,128,128]{2,1,0:T(8,128)(2,1)S(1)} fusion(bf16[128,128]{1,0:T(8,128)(2,1)} %param.8, bf16[128]{0:T(256)(128)(2,1)S(1)} %convert_element_type.19), kind=kLoop, calls=%fused_computation.6 | loop fusion | flops 16384 | bytes 65792 | tf_op jit(solution)/shard_map/broadcast_in_dim | solution.py:186
  4.4 0.0 collective-permute-start
  4.5 5.8 %collective-permute-done = bf16[1,128,128]{2,1,0:T(8,128)(2,1)S(1)} collective-permute-done((bf16[1,128,128]{2,1,0:T(8,128)(2,1)S(1)}, bf16[1,128,128]{2,1,0:T(8,128)(2,1)S(1)}, u32[]{:S(2)}, u32[]{:S(2)}) %collective-permute-start) | collective-permute-done | bytes 32800 | tf_op jit(solution)/shard_map/ppermute | solution.py:19
  10.3 2.8 %collective-permute-start.1 = (bf16[2,128,128]{2,1,0:T(8,128)(2,1)S(1)}, bf16[2,128,128]{2,1,0:T(8,128)(2,1)S(1)}, u32[]{:S(2)}, u32[]{:S(2)}) collective-permute-start(bf16[2,128,128]{2,1,0:T(8,128)(2,1)S(1)} %pad_maximum_fusion.refs_0_), channel_id=1, source_target_pairs={{0,8},{4,12},{8,0},{12,4},{1,9},{5,13},{9,1},{13,5},{2,10},{6,14},... | collective-permute-start | bytes 196616 | tf_op jit(solution)/shard_map/ppermute | solution.py:19
  13.1 0.7 %reshape.14.sign_ref = s32[4,1024]{1,0:T(4,128)S(1)} reshape(s32[4096]{0:T(1024)} %param.12) | data formatting | bytes 32768 | tf_op jit(solution)/shard_map/reshape | solution.py:196
  13.8 0.0 copy-start
  13.8 0.9 %copy-done = bf16[128,1024]{1,0:T(8,128)(2,1)S(1)} copy-done((bf16[128,1024]{1,0:T(8,128)(2,1)S(1)}, bf16[128,1024]{1,0:T(8,128)(2,1)}, u32[]{:S(2)}) %copy-start) | copy-done | bytes 262168
  14.8 0.0 copy-start.1
  14.8 0.8 %copy-done.1 = s32[8192]{0:T(1024)S(1)} copy-done((s32[8192]{0:T(1024)S(1)}, s32[8192]{0:T(1024)}, u32[]{:S(2)}) %copy-start.1) | copy-done | bytes 32792
  15.5 1.4 %shard_map.82.refs_0_ = f32[2,128,2048]{2,1,0:T(8,128)S(1)} custom-call(bf16[128,1024]{1,0:T(8,128)(2,1)S(1)} %copy-done, s32[4,1024]{1,0:T(4,128)S(1)} %reshape.14.sign_ref, s32[64,128]{1,0:T(8,128)S(1)} %bitcast.5), custom_call_target="tpu_custom_call" | custom-call | tf_op jit(solution)/shard_map/pallas_call | solution.py:200
  16.9 0.0 copy-start.2
  16.9 0.0 copy-start.3
  16.9 0.0 collective-permute-done.2.cot_ref
  16.9 1.5 %shard_map.83.refs_2_ = f32[2,128,2048]{2,1,0:T(8,128)S(1)} custom-call(bf16[128,1024]{1,0:T(8,128)(2,1)S(1)} %collective-permute-done.2.cot_ref, s32[4,1024]{1,0:T(4,128)S(1)} %reshape.14.sign_ref, s32[64,128]{1,0:T(8,128)S(1)} %bitcast.6, f32[2,128,2048]{2,1,0:T(8,128)S(1)} %shard_map.82.refs_0_), custom_call_target="tpu_custom_call" | custom-call | tf_op jit(solution)/shard_map/pallas_call | solution.py:207
  18.4 0.0 collective-permute-done.1.refs_1_
  18.4 0.0 copy-done.2
  18.4 0.0 copy-done.3
  18.5 1.5 %shard_map.84 = f32[32,2048]{1,0:T(8,128)S(1)} custom-call(bf16[2,128,128]{2,1,0:T(8,128)(2,1)S(1)} %pad_maximum_fusion.refs_0_, bf16[2,128,128]{2,1,0:T(8,128)(2,1)S(1)} %collective-permute-done.1.refs_1_, f32[2,128,2048]{2,1,0:T(8,128)S(1)} %shard_map.83.refs_2_, s32[64,128]{1,0:T(8,128)S(1)} %bitcast.7, s32[1,32]{1,0:T(1,128)S(1)} %bitcast.9), custom_call_target="tpu_custom_call" | custom-call | tf_op jit(solution)/shard_map/pallas_call | solution.py:219
  19.9 0.0 collective-permute-start.3
  19.9 1.4 %shard_map.85 = f32[32,2048]{1,0:T(8,128)S(1)} custom-call(bf16[2,128,128]{2,1,0:T(8,128)(2,1)S(1)} %pad_maximum_fusion.refs_0_, bf16[2,128,128]{2,1,0:T(8,128)(2,1)S(1)} %collective-permute-done.1.refs_1_, f32[2,128,2048]{2,1,0:T(8,128)S(1)} %shard_map.83.refs_2_, s32[64,128]{1,0:T(8,128)S(1)} %bitcast.8, s32[1,32]{1,0:T(1,128)S(1)} %bitcast.10), custom_call_target="tpu_custom_call" | custom-call | tf_op jit(solution)/shard_map/pallas_call | solution.py:219
  21.4 0.1 collective-permute-done.3
  21.5 1.6 %collective-permute-start.4 = (bf16[16,2048]{1,0:T(8,128)(2,1)S(1)}, bf16[16,2048]{1,0:T(8,128)(2,1)S(1)}, u32[]{:S(2)}, u32[]{:S(2)}) collective-permute-start(bf16[16,2048]{1,0:T(8,128)(2,1)S(1)} %slice.17), channel_id=1, source_target_pairs={{0,2},{1,3},{2,0},{3,1},{4,6},{5,7},{6,4},{7,5},{8,10},{9,11},{10,... | collective-permute-start | bytes 196616 | tf_op jit(solution)/shard_map/ppermute | solution.py:19
  23.1 2.9 %collective-permute-done.4 = bf16[16,2048]{1,0:T(8,128)(2,1)S(1)} collective-permute-done((bf16[16,2048]{1,0:T(8,128)(2,1)S(1)}, bf16[16,2048]{1,0:T(8,128)(2,1)S(1)}, u32[]{:S(2)}, u32[]{:S(2)}) %collective-permute-start.4) | collective-permute-done | bytes 65568 | tf_op jit(solution)/shard_map/ppermute | solution.py:19
  26.1 0.2 collective-permute-start.5
  26.3 5.4 %collective-permute-done.5 = bf16[16,2048]{1,0:T(8,128)(2,1)S(1)} collective-permute-done((bf16[16,2048]{1,0:T(8,128)(2,1)S(1)}, bf16[16,2048]{1,0:T(8,128)(2,1)S(1)}, u32[]{:S(2)}, u32[]{:S(2)}) %collective-permute-start.5) | collective-permute-done | bytes 65568 | tf_op jit(solution)/shard_map/ppermute | solution.py:19
  31.7 1.3 %collective-permute-start.6 = (bf16[16,2048]{1,0:T(8,128)(2,1)S(1)}, bf16[16,2048]{1,0:T(8,128)(2,1)S(1)}, u32[]{:S(2)}, u32[]{:S(2)}) collective-permute-start(bf16[16,2048]{1,0:T(8,128)(2,1)S(1)} %multiply_convert_fusion.low_ref), channel_id=1, source_target_pairs={{0,4},{4,0},{8,12},{12,8},{1,5},{5,1},{9,13},{13,9},{2,6},{6,2},{1... | collective-permute-start | bytes 196616 | tf_op jit(solution)/shard_map/ppermute | solution.py:19
  33.1 6.6 %shard_map.86.refs_0_ = f32[16,2048]{1,0:T(8,128)S(1)} custom-call(bf16[16,2048]{1,0:T(8,128)(2,1)S(1)} %multiply_convert_fusion.low_ref, bf16[2048,8192]{1,0:T(8,128)(2,1)} %matrix_ref.3), custom_call_target="tpu_custom_call" | custom-call | tf_op jit(solution)/shard_map/pallas_call | solution.py:247
  39.6 0.0 collective-permute-done.6.low_ref
  39.6 6.6 %shard_map.87 = (f32[8,2048]{1,0:T(8,128)S(1)}, f32[8,2048]{1,0:T(8,128)S(1)}) custom-call(bf16[16,2048]{1,0:T(8,128)(2,1)S(1)} %collective-permute-done.6.low_ref, bf16[2048,8192]{1,0:T(8,128)(2,1)} %matrix_ref.3, f32[16,2048]{1,0:T(8,128)S(1)} %shard_map.86.refs_0_), custom_call_target="tpu_custom_call" | custom-call | tf_op jit(solution)/shard_map/pallas_call | solution.py:256
  46.2 0.1 collective-permute-start.7
  46.3 1.2 %collective-permute-done.7 = f32[8,2048]{1,0:T(8,128)S(1)} collective-permute-done((f32[8,2048]{1,0:T(8,128)S(1)}, f32[8,2048]{1,0:T(8,128)S(1)}, u32[]{:S(2)}, u32[]{:S(2)}) %collective-permute-start.7) | collective-permute-done | bytes 65568 | tf_op jit(solution)/shard_map/ppermute | solution.py:19
  47.5 0.6 %add_convert_fusion = bf16[8,2048]{1,0:T(8,128)(2,1)} fusion(f32[8,2048]{1,0:T(8,128)S(1)} %get-tuple-element.7, f32[8,2048]{1,0:T(8,128)S(1)} %collective-permute-done.7), kind=kLoop, calls=%fused_computation.5 | loop fusion | flops 32768 | bytes 163840 | tf_op jit(solution)/shard_map/convert_element_type | solution.py:264
  (5 shorter events, 0.1 us)
Async XLA Ops:
  0.0 16.9 %collective-permute-start.2 = (bf16[128,1024]{1,0:T(8,128)(2,1)}, bf16[128,1024]{1,0:T(8,128)(2,1)S(1)}, u32[]{:S(2)}, u32[]{:S(2)}) collective-permute-start(bf16[128,1024]{1,0:T(8,128)(2,1)} %cot_ref.1), channel_id=1, source_target_pairs={{0,4},{4,0},{8,12},{12,8},{1,5},{5,1},{9,13},{13,9},{2,6},{6,2},{1... | collective-permute-start | bytes 786440 | tf_op jit(solution)/shard_map/ppermute | solution.py:19
  4.4 5.8 %collective-permute-start = (bf16[1,128,128]{2,1,0:T(8,128)(2,1)S(1)}, bf16[1,128,128]{2,1,0:T(8,128)(2,1)S(1)}, u32[]{:S(2)}, u32[]{:S(2)}) collective-permute-start(bf16[1,128,128]{2,1,0:T(8,128)(2,1)S(1)} %multiply_bitcast_fusion), channel_id=1, source_target_pairs={{0,4},{4,0},{8,12},{12,8},{1,5},{5,1},{9,13},{13,9},{2,6},{6,2},{1... | collective-permute-start | bytes 98312 | tf_op jit(solution)/shard_map/ppermute | solution.py:19
  10.3 8.2 %collective-permute-start.1 = (bf16[2,128,128]{2,1,0:T(8,128)(2,1)S(1)}, bf16[2,128,128]{2,1,0:T(8,128)(2,1)S(1)}, u32[]{:S(2)}, u32[]{:S(2)}) collective-permute-start(bf16[2,128,128]{2,1,0:T(8,128)(2,1)S(1)} %pad_maximum_fusion.refs_0_), channel_id=1, source_target_pairs={{0,8},{4,12},{8,0},{12,4},{1,9},{5,13},{9,1},{13,5},{2,10},{6,14},... | collective-permute-start | bytes 196616 | tf_op jit(solution)/shard_map/ppermute | solution.py:19
  13.8 0.9 %copy-start = (bf16[128,1024]{1,0:T(8,128)(2,1)S(1)}, bf16[128,1024]{1,0:T(8,128)(2,1)}, u32[]{:S(2)}) copy-start(bf16[128,1024]{1,0:T(8,128)(2,1)} %cot_ref.1) | copy-start | bytes 786436
  14.8 0.8 %copy-start.1 = (s32[8192]{0:T(1024)S(1)}, s32[8192]{0:T(1024)}, u32[]{:S(2)}) copy-start(s32[8192]{0:T(1024)} %param.14) | copy-start | bytes 98308
  16.9 1.5 %copy-start.2 = (s32[8192]{0:T(1024)S(1)}, s32[8192]{0:T(1024)}, u32[]{:S(2)}) copy-start(s32[8192]{0:T(1024)} %param.13) | copy-start | bytes 98308
  16.9 1.5 %copy-start.3 = (s32[32]{0:T(128)S(1)}, s32[32]{0:T(128)}, u32[]{:S(2)}) copy-start(s32[32]{0:T(128)} %param.10) | copy-start | bytes 388
  19.9 1.6 %collective-permute-start.3 = (f32[32,2048]{1,0:T(8,128)S(1)}, f32[32,2048]{1,0:T(8,128)S(1)}, u32[]{:S(2)}, u32[]{:S(2)}) collective-permute-start(f32[32,2048]{1,0:T(8,128)S(1)} %shard_map.84), channel_id=1, source_target_pairs={{0,1},{1,0},{2,3},{3,2},{4,5},{5,4},{6,7},{7,6},{8,9},{9,8},{10,11... | collective-permute-start | bytes 786440 | tf_op jit(solution)/shard_map/ppermute | solution.py:19
  21.5 4.5 %collective-permute-start.4 = (bf16[16,2048]{1,0:T(8,128)(2,1)S(1)}, bf16[16,2048]{1,0:T(8,128)(2,1)S(1)}, u32[]{:S(2)}, u32[]{:S(2)}) collective-permute-start(bf16[16,2048]{1,0:T(8,128)(2,1)S(1)} %slice.17), channel_id=1, source_target_pairs={{0,2},{1,3},{2,0},{3,1},{4,6},{5,7},{6,4},{7,5},{8,10},{9,11},{10,... | collective-permute-start | bytes 196616 | tf_op jit(solution)/shard_map/ppermute | solution.py:19
  26.1 5.6 %collective-permute-start.5 = (bf16[16,2048]{1,0:T(8,128)(2,1)S(1)}, bf16[16,2048]{1,0:T(8,128)(2,1)S(1)}, u32[]{:S(2)}, u32[]{:S(2)}) collective-permute-start(bf16[16,2048]{1,0:T(8,128)(2,1)S(1)} %fusion), channel_id=1, source_target_pairs={{0,8},{4,12},{8,0},{12,4},{1,9},{5,13},{9,1},{13,5},{2,10},{6,14},... | collective-permute-start | bytes 196616 | tf_op jit(solution)/shard_map/ppermute | solution.py:19
  31.7 7.9 %collective-permute-start.6 = (bf16[16,2048]{1,0:T(8,128)(2,1)S(1)}, bf16[16,2048]{1,0:T(8,128)(2,1)S(1)}, u32[]{:S(2)}, u32[]{:S(2)}) collective-permute-start(bf16[16,2048]{1,0:T(8,128)(2,1)S(1)} %multiply_convert_fusion.low_ref), channel_id=1, source_target_pairs={{0,4},{4,0},{8,12},{12,8},{1,5},{5,1},{9,13},{13,9},{2,6},{6,2},{1... | collective-permute-start | bytes 196616 | tf_op jit(solution)/shard_map/ppermute | solution.py:19
  46.2 1.3 %collective-permute-start.7 = (f32[8,2048]{1,0:T(8,128)S(1)}, f32[8,2048]{1,0:T(8,128)S(1)}, u32[]{:S(2)}, u32[]{:S(2)}) collective-permute-start(f32[8,2048]{1,0:T(8,128)S(1)} %get-tuple-element.8), channel_id=1, source_target_pairs={{0,1},{1,0},{2,3},{3,2},{4,5},{5,4},{6,7},{7,6},{8,9},{9,8},{10,11... | collective-permute-start | bytes 196616 | tf_op jit(solution)/shard_map/ppermute | solution.py:19

commit v2 on v1

v2 whole, which is shorter than its diff:
```python
import functools
import math

import jax
import jax.numpy as jnp
from jax import lax
from jax.experimental import pallas as pl
from jax.experimental.pallas import tpu as pltpu
from jax.sharding import PartitionSpec as P

f32 = jnp.float32
bf16 = jnp.bfloat16
contract_last = (((1,), (1,)), ((), ()))
vmem_bytes = 14 * 2**20


def in_hbm(values):
    return pltpu.with_memory_space_constraint(values, pltpu.HBM)


def swap(values, axis, mask):
    size = lax.axis_size(axis)
    return lax.ppermute(values, axis, [(rank, rank ^ mask) for rank in range(size)])


def bit_sign(index, bit_pos):
    return (1 - 2 * (index >> bit_pos & 1)).astype(f32)


def parity_sign(bits, bit_count):
    parity = bits & 1
    for bit_pos in range(1, bit_count):
        parity = parity ^ (bits >> bit_pos & 1)
    return (1 - 2 * parity).astype(f32)


def sign_columns(index, size):
    columns = index.shape[1]
    first = min(size, 16)
    row_id = lax.broadcasted_iota(jnp.int32, (first, columns), 0)
    first_bits = first.bit_length() - 1
    table = parity_sign(row_id & index, first_bits).astype(bf16)
    for bit_pos in range(first_bits, size.bit_length() - 1):
        table = jnp.concatenate([table, table * bit_sign(index, bit_pos).astype(bf16)], axis=0)
    return table


def index_row(ref, start, count):
    rows = [ref[pl.ds(start + step, 1), :] for step in range(count)]
    return jnp.concatenate(rows, axis=1)


def cot_products(values, index, block):
    size = values.shape[1]
    base_size = min(size, block)
    base = sign_columns(index, base_size)
    total = None
    for part in range(size // base_size):
        table = base
        if part > 0:
            sign = parity_sign((index // base_size) & part, (size // base_size).bit_length() - 1)
            table = base * sign.astype(bf16)
        piece = jnp.dot(
            values[:, part * base_size : (part + 1) * base_size], table, preferred_element_type=f32
        )
        total = piece if total is None else total + piece
    return total


def right_block(values, col_ref, rank, block_id, row_count, store):
    width = values.shape[1]
    lanes = col_ref.shape[1]
    half_rows = col_ref.shape[0] // 2
    first_row = (rank & 1) * half_rows
    group = min(4, half_rows // 2)
    row_bits = row_count.bit_length() - 1
    for step in range(half_rows // group):
        index = index_row(col_ref, first_row + step * group, group)
        part = cot_products(values, index % width, 256)
        part = part * parity_sign((index // width) & block_id, row_bits)
        half = step * group // (half_rows // 2)
        at = step * group * lanes % (half_rows // 2 * lanes)
        store(half, slice(at, at + group * lanes), part)


def block_signs(sign_ref, block_id, width):
    rows = width // sign_ref.shape[1]
    return index_row(sign_ref, block_id * rows, rows).astype(bf16)


def matrix_slice(matrix_ref, is_own, depth):
    half = (lax.axis_index("rows") & 1) ^ (0 if is_own else 1)
    first = pl.multiple_of((half * 2 + (lax.axis_index("ex") & 1)) * depth, depth)
    return matrix_ref.at[:, pl.ds(first, depth)]


def sign_kernel(hidden_in, sign_in, out_ref, hidden_ref, sign_ref, sems):
    copies = [
        pltpu.make_async_copy(hidden_in, hidden_ref, sems.at[0]),
        pltpu.make_async_copy(sign_in, sign_ref, sems.at[1]),
    ]
    for copy in copies:
        copy.start()
    for copy in copies:
        copy.wait()
    out_ref[0] = hidden_ref[...] * sign_ref[...].astype(bf16)


def first_kernel(row_count, cot_in, sign_in, col_in, row_in, len_in, *refs):
    right_ref, near_sign_ref, col_ref, row_ref, len_ref, token_ref, cot_ref, sign_ref, sems = refs
    pairs = (
        (cot_in, cot_ref),
        (sign_in, sign_ref),
        (col_in, col_ref),
        (row_in, row_ref),
        (len_in, len_ref),
    )
    copies = [pltpu.make_async_copy(*pair, sems.at[at]) for at, pair in enumerate(pairs)]
    for copy in copies:
        copy.start()
    token_ref[...] = jnp.zeros_like(token_ref)
    for copy in copies:
        copy.wait()
    rank = lax.axis_index("rows")
    width = cot_ref.shape[1]
    near_sign_ref[...] = block_signs(sign_ref, rank ^ 1, width)
    values = cot_ref[...] * block_signs(sign_ref, rank, width)

    def store(half, columns, part):
        right_ref[half, :, columns] = part

    right_block(values, col_ref, rank, rank, row_count, store)


def right_kernel(row_count, cot_ref, sign_ref, col_ref, own_ref, out_ref):
    rank = lax.axis_index("rows")

    def store(half, columns, part):
        out_ref[half, :, columns] = own_ref[half, :, columns] + part

    right_block(cot_ref[...] * sign_ref[...], col_ref, rank, rank ^ 1, row_count, store)


def feature_kernel(flip, row_count, masks, hidden_refs, right_ref, row_ref, len_ref, out_ref):
    rank = lax.axis_index("rows")
    ex_rank = lax.axis_index("ex")
    ex_count = lax.axis_size("ex")
    half = (ex_rank & 1) ^ flip
    tokens = right_ref.shape[1]
    width = hidden_refs[0].shape[2]
    examples = out_ref.shape[0]
    lanes = row_ref.shape[1]
    quarter_rows = row_ref.shape[0] // 4
    first_row = ((rank & 1) * 2 + half) * quarter_rows
    row_bits = row_count.bit_length() - 1
    own = examples // ex_count
    shape = (examples, examples)
    row_id = lax.broadcasted_iota(jnp.int32, shape, 0)
    example = ((row_id // own) ^ (ex_rank & ~1) ^ (ex_count - 2)) * own + row_id % own
    other = lax.broadcasted_iota(jnp.int32, shape, 1)
    counts = jnp.broadcast_to(len_ref[...], shape)
    ends = jnp.sum(jnp.where(other <= example, counts, 0), axis=1, keepdims=True)
    starts = jnp.sum(jnp.where(other < example, counts, 0), axis=1, keepdims=True)
    position = ex_rank * tokens + lax.broadcasted_iota(jnp.int32, (examples, tokens), 1)
    member = jnp.logical_and(position >= starts, position < ends).astype(f32).astype(bf16)
    blocks = []
    for ref in hidden_refs:
        for block in range(ref.shape[0]):
            blocks.append(ref[block])
    group = min(4, quarter_rows)
    for step in range(quarter_rows // group):
        index = index_row(row_ref, first_row + step * group, group)
        base = sign_columns(index % width, width)
        high = index // width
        left = None
        for mask, values in zip(masks, blocks):
            table = base * parity_sign(high & (rank ^ mask), row_bits).astype(bf16)
            piece = jnp.dot(values, table, preferred_element_type=f32)
            left = piece if left is None else left + piece
        columns = slice(step * group * lanes, (step + 1) * group * lanes)
        product = left * right_ref[half, :, columns]
        high_part = product.astype(bf16)
        low_part = (product - high_part.astype(f32)).astype(bf16)
        out_ref[:, columns] = jnp.dot(member, high_part, preferred_element_type=f32) + jnp.dot(
            member, low_part, preferred_element_type=f32
        )


def load_kernel(is_own, matrix_ref, after_ref, out_ref, token_ref, sem):
    copy = pltpu.make_async_copy(matrix_slice(matrix_ref, is_own, out_ref.shape[1]), out_ref, sem)
    copy.start()
    token_ref[...] = jnp.zeros_like(token_ref)
    copy.wait()


def add_kernel(scale, kept_ref, received_ref, *refs):
    total = kept_ref[...] + received_ref[...].astype(f32)
    if scale is not None:
        refs[-1][...] = (total * scale).astype(bf16)
    else:
        send_ref, total_ref = refs[-2:]
        send_ref[...] = total[: send_ref.shape[0]].astype(bf16)
        total_ref[...] = total[total.shape[0] - total_ref.shape[0] :]


def score_kernel(is_own, low_ref, matrix_ref, *refs):
    part = lax.dot_general(
        low_ref[...], matrix_ref[...], contract_last, preferred_element_type=f32
    )
    if is_own:
        refs[0][...] = part
    else:
        sum_ref, send_ref, keep_ref = refs
        part = part + sum_ref[...]
        own = part.shape[0] // 2
        lower = (lax.axis_index("ex") & 1) == 0
        keep_ref[...] = jnp.where(lower, part[:own], part[own:])
        send_ref[...] = jnp.where(lower, part[own:], part[:own])


def local(hidden_acts, cotangent, lengths, row_signs, col_signs, feat_row, feat_col, inverse_rows):
    row_count = lax.axis_size("rows")
    ex_count = lax.axis_size("ex")
    tokens, width = hidden_acts.shape
    model_width = col_signs.shape[0]
    feature_count = feat_row.shape[0]
    example_count = lengths.shape[0]
    quarter = feature_count // 4
    own_examples = example_count // ex_count
    norm_scale = 1.0 / math.sqrt(width * row_count * model_width)
    whole = pl.BlockSpec(memory_space=pltpu.VMEM)
    params = pltpu.CompilerParams(vmem_limit_bytes=vmem_bytes)

    anywhere = pl.BlockSpec(memory_space=pltpu.HBM)
    out_rows = inverse_rows.shape[0]

    near_cot = swap(cotangent, "rows", 1)
    signed = pl.pallas_call(
        sign_kernel,
        out_shape=pltpu.VMEM((1, tokens, width), bf16),
        in_specs=[anywhere] * 2,
        out_specs=whole,
        scratch_shapes=[
            pltpu.VMEM((tokens, width), bf16),
            pltpu.VMEM((1, width), jnp.int32),
            pltpu.SemaphoreType.DMA((2,)),
        ],
        compiler_params=params,
    )(in_hbm(hidden_acts), in_hbm(row_signs.reshape(1, -1)))
    held = signed
    masks = [0]
    step = 2
    while step < row_count:
        held = jnp.concatenate([held, swap(held, "rows", step)], axis=0)
        masks += [mask | step for mask in masks]
        step *= 2
    masks += [mask | 1 for mask in masks]

    cot_width = cotangent.shape[1]
    right_shape = pltpu.VMEM((2, tokens, quarter), f32)
    lanes = min(128, cot_width)
    right, near_signs, col_index, row_index, counts, token = pl.pallas_call(
        functools.partial(first_kernel, row_count),
        out_shape=(
            right_shape,
            pltpu.VMEM((1, cot_width), bf16),
            pltpu.VMEM((feature_count // 128, 128), jnp.int32),
            pltpu.VMEM((feature_count // 128, 128), jnp.int32),
            pltpu.VMEM((1, example_count), jnp.int32),
            pltpu.VMEM((1, 1, 128), bf16),
        ),
        in_specs=[anywhere] * 5,
        out_specs=(whole,) * 6,
        scratch_shapes=[
            pltpu.VMEM(cotangent.shape, bf16),
            pltpu.VMEM((model_width // lanes, lanes), jnp.int32),
            pltpu.SemaphoreType.DMA((5,)),
        ],
        compiler_params=params,
    )(
        in_hbm(cotangent),
        in_hbm(col_signs.reshape(-1, lanes)),
        in_hbm(feat_col.reshape(-1, 128)),
        in_hbm(feat_row.reshape(-1, 128)),
        in_hbm(lengths.reshape(1, -1)),
    )
    held = held + token[:, :, :1]
    hidden_parts = (held, swap(held, "rows", 1))
    right = pl.pallas_call(
        functools.partial(right_kernel, row_count),
        out_shape=right_shape,
        in_specs=[whole] * 4,
        out_specs=whole,
        compiler_params=params,
    )(near_cot, near_signs, col_index, right)

    def features(flip):
        def kernel(*refs):
            feature_kernel(flip, row_count, masks, refs[:2], *refs[2:])

        return pl.pallas_call(
            kernel,
            out_shape=jax.ShapeDtypeStruct((example_count, quarter), f32),
            in_specs=[whole] * 5,
            out_specs=whole,
            compiler_params=params,
        )(*hidden_parts, right, row_index, counts)

    def load(is_own, after):
        return pl.pallas_call(
            functools.partial(load_kernel, is_own),
            out_shape=(pltpu.VMEM((out_rows, quarter), bf16), pltpu.VMEM((8, 128), f32)),
            in_specs=[anywhere, whole],
            out_specs=(whole, whole),
            scratch_shapes=[pltpu.SemaphoreType.DMA],
            compiler_params=params,
        )(in_hbm(inverse_rows), after)

    def add_up(kept, received, send_count, token, scale=None):
        count = received.shape[0]
        out_shape = [pltpu.VMEM((send_count, quarter), bf16)]
        if scale is None:
            out_shape.append(pltpu.VMEM((count - send_count % count, quarter), f32))
        return pl.pallas_call(
            functools.partial(add_kernel, scale),
            out_shape=out_shape,
            in_specs=[whole] * (2 + (token is not None)),
            out_specs=[whole] * len(out_shape),
            compiler_params=params,
        )(kept, received, *([] if token is None else [token]))

    ex_masks = [1 << bit for bit in range(1, ex_count.bit_length() - 1)][::-1]
    row_masks = [1 << bit for bit in range(1, row_count.bit_length() - 1)]
    received = swap(features(1), "ex", 1)
    total = features(0)
    matrices, token = [], None
    hops = [("ex", mask) for mask in ex_masks] + [("rows", mask) for mask in row_masks]
    for axis, mask in hops:
        count = received.shape[0]
        send, total = add_up(total, received, count // 2 if axis == "ex" else count, token)
        token = None
        if len(matrices) < 2:
            matrix, token = load(len(matrices) == 0, send)
            matrices.append(matrix)
        received = swap(send, axis, mask)
    own_matrix, near_matrix = matrices
    (low,) = add_up(total, received, received.shape[0], token, norm_scale)
    near_low = swap(low, "rows", 1)

    part = pl.pallas_call(
        functools.partial(score_kernel, True),
        out_shape=jax.ShapeDtypeStruct((2 * own_examples, out_rows), f32),
        in_specs=[whole, whole],
        out_specs=whole,
        compiler_params=params,
    )(low, own_matrix)
    own_shape = jax.ShapeDtypeStruct((own_examples, out_rows), f32)
    send, keep = pl.pallas_call(
        functools.partial(score_kernel, False),
        out_shape=(own_shape, own_shape),
        in_specs=[whole, whole, whole],
        out_specs=(whole, whole),
        compiler_params=params,
    )(near_low, near_matrix, part)
    return (keep + swap(send, "ex", 1)).astype(bf16)


def solution(mesh):
    placed = (
        P(("parts", "ex"), "rows"),
        P(("parts", "ex"), "rows"),
        P("parts"),
        P("rows"),
        P(),
        P(),
        P(),
        P("rows", None),
    )
    return jax.shard_map(
        local, mesh=mesh, in_specs=placed, out_specs=P(("parts", "ex"), "rows"), check_vma=False
    )
```

time: 48.5 us -> 37.5 us (0.77)
  waiting for transfers between devices: 15.5 us -> 2.87 us
  starting transfers between devices: 9 us -> 14.7 us
  local copies, waits for them, and re-layouts: 2.46 us -> 0 us
  other arithmetic: 2.15 us -> 0.67 us
    ppermute x8, waiting for transfers between devices: 15.5 us -> 2.87 us  [swap(): lax.ppermute(values, axis, [(rank, rank ^ mask) for rank in range(size)])]
    pallas_call x2 -> x8, Pallas kernels: 2.86 us -> 11.5 us  [the longest x2 6.78 us: load(): pl.pallas_call(functools.partial(load_kernel, is_own), out_shape=(pltpu.V...]
    ppermute x8, starting transfers between devices: 9 us -> 14.7 us  [swap(): lax.ppermute(values, axis, [(rank, rank ^ mask) for rank in range(size)])]
    pallas_call x1, Pallas kernels: 6.58 us -> 2.27 us  [local(): pl.pallas_call(functools.partial(score_kernel, False), out_shape=(own_sha...]
    pallas_call x1, Pallas kernels: 6.56 us -> 2.26 us  [local(): pl.pallas_call(functools.partial(score_kernel, True), out_shape=jax.Shape...]
    unnamed x8 -> x0, local copies, waits for them, and re-layouts: 1.72 us -> none
    broadcast_in_dim x1 -> x0, other arithmetic: 0.76 us -> none  [local(): hidden_parts = [signed[None]]]
    reshape x1 -> x0, local copies, waits for them, and re-layouts: 0.73 us -> none  [local(): col_table = col_signs.reshape(row_count, model_width // row_count)]
  transfers between devices with their start and end apart: 8 -> 8, of which waited for: 5 -> 5; matrix products, arithmetic and copies ran while one was open for 4% -> 0% of each run, Pallas kernels for 22% -> 41%
where the time goes in v2:
time: 37.5 us; the launch traced here: 37.3 us
  Pallas kernels  18.9 us (50%)
  starting transfers between devices  14.7 us (39%)
  waiting for transfers between devices  2.87 us (8%)
  other arithmetic  0.67 us (2%)
    ppermute x8, starting transfers between devices, swap(): lax.ppermute(values, axis, [(rank, rank ^ mask) for rank in range(size)])  14.7 us
    pallas_call x2, Pallas kernels, load(): pl.pallas_call(functools.partial(load_kernel, is_own), out_shape=(pltpu.V...  6.78 us
    pallas_call x2, Pallas kernels, features(): pl.pallas_call(kernel, out_shape=jax.ShapeDtypeStruct((example_count, qua...  2.89 us
    ppermute x8, waiting for transfers between devices, swap(): lax.ppermute(values, axis, [(rank, rank ^ mask) for rank in range(size)])  2.87 us
    pallas_call x1, Pallas kernels, local(): pl.pallas_call(functools.partial(first_kernel, row_count), out_shape=(rig...  2.41 us
    pallas_call x1, Pallas kernels, local(): pl.pallas_call(functools.partial(score_kernel, False), out_shape=(own_sha...  2.27 us
    pallas_call x1, Pallas kernels, local(): pl.pallas_call(functools.partial(score_kernel, True), out_shape=jax.Shape...  2.26 us
    pallas_call x1, Pallas kernels, local(): pl.pallas_call(functools.partial(right_kernel, row_count), out_shape=righ...  1.43 us
  transfers between devices with their start and end apart: 8, of which 5 were waited for; matrix products, arithmetic and copies ran while one was open for 0% of the time, Pallas kernels for 41%

profile of v2, /device:TPU:0, one launch (start us, length us, event | category | flops | bytes accessed | tf_op | source)
XLA Modules:
  0.0 37.3 jit_solution(16813658404785184758)
XLA Ops:
  0.0 3.0 %collective-permute-start.2 = (bf16[128,1024]{1,0:T(8,128)(2,1)}, bf16[128,1024]{1,0:T(8,128)(2,1)S(1)}, u32[]{:S(2)}, u32[]{:S(2)}) collective-permute-start(bf16[128,1024]{1,0:T(8,128)(2,1)} %cot_in.1), channel_id=1, source_target_pairs={{0,4},{4,0},{8,12},{12,8},{1,5},{5,1},{9,13},{13,9},{2,6},{6,2},{1... | collective-permute-start | bytes 786440 | tf_op jit(solution)/shard_map/ppermute | solution.py:23
  3.0 0.8 %shard_map.82 = bf16[1,128,128]{2,1,0:T(8,128)(2,1)S(1)} custom-call(bf16[128,128]{1,0:T(8,128)(2,1)} %hidden_in.1, s32[1,128]{1,0:T(1,128)} %bitcast.11), custom_call_target="tpu_custom_call" | custom-call | tf_op jit(solution)/shard_map/pallas_call | solution.py:238
  3.8 2.7 %collective-permute-start = (bf16[1,128,128]{2,1,0:T(8,128)(2,1)S(1)}, bf16[1,128,128]{2,1,0:T(8,128)(2,1)S(1)}, u32[]{:S(2)}, u32[]{:S(2)}) collective-permute-start(bf16[1,128,128]{2,1,0:T(8,128)(2,1)S(1)} %shard_map.82), channel_id=1, source_target_pairs={{0,8},{4,12},{8,0},{12,4},{1,9},{5,13},{9,1},{13,5},{2,10},{6,14},... | collective-permute-start | bytes 98312 | tf_op jit(solution)/shard_map/ppermute | solution.py:23
  6.5 2.4 %shard_map.83 = (f32[2,128,2048]{2,1,0:T(8,128)S(1)}, bf16[1,1024]{1,0:T(2,128)(2,1)S(1)}, s32[64,128]{1,0:T(8,128)S(1)}, s32[64,128]{1,0:T(8,128)S(1)}, s32[1,3...) custom-call(bf16[128,1024]{1,0:T(8,128)(2,1)} %cot_in.1, s32[32,128]{1,0:T(8,128)} %bitcast.10, s32[64,128]{1,0:T(8,128)} %bitcast.8, ...), custom_call_target="tpu_custom_call" | custom-call | tf_op jit(solution)/shard_map/pallas_call | solution.py:262
  8.9 0.6 %collective-permute-done = bf16[1,128,128]{2,1,0:T(8,128)(2,1)S(1)} collective-permute-done((bf16[1,128,128]{2,1,0:T(8,128)(2,1)S(1)}, bf16[1,128,128]{2,1,0:T(8,128)(2,1)S(1)}, u32[]{:S(2)}, u32[]{:S(2)}) %collective-permute-start) | collective-permute-done | bytes 32800 | tf_op jit(solution)/shard_map/ppermute | solution.py:23
  9.6 3.6 %collective-permute-start.1 = (bf16[2,128,128]{2,1,0:T(8,128)(2,1)S(1)}, bf16[2,128,128]{2,1,0:T(8,128)(2,1)S(1)}, u32[]{:S(2)}, u32[]{:S(2)}) collective-permute-start(bf16[2,128,128]{2,1,0:T(8,128)(2,1)S(1)} %maximum_add_fusion.refs_0_), channel_id=1, source_target_pairs={{0,4},{4,0},{8,12},{12,8},{1,5},{5,1},{9,13},{13,9},{2,6},{6,2},{1... | collective-permute-start | bytes 196616 | tf_op jit(solution)/shard_map/ppermute | solution.py:23
  13.1 0.0 collective-permute-done.2.cot_ref
  13.1 1.4 %shard_map.84.refs_2_ = f32[2,128,2048]{2,1,0:T(8,128)S(1)} custom-call(bf16[128,1024]{1,0:T(8,128)(2,1)S(1)} %collective-permute-done.2.cot_ref, bf16[1,1024]{1,0:T(2,128)(2,1)S(1)} %get-tuple-element.22.sign_ref, s32[64,128]{1,0:T(8,128)S(1)} %get-tuple-element.23.col_ref, f32[2,128,2048]{2,1,0:T(8,128)S(1)} %get-tuple-element.24.own_ref), custom_call_target="tpu_custom_call" | custom-call | tf_op jit(solution)/shard_map/pallas_call | solution.py:289
  14.6 0.8 %collective-permute-done.1.refs_1_ = bf16[2,128,128]{2,1,0:T(8,128)(2,1)S(1)} collective-permute-done((bf16[2,128,128]{2,1,0:T(8,128)(2,1)S(1)}, bf16[2,128,128]{2,1,0:T(8,128)(2,1)S(1)}, u32[]{:S(2)}, u32[]{:S(2)}) %collective-permute-start.1) | collective-permute-done | bytes 65568 | tf_op jit(solution)/shard_map/ppermute | solution.py:23
  15.4 1.4 %shard_map.86 = f32[32,2048]{1,0:T(8,128)S(1)} custom-call(bf16[2,128,128]{2,1,0:T(8,128)(2,1)S(1)} %maximum_add_fusion.refs_0_, bf16[2,128,128]{2,1,0:T(8,128)(2,1)S(1)} %collective-permute-done.1.refs_1_, f32[2,128,2048]{2,1,0:T(8,128)S(1)} %shard_map.84.refs_2_, s32[64,128]{1,0:T(8,128)S(1)} %get-tuple-element.25.refs_3_, ...), custom_call_target="tpu_custom_call" | custom-call | tf_op jit(solution)/shard_map/pallas_call | solution.py:301
  16.8 0.0 collective-permute-start.3
  16.8 1.5 %shard_map.85.kept_ref = f32[32,2048]{1,0:T(8,128)S(1)} custom-call(bf16[2,128,128]{2,1,0:T(8,128)(2,1)S(1)} %maximum_add_fusion.refs_0_, bf16[2,128,128]{2,1,0:T(8,128)(2,1)S(1)} %collective-permute-done.1.refs_1_, f32[2,128,2048]{2,1,0:T(8,128)S(1)} %shard_map.84.refs_2_, s32[64,128]{1,0:T(8,128)S(1)} %get-tuple-element.25.refs_3_, ...), custom_call_target="tpu_custom_call" | custom-call | tf_op jit(solution)/shard_map/pallas_call | solution.py:301
  18.3 0.1 collective-permute-done.3.received_ref
  18.4 1.6 %collective-permute-start.4 = (bf16[16,2048]{1,0:T(8,128)(2,1)S(1)}, bf16[16,2048]{1,0:T(8,128)(2,1)S(1)}, u32[]{:S(2)}, u32[]{:S(2)}) collective-permute-start(bf16[16,2048]{1,0:T(8,128)(2,1)S(1)} %get-tuple-element.28.after_ref), channel_id=1, source_target_pairs={{0,2},{1,3},{2,0},{3,1},{4,6},{5,7},{6,4},{7,5},{8,10},{9,11},{10,... | collective-permute-start | bytes 196616 | tf_op jit(solution)/shard_map/ppermute | solution.py:23
  20.0 3.4 %shard_map.88 = (bf16[2048,2048]{1,0:T(8,128)(2,1)S(1)}, f32[8,128]{1,0:T(8,128)S(1)}) custom-call(bf16[2048,8192]{1,0:T(8,128)(2,1)} %matrix_ref.3, bf16[16,2048]{1,0:T(8,128)(2,1)S(1)} %get-tuple-element.28.after_ref), custom_call_target="tpu_custom_call" | custom-call | tf_op jit(solution)/shard_map/pallas_call | solution.py:310
  23.4 0.0 collective-permute-done.4.received_ref
  23.4 1.9 %collective-permute-start.5 = (bf16[16,2048]{1,0:T(8,128)(2,1)S(1)}, bf16[16,2048]{1,0:T(8,128)(2,1)S(1)}, u32[]{:S(2)}, u32[]{:S(2)}) collective-permute-start(bf16[16,2048]{1,0:T(8,128)(2,1)S(1)} %get-tuple-element.31.after_ref), channel_id=1, source_target_pairs={{0,8},{4,12},{8,0},{12,4},{1,9},{5,13},{9,1},{13,5},{2,10},{6,14},... | collective-permute-start | bytes 196616 | tf_op jit(solution)/shard_map/ppermute | solution.py:23
  25.3 3.4 %shard_map.90 = (bf16[2048,2048]{1,0:T(8,128)(2,1)S(1)}, f32[8,128]{1,0:T(8,128)S(1)}) custom-call(bf16[2048,8192]{1,0:T(8,128)(2,1)} %matrix_ref.3, bf16[16,2048]{1,0:T(8,128)(2,1)S(1)} %get-tuple-element.31.after_ref), custom_call_target="tpu_custom_call" | custom-call | tf_op jit(solution)/shard_map/pallas_call | solution.py:310
  28.7 0.0 collective-permute-done.5.received_ref
  28.8 2.0 %collective-permute-start.6 = (bf16[16,2048]{1,0:T(8,128)(2,1)S(1)}, bf16[16,2048]{1,0:T(8,128)(2,1)S(1)}, u32[]{:S(2)}, u32[]{:S(2)}) collective-permute-start(bf16[16,2048]{1,0:T(8,128)(2,1)S(1)} %shard_map.91.low_ref), channel_id=1, source_target_pairs={{0,4},{4,0},{8,12},{12,8},{1,5},{5,1},{9,13},{13,9},{2,6},{6,2},{1... | collective-permute-start | bytes 196616 | tf_op jit(solution)/shard_map/ppermute | solution.py:23
  30.7 2.3 %shard_map.92.refs_0_ = f32[16,2048]{1,0:T(8,128)S(1)} custom-call(bf16[16,2048]{1,0:T(8,128)(2,1)S(1)} %shard_map.91.low_ref, bf16[2048,2048]{1,0:T(8,128)(2,1)S(1)} %get-tuple-element.34.matrix_ref), custom_call_target="tpu_custom_call" | custom-call | tf_op jit(solution)/shard_map/pallas_call | solution.py:350
  33.0 0.1 collective-permute-done.6.low_ref
  33.1 2.3 %shard_map.93 = (f32[8,2048]{1,0:T(8,128)S(1)}, f32[8,2048]{1,0:T(8,128)S(1)}) custom-call(bf16[16,2048]{1,0:T(8,128)(2,1)S(1)} %collective-permute-done.6.low_ref, bf16[2048,2048]{1,0:T(8,128)(2,1)S(1)} %get-tuple-element.33.matrix_ref, f32[16,2048]{1,0:T(8,128)S(1)} %shard_map.92.refs_0_), custom_call_target="tpu_custom_call" | custom-call | tf_op jit(solution)/shard_map/pallas_call | solution.py:358
  35.4 0.0 collective-permute-start.7
  35.4 1.3 %collective-permute-done.7 = f32[8,2048]{1,0:T(8,128)S(1)} collective-permute-done((f32[8,2048]{1,0:T(8,128)S(1)}, f32[8,2048]{1,0:T(8,128)S(1)}, u32[]{:S(2)}, u32[]{:S(2)}) %collective-permute-start.7) | collective-permute-done | bytes 65568 | tf_op jit(solution)/shard_map/ppermute | solution.py:23
  36.6 0.6 %add_convert_fusion = bf16[8,2048]{1,0:T(8,128)(2,1)} fusion(f32[8,2048]{1,0:T(8,128)S(1)} %get-tuple-element.35, f32[8,2048]{1,0:T(8,128)S(1)} %collective-permute-done.7), kind=kLoop, calls=%fused_computation.1 | loop fusion | flops 32768 | bytes 163840 | tf_op jit(solution)/shard_map/convert_element_type | solution.py:365
  (4 shorter events, 0.1 us)
Async XLA Ops:
  0.0 13.1 %collective-permute-start.2 = (bf16[128,1024]{1,0:T(8,128)(2,1)}, bf16[128,1024]{1,0:T(8,128)(2,1)S(1)}, u32[]{:S(2)}, u32[]{:S(2)}) collective-permute-start(bf16[128,1024]{1,0:T(8,128)(2,1)} %cot_in.1), channel_id=1, source_target_pairs={{0,4},{4,0},{8,12},{12,8},{1,5},{5,1},{9,13},{13,9},{2,6},{6,2},{1... | collective-permute-start | bytes 786440 | tf_op jit(solution)/shard_map/ppermute | solution.py:23
  3.8 5.7 %collective-permute-start = (bf16[1,128,128]{2,1,0:T(8,128)(2,1)S(1)}, bf16[1,128,128]{2,1,0:T(8,128)(2,1)S(1)}, u32[]{:S(2)}, u32[]{:S(2)}) collective-permute-start(bf16[1,128,128]{2,1,0:T(8,128)(2,1)S(1)} %shard_map.82), channel_id=1, source_target_pairs={{0,8},{4,12},{8,0},{12,4},{1,9},{5,13},{9,1},{13,5},{2,10},{6,14},... | collective-permute-start | bytes 98312 | tf_op jit(solution)/shard_map/ppermute | solution.py:23
  9.6 5.8 %collective-permute-start.1 = (bf16[2,128,128]{2,1,0:T(8,128)(2,1)S(1)}, bf16[2,128,128]{2,1,0:T(8,128)(2,1)S(1)}, u32[]{:S(2)}, u32[]{:S(2)}) collective-permute-start(bf16[2,128,128]{2,1,0:T(8,128)(2,1)S(1)} %maximum_add_fusion.refs_0_), channel_id=1, source_target_pairs={{0,4},{4,0},{8,12},{12,8},{1,5},{5,1},{9,13},{13,9},{2,6},{6,2},{1... | collective-permute-start | bytes 196616 | tf_op jit(solution)/shard_map/ppermute | solution.py:23
  16.8 1.6 %collective-permute-start.3 = (f32[32,2048]{1,0:T(8,128)S(1)}, f32[32,2048]{1,0:T(8,128)S(1)}, u32[]{:S(2)}, u32[]{:S(2)}) collective-permute-start(f32[32,2048]{1,0:T(8,128)S(1)} %shard_map.86), channel_id=1, source_target_pairs={{0,1},{1,0},{2,3},{3,2},{4,5},{5,4},{6,7},{7,6},{8,9},{9,8},{10,11... | collective-permute-start | bytes 786440 | tf_op jit(solution)/shard_map/ppermute | solution.py:23
  18.4 5.0 %collective-permute-start.4 = (bf16[16,2048]{1,0:T(8,128)(2,1)S(1)}, bf16[16,2048]{1,0:T(8,128)(2,1)S(1)}, u32[]{:S(2)}, u32[]{:S(2)}) collective-permute-start(bf16[16,2048]{1,0:T(8,128)(2,1)S(1)} %get-tuple-element.28.after_ref), channel_id=1, source_target_pairs={{0,2},{1,3},{2,0},{3,1},{4,6},{5,7},{6,4},{7,5},{8,10},{9,11},{10,... | collective-permute-start | bytes 196616 | tf_op jit(solution)/shard_map/ppermute | solution.py:23
  23.4 5.3 %collective-permute-start.5 = (bf16[16,2048]{1,0:T(8,128)(2,1)S(1)}, bf16[16,2048]{1,0:T(8,128)(2,1)S(1)}, u32[]{:S(2)}, u32[]{:S(2)}) collective-permute-start(bf16[16,2048]{1,0:T(8,128)(2,1)S(1)} %get-tuple-element.31.after_ref), channel_id=1, source_target_pairs={{0,8},{4,12},{8,0},{12,4},{1,9},{5,13},{9,1},{13,5},{2,10},{6,14},... | collective-permute-start | bytes 196616 | tf_op jit(solution)/shard_map/ppermute | solution.py:23
  28.8 4.3 %collective-permute-start.6 = (bf16[16,2048]{1,0:T(8,128)(2,1)S(1)}, bf16[16,2048]{1,0:T(8,128)(2,1)S(1)}, u32[]{:S(2)}, u32[]{:S(2)}) collective-permute-start(bf16[16,2048]{1,0:T(8,128)(2,1)S(1)} %shard_map.91.low_ref), channel_id=1, source_target_pairs={{0,4},{4,0},{8,12},{12,8},{1,5},{5,1},{9,13},{13,9},{2,6},{6,2},{1... | collective-permute-start | bytes 196616 | tf_op jit(solution)/shard_map/ppermute | solution.py:23
  35.4 1.3 %collective-permute-start.7 = (f32[8,2048]{1,0:T(8,128)S(1)}, f32[8,2048]{1,0:T(8,128)S(1)}, u32[]{:S(2)}, u32[]{:S(2)}) collective-permute-start(f32[8,2048]{1,0:T(8,128)S(1)} %get-tuple-element.36), channel_id=1, source_target_pairs={{0,1},{1,0},{2,3},{3,2},{4,5},{5,4},{6,7},{7,6},{8,9},{9,8},{10,11... | collective-permute-start | bytes 196616 | tf_op jit(solution)/shard_map/ppermute | solution.py:23

commit v3 on v2

--- a/solution.py
+++ b/solution.py
@@ -88,10 +88,11 @@
     return index_row(sign_ref, block_id * rows, rows).astype(bf16)
 
 
-def matrix_slice(matrix_ref, is_own, depth):
-    half = (lax.axis_index("rows") & 1) ^ (0 if is_own else 1)
+def matrix_chunk(matrix_ref, chunk, shape):
+    rows, depth = shape
+    half = (lax.axis_index("rows") & 1) ^ (chunk // 2)
     first = pl.multiple_of((half * 2 + (lax.axis_index("ex") & 1)) * depth, depth)
-    return matrix_ref.at[:, pl.ds(first, depth)]
+    return matrix_ref.at[pl.ds(chunk % 2 * rows, rows), pl.ds(first, depth)]
 
 
 def sign_kernel(hidden_in, sign_in, out_ref, hidden_ref, sign_ref, sems):
@@ -106,53 +107,52 @@
     out_ref[0] = hidden_ref[...] * sign_ref[...].astype(bf16)
 
 
-def first_kernel(row_count, cot_in, sign_in, col_in, row_in, len_in, *refs):
-    right_ref, near_sign_ref, col_ref, row_ref, len_ref, token_ref, cot_ref, sign_ref, sems = refs
+def own_kernel(row_count, *refs):
+    (cot_in, sign_in, col_in, row_in, len_in, matrix_ref), refs = refs[:6], refs[6:]
+    right_ref, near_sign_ref, table_ref, member_ref, held_ref, col_ref, row_ref = refs[:7]
+    cot_ref, sign_ref, len_ref, sems = refs[7:]
     pairs = (
         (cot_in, cot_ref),
         (sign_in, sign_ref),
         (col_in, col_ref),
         (row_in, row_ref),
         (len_in, len_ref),
+        (matrix_chunk(matrix_ref, 0, held_ref.shape), held_ref),
     )
     copies = [pltpu.make_async_copy(*pair, sems.at[at]) for at, pair in enumerate(pairs)]
     for copy in copies:
         copy.start()
-    token_ref[...] = jnp.zeros_like(token_ref)
-    for copy in copies:
+    for copy in copies[:-1]:
         copy.wait()
     rank = lax.axis_index("rows")
     width = cot_ref.shape[1]
     near_sign_ref[...] = block_signs(sign_ref, rank ^ 1, width)
-    values = cot_ref[...] * block_signs(sign_ref, rank, width)
 
     def store(half, columns, part):
         right_ref[half, :, columns] = part
 
+    values = cot_ref[...] * block_signs(sign_ref, rank, width)
     right_block(values, col_ref, rank, rank, row_count, store)
-
-
-def right_kernel(row_count, cot_ref, sign_ref, col_ref, own_ref, out_ref):
+    tables(row_ref, len_ref, table_ref, member_ref)
+    copies[-1].wait()
+
+
+def tables(row_ref, len_ref, table_ref, member_ref):
     rank = lax.axis_index("rows")
-
-    def store(half, columns, part):
-        out_ref[half, :, columns] = own_ref[half, :, columns] + part
-
-    right_block(cot_ref[...] * sign_ref[...], col_ref, rank, rank ^ 1, row_count, store)
-
-
-def feature_kernel(flip, row_count, masks, hidden_refs, right_ref, row_ref, len_ref, out_ref):
-    rank = lax.axis_index("rows")
+    lanes = row_ref.shape[1]
+    quarter_rows = row_ref.shape[0] // 4
+    first_row = (rank & 1) * 2 * quarter_rows
+    width = table_ref.shape[1]
+    group = min(4, quarter_rows)
+    for step in range(2 * quarter_rows // group):
+        index = index_row(row_ref, first_row + step * group, group)
+        at = step * group % quarter_rows * lanes
+        table_ref[step * group // quarter_rows, :, at : at + group * lanes] = sign_columns(
+            index % width, width
+        )
+    examples, tokens = member_ref.shape
     ex_rank = lax.axis_index("ex")
     ex_count = lax.axis_size("ex")
-    half = (ex_rank & 1) ^ flip
-    tokens = right_ref.shape[1]
-    width = hidden_refs[0].shape[2]
-    examples = out_ref.shape[0]
-    lanes = row_ref.shape[1]
-    quarter_rows = row_ref.shape[0] // 4
-    first_row = ((rank & 1) * 2 + half) * quarter_rows
-    row_bits = row_count.bit_length() - 1
     own = examples // ex_count
     shape = (examples, examples)
     row_id = lax.broadcasted_iota(jnp.int32, shape, 0)
@@ -162,22 +162,50 @@
     ends = jnp.sum(jnp.where(other <= example, counts, 0), axis=1, keepdims=True)
     starts = jnp.sum(jnp.where(other < example, counts, 0), axis=1, keepdims=True)
     position = ex_rank * tokens + lax.broadcasted_iota(jnp.int32, (examples, tokens), 1)
-    member = jnp.logical_and(position >= starts, position < ends).astype(f32).astype(bf16)
+    inside = jnp.logical_and(position >= starts, position < ends)
+    member_ref[...] = inside.astype(f32).astype(bf16)
+
+
+def right_kernel(row_count, cot_ref, sign_ref, col_ref, own_ref, out_ref):
+    rank = lax.axis_index("rows")
+
+    def store(half, columns, part):
+        out_ref[half, :, columns] = own_ref[half, :, columns] + part
+
+    right_block(cot_ref[...] * sign_ref[...], col_ref, rank, rank ^ 1, row_count, store)
+
+
+def feature_kernel(flip, row_count, masks, hidden_refs, right_ref, row_ref, table_ref, member_ref, out_ref):
+    rank = lax.axis_index("rows")
+    half = (lax.axis_index("ex") & 1) ^ flip
+    width = table_ref.shape[1]
+    lanes = row_ref.shape[1]
+    quarter_rows = row_ref.shape[0] // 4
+    first_row = ((rank & 1) * 2 + half) * quarter_rows
+    row_bits = row_count.bit_length() - 1
     blocks = []
     for ref in hidden_refs:
         for block in range(ref.shape[0]):
             blocks.append(ref[block])
+    member = member_ref[...]
     group = min(4, quarter_rows)
     for step in range(quarter_rows // group):
+        columns = slice(step * group * lanes, (step + 1) * group * lanes)
         index = index_row(row_ref, first_row + step * group, group)
-        base = sign_columns(index % width, width)
+        base = table_ref[half, :, columns]
         high = index // width
         left = None
-        for mask, values in zip(masks, blocks):
-            table = base * parity_sign(high & (rank ^ mask), row_bits).astype(bf16)
-            piece = jnp.dot(values, table, preferred_element_type=f32)
+        for first in range(0, len(masks), 4):
+            table = [
+                base * parity_sign(high & (rank ^ mask), row_bits).astype(bf16)
+                for mask in masks[first : first + 4]
+            ]
+            piece = jnp.dot(
+                jnp.concatenate(blocks[first : first + 4], axis=1),
+                jnp.concatenate(table, axis=0),
+                preferred_element_type=f32,
+            )
             left = piece if left is None else left + piece
-        columns = slice(step * group * lanes, (step + 1) * group * lanes)
         product = left * right_ref[half, :, columns]
         high_part = product.astype(bf16)
         low_part = (product - high_part.astype(f32)).astype(bf16)
@@ -186,8 +214,8 @@
         )
 
 
-def load_kernel(is_own, matrix_ref, after_ref, out_ref, token_ref, sem):
-    copy = pltpu.make_async_copy(matrix_slice(matrix_ref, is_own, out_ref.shape[1]), out_ref, sem)
+def load_kernel(chunk, matrix_ref, after_ref, out_ref, token_ref, sem):
+    copy = pltpu.make_async_copy(matrix_chunk(matrix_ref, chunk, out_ref.shape), out_ref, sem)
     copy.start()
     token_ref[...] = jnp.zeros_like(token_ref)
     copy.wait()
@@ -203,19 +231,33 @@
         total_ref[...] = total[total.shape[0] - total_ref.shape[0] :]
 
 
-def score_kernel(is_own, low_ref, matrix_ref, *refs):
-    part = lax.dot_general(
-        low_ref[...], matrix_ref[...], contract_last, preferred_element_type=f32
-    )
-    if is_own:
-        refs[0][...] = part
-    else:
-        sum_ref, send_ref, keep_ref = refs
-        part = part + sum_ref[...]
-        own = part.shape[0] // 2
-        lower = (lax.axis_index("ex") & 1) == 0
-        keep_ref[...] = jnp.where(lower, part[:own], part[own:])
-        send_ref[...] = jnp.where(lower, part[own:], part[:own])
+def own_score_kernel(low_ref, lower_ref, upper_ref, matrix_ref, out_ref, held_ref, sem):
+    copy = pltpu.make_async_copy(matrix_chunk(matrix_ref, 3, held_ref.shape), held_ref, sem)
+    copy.start()
+
+    @pl.when(lax.axis_index("rows") >= 0)
+    def _():
+        rows = held_ref.shape[0]
+        low = low_ref[...]
+        for at, ref in enumerate((lower_ref, upper_ref)):
+            out_ref[:, at * rows : (at + 1) * rows] = lax.dot_general(
+                low, ref[...], contract_last, preferred_element_type=f32
+            )
+
+    copy.wait()
+
+
+def near_score_kernel(low_ref, lower_ref, upper_ref, sum_ref, send_ref, keep_ref):
+    rows = lower_ref.shape[0]
+    low = low_ref[...]
+    own = low.shape[0] // 2
+    lower = (lax.axis_index("ex") & 1) == 0
+    for at, ref in enumerate((lower_ref, upper_ref)):
+        columns = slice(at * rows, (at + 1) * rows)
+        part = lax.dot_general(low, ref[...], contract_last, preferred_element_type=f32)
+        part = part + sum_ref[:, columns]
+        keep_ref[:, columns] = jnp.where(lower, part[:own], part[own:])
+        send_ref[:, columns] = jnp.where(lower, part[own:], part[:own])
 
 
 def local(hidden_acts, cotangent, lengths, row_signs, col_signs, feat_row, feat_col, inverse_rows):
@@ -233,6 +275,9 @@
 
     anywhere = pl.BlockSpec(memory_space=pltpu.HBM)
     out_rows = inverse_rows.shape[0]
+
+    chunk = (out_rows // 2, quarter)
+    table_shape = (feature_count // 128, 128)
 
     near_cot = swap(cotangent, "rows", 1)
     signed = pl.pallas_call(
@@ -247,34 +292,38 @@
         ],
         compiler_params=params,
     )(in_hbm(hidden_acts), in_hbm(row_signs.reshape(1, -1)))
-    held = signed
-    masks = [0]
-    step = 2
+    group = min(row_count, 4)
+    hidden_parts = [signed] + [swap(signed, "rows", mask) for mask in range(1, group)]
+    masks = list(range(group))
+    step = group
     while step < row_count:
-        held = jnp.concatenate([held, swap(held, "rows", step)], axis=0)
+        held = jnp.concatenate(hidden_parts, axis=0)
+        hidden_parts = [held, swap(held, "rows", step)]
         masks += [mask | step for mask in masks]
         step *= 2
-    masks += [mask | 1 for mask in masks]
+    parts = len(hidden_parts)
 
     cot_width = cotangent.shape[1]
+    lanes = min(128, cot_width)
     right_shape = pltpu.VMEM((2, tokens, quarter), f32)
-    lanes = min(128, cot_width)
-    right, near_signs, col_index, row_index, counts, token = pl.pallas_call(
-        functools.partial(first_kernel, row_count),
+    right, near_signs, hidden_table, member, matrix_0, col_index, row_index = pl.pallas_call(
+        functools.partial(own_kernel, row_count),
         out_shape=(
             right_shape,
             pltpu.VMEM((1, cot_width), bf16),
-            pltpu.VMEM((feature_count // 128, 128), jnp.int32),
-            pltpu.VMEM((feature_count // 128, 128), jnp.int32),
-            pltpu.VMEM((1, example_count), jnp.int32),
-            pltpu.VMEM((1, 1, 128), bf16),
+            pltpu.VMEM((2, width, quarter), bf16),
+            pltpu.VMEM((example_count, tokens), bf16),
+            pltpu.VMEM(chunk, bf16),
+            pltpu.VMEM(table_shape, jnp.int32),
+            pltpu.VMEM(table_shape, jnp.int32),
         ),
-        in_specs=[anywhere] * 5,
-        out_specs=(whole,) * 6,
+        in_specs=[anywhere] * 6,
+        out_specs=(whole,) * 7,
         scratch_shapes=[
             pltpu.VMEM(cotangent.shape, bf16),
             pltpu.VMEM((model_width // lanes, lanes), jnp.int32),
-            pltpu.SemaphoreType.DMA((5,)),
+            pltpu.VMEM((1, example_count), jnp.int32),
+            pltpu.SemaphoreType.DMA((6,)),
         ],
         compiler_params=params,
     )(
@@ -283,9 +332,8 @@
         in_hbm(feat_col.reshape(-1, 128)),
         in_hbm(feat_row.reshape(-1, 128)),
         in_hbm(lengths.reshape(1, -1)),
+        in_hbm(inverse_rows),
     )
-    held = held + token[:, :, :1]
-    hidden_parts = (held, swap(held, "rows", 1))
     right = pl.pallas_call(
         functools.partial(right_kernel, row_count),
         out_shape=right_shape,
@@ -296,20 +344,20 @@
 
     def features(flip):
         def kernel(*refs):
-            feature_kernel(flip, row_count, masks, refs[:2], *refs[2:])
+            feature_kernel(flip, row_count, masks, refs[:parts], *refs[parts:])
 
         return pl.pallas_call(
             kernel,
             out_shape=jax.ShapeDtypeStruct((example_count, quarter), f32),
-            in_specs=[whole] * 5,
+            in_specs=[whole] * (parts + 4),
             out_specs=whole,
             compiler_params=params,
-        )(*hidden_parts, right, row_index, counts)
-
-    def load(is_own, after):
+        )(*hidden_parts, right, row_index, hidden_table, member)
+
+    def load(chunk_id, after):
         return pl.pallas_call(
-            functools.partial(load_kernel, is_own),
-            out_shape=(pltpu.VMEM((out_rows, quarter), bf16), pltpu.VMEM((8, 128), f32)),
+            functools.partial(load_kernel, chunk_id),
+            out_shape=(pltpu.VMEM(chunk, bf16), pltpu.VMEM((8, 128), f32)),
             in_specs=[anywhere, whole],
             out_specs=(whole, whole),
             scratch_shapes=[pltpu.SemaphoreType.DMA],
@@ -340,28 +388,29 @@
         send, total = add_up(total, received, count // 2 if axis == "ex" else count, token)
         token = None
         if len(matrices) < 2:
-            matrix, token = load(len(matrices) == 0, send)
+            matrix, token = load(1 + len(matrices), send)
             matrices.append(matrix)
         received = swap(send, axis, mask)
-    own_matrix, near_matrix = matrices
+    matrix_1, matrix_2 = matrices
     (low,) = add_up(total, received, received.shape[0], token, norm_scale)
     near_low = swap(low, "rows", 1)
 
-    part = pl.pallas_call(
-        functools.partial(score_kernel, True),
-        out_shape=jax.ShapeDtypeStruct((2 * own_examples, out_rows), f32),
-        in_specs=[whole, whole],
-        out_specs=whole,
+    part, matrix_3 = pl.pallas_call(
+        own_score_kernel,
+        out_shape=(pltpu.VMEM((2 * own_examples, out_rows), f32), pltpu.VMEM(chunk, bf16)),
+        in_specs=[whole] * 3 + [anywhere],
+        out_specs=(whole, whole),
+        scratch_shapes=[pltpu.SemaphoreType.DMA],
         compiler_params=params,
-    )(low, own_matrix)
-    own_shape = jax.ShapeDtypeStruct((own_examples, out_rows), f32)
+    )(low, matrix_0, matrix_1, in_hbm(inverse_rows))
+    own_shape = pltpu.VMEM((own_examples, out_rows), f32)
     send, keep = pl.pallas_call(
-        functools.partial(score_kernel, False),
+        near_score_kernel,
         out_shape=(own_shape, own_shape),
-        in_specs=[whole, whole, whole],
+        in_specs=[whole] * 4,
         out_specs=(whole, whole),
         compiler_params=params,
-    )(near_low, near_matrix, part)
+    )(near_low, matrix_2, matrix_3, part)
     return (keep + swap(send, "ex", 1)).astype(bf16)
 
 

time: 37.5 us -> 35 us (0.933)
  waiting for transfers between devices: 2.87 us -> 6.3 us
  starting transfers between devices: 14.7 us -> 11.3 us
  Pallas kernels: 18.9 us -> 16.4 us
    ppermute x8 -> x9, waiting for transfers between devices: 2.87 us -> 6.3 us  [swap(): lax.ppermute(values, axis, [(rank, rank ^ mask) for rank in range(size)])]
    ppermute x8 -> x9, starting transfers between devices: 14.7 us -> 11.3 us  [swap(): lax.ppermute(values, axis, [(rank, rank ^ mask) for rank in range(size)])]
    pallas_call x5, Pallas kernels: 13.7 us -> 11.7 us  [the longest x2 4.39 us: load(): pl.pallas_call(functools.partial(load_kernel, chunk_id), out_shape=(pltpu...]
    pallas_call x2, Pallas kernels: 2.89 us -> 2.43 us  [features(): pl.pallas_call(kernel, out_shape=jax.ShapeDtypeStruct((example_count, qua...]
  transfers between devices with their start and end apart: 8 -> 9, of which waited for: 5 -> 6; matrix products, arithmetic and copies ran while one was open for 0% -> 0% of each run, Pallas kernels for 41% -> 37%
where the time goes in v3:
time: 35 us; the launch traced here: 34.8 us
  Pallas kernels  16.4 us (47%)
  starting transfers between devices  11.3 us (32%)
  waiting for transfers between devices  6.3 us (18%)
  other arithmetic  0.62 us (2%)
    ppermute x9, starting transfers between devices, swap(): lax.ppermute(values, axis, [(rank, rank ^ mask) for rank in range(size)])  11.3 us
    ppermute x9, waiting for transfers between devices, swap(): lax.ppermute(values, axis, [(rank, rank ^ mask) for rank in range(size)])  6.3 us
    pallas_call x2, Pallas kernels, load(): pl.pallas_call(functools.partial(load_kernel, chunk_id), out_shape=(pltpu...  4.39 us
    pallas_call x1, Pallas kernels, local(): pl.pallas_call(functools.partial(own_kernel, row_count), out_shape=(right...  2.75 us
    pallas_call x2, Pallas kernels, features(): pl.pallas_call(kernel, out_shape=jax.ShapeDtypeStruct((example_count, qua...  2.43 us
    pallas_call x1, Pallas kernels, local(): pl.pallas_call(own_score_kernel, out_shape=(pltpu.VMEM((2 * own_examples,...  2.29 us
    pallas_call x1, Pallas kernels, local(): pl.pallas_call(near_score_kernel, out_shape=(own_shape, own_shape), in_sp...  2.27 us
    pallas_call x1, Pallas kernels, local(): pl.pallas_call(functools.partial(right_kernel, row_count), out_shape=righ...  1.44 us
  transfers between devices with their start and end apart: 9, of which 6 were waited for; matrix products, arithmetic and copies ran while one was open for 0% of the time, Pallas kernels for 37%

profile of v3, /device:TPU:0, one launch (start us, length us, event | category | flops | bytes accessed | tf_op | source)
XLA Modules:
  0.0 34.8 jit_solution(641029520018729367)
XLA Ops:
  0.0 3.0 %collective-permute-start.3 = (bf16[128,1024]{1,0:T(8,128)(2,1)}, bf16[128,1024]{1,0:T(8,128)(2,1)S(1)}, u32[]{:S(2)}, u32[]{:S(2)}) collective-permute-start(bf16[128,1024]{1,0:T(8,128)(2,1)} %refs_0_.1), channel_id=1, source_target_pairs={{0,4},{4,0},{8,12},{12,8},{1,5},{5,1},{9,13},{13,9},{2,6},{6,2},{1... | collective-permute-start | bytes 786440 | tf_op jit(solution)/shard_map/ppermute | solution.py:23
  3.0 0.8 %shard_map.82.refs_0_ = bf16[1,128,128]{2,1,0:T(8,128)(2,1)S(1)} custom-call(bf16[128,128]{1,0:T(8,128)(2,1)} %hidden_in.1, s32[1,128]{1,0:T(1,128)} %bitcast.8), custom_call_target="tpu_custom_call" | custom-call | tf_op jit(solution)/shard_map/pallas_call | solution.py:283
  3.8 2.5 %collective-permute-start.2 = (bf16[1,128,128]{2,1,0:T(8,128)(2,1)S(1)}, bf16[1,128,128]{2,1,0:T(8,128)(2,1)S(1)}, u32[]{:S(2)}, u32[]{:S(2)}) collective-permute-start(bf16[1,128,128]{2,1,0:T(8,128)(2,1)S(1)} %shard_map.82.refs_0_), channel_id=1, source_target_pairs={{0,12},{4,8},{8,4},{12,0},{1,13},{5,9},{9,5},{13,1},{2,14},{6,10},... | collective-permute-start | bytes 98312 | tf_op jit(solution)/shard_map/ppermute | solution.py:23
  6.4 0.2 collective-permute-start.1
  6.6 1.7 %collective-permute-start = (bf16[1,128,128]{2,1,0:T(8,128)(2,1)S(1)}, bf16[1,128,128]{2,1,0:T(8,128)(2,1)S(1)}, u32[]{:S(2)}, u32[]{:S(2)}) collective-permute-start(bf16[1,128,128]{2,1,0:T(8,128)(2,1)S(1)} %shard_map.82.refs_0_), channel_id=1, source_target_pairs={{0,4},{4,0},{8,12},{12,8},{1,5},{5,1},{9,13},{13,9},{2,6},{6,2},{1... | collective-permute-start | bytes 98312 | tf_op jit(solution)/shard_map/ppermute | solution.py:23
  8.3 2.8 %shard_map.83 = (f32[2,128,2048]{2,1,0:T(8,128)S(1)}, bf16[1,1024]{1,0:T(2,128)(2,1)S(1)}, bf16[2,128,2048]{2,1,0:T(8,128)(2,1)S(1)}, bf16[32,128]{1,0:T(8,128)(...) custom-call(bf16[128,1024]{1,0:T(8,128)(2,1)} %refs_0_.1, ...), custom_call_target="tpu_custom_call" | custom-call | tf_op jit(solution)/shard_map/pallas_call | solution.py:309
  11.0 0.0 collective-permute-done.3.cot_ref
  11.0 1.4 %shard_map.84.refs_4_ = f32[2,128,2048]{2,1,0:T(8,128)S(1)} custom-call(bf16[128,1024]{1,0:T(8,128)(2,1)S(1)} %collective-permute-done.3.cot_ref, bf16[1,1024]{1,0:T(2,128)(2,1)S(1)} %get-tuple-element.24.sign_ref, s32[64,128]{1,0:T(8,128)S(1)} %get-tuple-element.25.col_ref, f32[2,128,2048]{2,1,0:T(8,128)S(1)} %get-tuple-element.26.own_ref), custom_call_target="tpu_custom_call" | custom-call | tf_op jit(solution)/shard_map/pallas_call | solution.py:337
  12.5 0.6 %collective-permute-done.2.refs_3_ = bf16[1,128,128]{2,1,0:T(8,128)(2,1)S(1)} collective-permute-done((bf16[1,128,128]{2,1,0:T(8,128)(2,1)S(1)}, bf16[1,128,128]{2,1,0:T(8,128)(2,1)S(1)}, u32[]{:S(2)}, u32[]{:S(2)}) %collective-permute-start.2) | collective-permute-done | bytes 32800 | tf_op jit(solution)/shard_map/ppermute | solution.py:23
  13.1 0.0 collective-permute-done.1.refs_2_
  13.1 0.0 collective-permute-done.refs_1_
  13.1 1.2 %shard_map.86 = f32[32,2048]{1,0:T(8,128)S(1)} custom-call(bf16[1,128,128]{2,1,0:T(8,128)(2,1)S(1)} %shard_map.82.refs_0_, bf16[1,128,128]{2,1,0:T(8,128)(2,1)S(1)} %collective-permute-done.refs_1_, bf16[1,128,128]{2,1,0:T(8,128)(2,1)S(1)} %collective-permute-done.1.refs_2_, bf16[1,128,128]{2,1,0:T(8,128)(2,1)S(1)} %collective-permute-done.2.refs_3_, ...), custom_call_target="tpu_custom_call" | custom-call | tf_op jit(solution)/shard_map/pallas_call | solution.py:349
  14.4 0.1 collective-permute-start.4
  14.4 1.2 %shard_map.85.kept_ref = f32[32,2048]{1,0:T(8,128)S(1)} custom-call(bf16[1,128,128]{2,1,0:T(8,128)(2,1)S(1)} %shard_map.82.refs_0_, bf16[1,128,128]{2,1,0:T(8,128)(2,1)S(1)} %collective-permute-done.refs_1_, bf16[1,128,128]{2,1,0:T(8,128)(2,1)S(1)} %collective-permute-done.1.refs_2_, bf16[1,128,128]{2,1,0:T(8,128)(2,1)S(1)} %collective-permute-done.2.refs_3_, ...), custom_call_target="tpu_custom_call" | custom-call | tf_op jit(solution)/shard_map/pallas_call | solution.py:349
  15.6 0.3 collective-permute-done.4.received_ref
  16.0 1.6 %collective-permute-start.5 = (bf16[16,2048]{1,0:T(8,128)(2,1)S(1)}, bf16[16,2048]{1,0:T(8,128)(2,1)S(1)}, u32[]{:S(2)}, u32[]{:S(2)}) collective-permute-start(bf16[16,2048]{1,0:T(8,128)(2,1)S(1)} %get-tuple-element.31.after_ref), channel_id=1, source_target_pairs={{0,2},{1,3},{2,0},{3,1},{4,6},{5,7},{6,4},{7,5},{8,10},{9,11},{10,... | collective-permute-start | bytes 196616 | tf_op jit(solution)/shard_map/ppermute | solution.py:23
  17.5 2.2 %shard_map.88 = (bf16[1024,2048]{1,0:T(8,128)(2,1)S(1)}, f32[8,128]{1,0:T(8,128)S(1)}) custom-call(bf16[2048,8192]{1,0:T(8,128)(2,1)} %matrix_ref.5, bf16[16,2048]{1,0:T(8,128)(2,1)S(1)} %get-tuple-element.31.after_ref), custom_call_target="tpu_custom_call" | custom-call | tf_op jit(solution)/shard_map/pallas_call | solution.py:358
  19.7 0.6 %collective-permute-done.5.received_ref = bf16[16,2048]{1,0:T(8,128)(2,1)S(1)} collective-permute-done((bf16[16,2048]{1,0:T(8,128)(2,1)S(1)}, bf16[16,2048]{1,0:T(8,128)(2,1)S(1)}, u32[]{:S(2)}, u32[]{:S(2)}) %collective-permute-start.5) | collective-permute-done | bytes 65568 | tf_op jit(solution)/shard_map/ppermute | solution.py:23
  20.3 1.7 %collective-permute-start.6 = (bf16[16,2048]{1,0:T(8,128)(2,1)S(1)}, bf16[16,2048]{1,0:T(8,128)(2,1)S(1)}, u32[]{:S(2)}, u32[]{:S(2)}) collective-permute-start(bf16[16,2048]{1,0:T(8,128)(2,1)S(1)} %get-tuple-element.34.after_ref), channel_id=1, source_target_pairs={{0,8},{4,12},{8,0},{12,4},{1,9},{5,13},{9,1},{13,5},{2,10},{6,14},... | collective-permute-start | bytes 196616 | tf_op jit(solution)/shard_map/ppermute | solution.py:23
  22.1 2.2 %shard_map.90 = (bf16[1024,2048]{1,0:T(8,128)(2,1)S(1)}, f32[8,128]{1,0:T(8,128)S(1)}) custom-call(bf16[2048,8192]{1,0:T(8,128)(2,1)} %matrix_ref.5, bf16[16,2048]{1,0:T(8,128)(2,1)S(1)} %get-tuple-element.34.after_ref), custom_call_target="tpu_custom_call" | custom-call | tf_op jit(solution)/shard_map/pallas_call | solution.py:358
  24.3 2.0 %collective-permute-done.6.received_ref = bf16[16,2048]{1,0:T(8,128)(2,1)S(1)} collective-permute-done((bf16[16,2048]{1,0:T(8,128)(2,1)S(1)}, bf16[16,2048]{1,0:T(8,128)(2,1)S(1)}, u32[]{:S(2)}, u32[]{:S(2)}) %collective-permute-start.6) | collective-permute-done | bytes 65568 | tf_op jit(solution)/shard_map/ppermute | solution.py:23
  26.3 0.5 %collective-permute-start.7 = (bf16[16,2048]{1,0:T(8,128)(2,1)S(1)}, bf16[16,2048]{1,0:T(8,128)(2,1)S(1)}, u32[]{:S(2)}, u32[]{:S(2)}) collective-permute-start(bf16[16,2048]{1,0:T(8,128)(2,1)S(1)} %shard_map.91.low_ref), channel_id=1, source_target_pairs={{0,4},{4,0},{8,12},{12,8},{1,5},{5,1},{9,13},{13,9},{2,6},{6,2},{1... | collective-permute-start | bytes 196616 | tf_op jit(solution)/shard_map/ppermute | solution.py:23
  26.8 2.3 %shard_map.92 = (f32[16,2048]{1,0:T(8,128)S(1)}, bf16[1024,2048]{1,0:T(8,128)(2,1)S(1)}) custom-call(bf16[16,2048]{1,0:T(8,128)(2,1)S(1)} %shard_map.91.low_ref, bf16[1024,2048]{1,0:T(8,128)(2,1)S(1)} %get-tuple-element.37.lower_ref, bf16[1024,2048]{1,0:T(8,128)(2,1)S(1)} %get-tuple-element.38.upper_ref, bf16[2048,8192]{1,0:T(8,128)(2,1)} %matrix_ref.5), custom_call_target="tpu_custom_call" | custom-call | tf_op jit(solution)/shard_map/pallas_call | solution.py:398
  29.1 1.5 %collective-permute-done.7.low_ref = bf16[16,2048]{1,0:T(8,128)(2,1)S(1)} collective-permute-done((bf16[16,2048]{1,0:T(8,128)(2,1)S(1)}, bf16[16,2048]{1,0:T(8,128)(2,1)S(1)}, u32[]{:S(2)}, u32[]{:S(2)}) %collective-permute-start.7) | collective-permute-done | bytes 65568 | tf_op jit(solution)/shard_map/ppermute | solution.py:23
  30.6 2.3 %shard_map.93 = (f32[8,2048]{1,0:T(8,128)S(1)}, f32[8,2048]{1,0:T(8,128)S(1)}) custom-call(bf16[16,2048]{1,0:T(8,128)(2,1)S(1)} %collective-permute-done.7.low_ref, bf16[1024,2048]{1,0:T(8,128)(2,1)S(1)} %get-tuple-element.36.lower_ref, bf16[1024,2048]{1,0:T(8,128)(2,1)S(1)} %get-tuple-element.39.upper_ref, f32[16,2048]{1,0:T(8,128)S(1)} %get-tuple-element.40.sum_ref), custom_call_target="tpu_custom_call" | custom-call | tf_op jit(solution)/shard_map/pallas_call | solution.py:407
  32.9 0.0 collective-permute-start.8
  32.9 1.3 %collective-permute-done.8 = f32[8,2048]{1,0:T(8,128)S(1)} collective-permute-done((f32[8,2048]{1,0:T(8,128)S(1)}, f32[8,2048]{1,0:T(8,128)S(1)}, u32[]{:S(2)}, u32[]{:S(2)}) %collective-permute-start.8) | collective-permute-done | bytes 65568 | tf_op jit(solution)/shard_map/ppermute | solution.py:23
  34.2 0.6 %add_convert_fusion = bf16[8,2048]{1,0:T(8,128)(2,1)} fusion(f32[8,2048]{1,0:T(8,128)S(1)} %get-tuple-element.41, f32[8,2048]{1,0:T(8,128)S(1)} %collective-permute-done.8), kind=kLoop, calls=%fused_computation | loop fusion | flops 32768 | bytes 163840 | tf_op jit(solution)/shard_map/convert_element_type | solution.py:414
  (3 shorter events, 0.1 us)
Async XLA Ops:
  0.0 11.0 %collective-permute-start.3 = (bf16[128,1024]{1,0:T(8,128)(2,1)}, bf16[128,1024]{1,0:T(8,128)(2,1)S(1)}, u32[]{:S(2)}, u32[]{:S(2)}) collective-permute-start(bf16[128,1024]{1,0:T(8,128)(2,1)} %refs_0_.1), channel_id=1, source_target_pairs={{0,4},{4,0},{8,12},{12,8},{1,5},{5,1},{9,13},{13,9},{2,6},{6,2},{1... | collective-permute-start | bytes 786440 | tf_op jit(solution)/shard_map/ppermute | solution.py:23
  3.8 9.3 %collective-permute-start.2 = (bf16[1,128,128]{2,1,0:T(8,128)(2,1)S(1)}, bf16[1,128,128]{2,1,0:T(8,128)(2,1)S(1)}, u32[]{:S(2)}, u32[]{:S(2)}) collective-permute-start(bf16[1,128,128]{2,1,0:T(8,128)(2,1)S(1)} %shard_map.82.refs_0_), channel_id=1, source_target_pairs={{0,12},{4,8},{8,4},{12,0},{1,13},{5,9},{9,5},{13,1},{2,14},{6,10},... | collective-permute-start | bytes 98312 | tf_op jit(solution)/shard_map/ppermute | solution.py:23
  6.4 6.8 %collective-permute-start.1 = (bf16[1,128,128]{2,1,0:T(8,128)(2,1)S(1)}, bf16[1,128,128]{2,1,0:T(8,128)(2,1)S(1)}, u32[]{:S(2)}, u32[]{:S(2)}) collective-permute-start(bf16[1,128,128]{2,1,0:T(8,128)(2,1)S(1)} %shard_map.82.refs_0_), channel_id=1, source_target_pairs={{0,8},{4,12},{8,0},{12,4},{1,9},{5,13},{9,1},{13,5},{2,10},{6,14},... | collective-permute-start | bytes 98312 | tf_op jit(solution)/shard_map/ppermute | solution.py:23
  6.6 6.6 %collective-permute-start = (bf16[1,128,128]{2,1,0:T(8,128)(2,1)S(1)}, bf16[1,128,128]{2,1,0:T(8,128)(2,1)S(1)}, u32[]{:S(2)}, u32[]{:S(2)}) collective-permute-start(bf16[1,128,128]{2,1,0:T(8,128)(2,1)S(1)} %shard_map.82.refs_0_), channel_id=1, source_target_pairs={{0,4},{4,0},{8,12},{12,8},{1,5},{5,1},{9,13},{13,9},{2,6},{6,2},{1... | collective-permute-start | bytes 98312 | tf_op jit(solution)/shard_map/ppermute | solution.py:23
  14.4 1.6 %collective-permute-start.4 = (f32[32,2048]{1,0:T(8,128)S(1)}, f32[32,2048]{1,0:T(8,128)S(1)}, u32[]{:S(2)}, u32[]{:S(2)}) collective-permute-start(f32[32,2048]{1,0:T(8,128)S(1)} %shard_map.86), channel_id=1, source_target_pairs={{0,1},{1,0},{2,3},{3,2},{4,5},{5,4},{6,7},{7,6},{8,9},{9,8},{10,11... | collective-permute-start | bytes 786440 | tf_op jit(solution)/shard_map/ppermute | solution.py:23
  16.0 4.3 %collective-permute-start.5 = (bf16[16,2048]{1,0:T(8,128)(2,1)S(1)}, bf16[16,2048]{1,0:T(8,128)(2,1)S(1)}, u32[]{:S(2)}, u32[]{:S(2)}) collective-permute-start(bf16[16,2048]{1,0:T(8,128)(2,1)S(1)} %get-tuple-element.31.after_ref), channel_id=1, source_target_pairs={{0,2},{1,3},{2,0},{3,1},{4,6},{5,7},{6,4},{7,5},{8,10},{9,11},{10,... | collective-permute-start | bytes 196616 | tf_op jit(solution)/shard_map/ppermute | solution.py:23
  20.3 5.9 %collective-permute-start.6 = (bf16[16,2048]{1,0:T(8,128)(2,1)S(1)}, bf16[16,2048]{1,0:T(8,128)(2,1)S(1)}, u32[]{:S(2)}, u32[]{:S(2)}) collective-permute-start(bf16[16,2048]{1,0:T(8,128)(2,1)S(1)} %get-tuple-element.34.after_ref), channel_id=1, source_target_pairs={{0,8},{4,12},{8,0},{12,4},{1,9},{5,13},{9,1},{13,5},{2,10},{6,14},... | collective-permute-start | bytes 196616 | tf_op jit(solution)/shard_map/ppermute | solution.py:23
  26.3 4.3 %collective-permute-start.7 = (bf16[16,2048]{1,0:T(8,128)(2,1)S(1)}, bf16[16,2048]{1,0:T(8,128)(2,1)S(1)}, u32[]{:S(2)}, u32[]{:S(2)}) collective-permute-start(bf16[16,2048]{1,0:T(8,128)(2,1)S(1)} %shard_map.91.low_ref), channel_id=1, source_target_pairs={{0,4},{4,0},{8,12},{12,8},{1,5},{5,1},{9,13},{13,9},{2,6},{6,2},{1... | collective-permute-start | bytes 196616 | tf_op jit(solution)/shard_map/ppermute | solution.py:23
  32.9 1.3 %collective-permute-start.8 = (f32[8,2048]{1,0:T(8,128)S(1)}, f32[8,2048]{1,0:T(8,128)S(1)}, u32[]{:S(2)}, u32[]{:S(2)}) collective-permute-start(f32[8,2048]{1,0:T(8,128)S(1)} %get-tuple-element.42), channel_id=1, source_target_pairs={{0,1},{1,0},{2,3},{3,2},{4,5},{5,4},{6,7},{7,6},{8,9},{9,8},{10,11... | collective-permute-start | bytes 196616 | tf_op jit(solution)/shard_map/ppermute | solution.py:23

commit v4 on v3

--- a/solution.py
+++ b/solution.py
@@ -67,20 +67,21 @@
     return total
 
 
-def right_block(values, col_ref, rank, block_id, row_count, store):
+def quarter_index(ref, flip):
+    rows = ref.shape[0] // 4
+    half = (lax.axis_index("ex") & 1) ^ flip
+    return index_row(ref, ((lax.axis_index("rows") & 1) * 2 + half) * rows, rows)
+
+
+def right_block(values, index, block_id, row_count):
     width = values.shape[1]
-    lanes = col_ref.shape[1]
-    half_rows = col_ref.shape[0] // 2
-    first_row = (rank & 1) * half_rows
-    group = min(4, half_rows // 2)
     row_bits = row_count.bit_length() - 1
-    for step in range(half_rows // group):
-        index = index_row(col_ref, first_row + step * group, group)
-        part = cot_products(values, index % width, 256)
-        part = part * parity_sign((index // width) & block_id, row_bits)
-        half = step * group // (half_rows // 2)
-        at = step * group * lanes % (half_rows // 2 * lanes)
-        store(half, slice(at, at + group * lanes), part)
+    parts = []
+    for first in range(0, index.shape[1], 512):
+        group = index[:, first : first + 512]
+        part = cot_products(values, group % width, 256)
+        parts.append(part * parity_sign((group // width) & block_id, row_bits))
+    return parts
 
 
 def block_signs(sign_ref, block_id, width):
@@ -128,28 +129,20 @@
     width = cot_ref.shape[1]
     near_sign_ref[...] = block_signs(sign_ref, rank ^ 1, width)
 
-    def store(half, columns, part):
-        right_ref[half, :, columns] = part
-
     values = cot_ref[...] * block_signs(sign_ref, rank, width)
-    right_block(values, col_ref, rank, rank, row_count, store)
+    for flip in range(2):
+        first = 0
+        for part in right_block(values, quarter_index(col_ref, flip), rank, row_count):
+            right_ref[flip, :, first : first + part.shape[1]] = part
+            first += part.shape[1]
     tables(row_ref, len_ref, table_ref, member_ref)
     copies[-1].wait()
 
 
 def tables(row_ref, len_ref, table_ref, member_ref):
-    rank = lax.axis_index("rows")
-    lanes = row_ref.shape[1]
-    quarter_rows = row_ref.shape[0] // 4
-    first_row = (rank & 1) * 2 * quarter_rows
     width = table_ref.shape[1]
-    group = min(4, quarter_rows)
-    for step in range(2 * quarter_rows // group):
-        index = index_row(row_ref, first_row + step * group, group)
-        at = step * group % quarter_rows * lanes
-        table_ref[step * group // quarter_rows, :, at : at + group * lanes] = sign_columns(
-            index % width, width
-        )
+    for flip in range(2):
+        table_ref[flip] = sign_columns(quarter_index(row_ref, flip) % width, width)
     examples, tokens = member_ref.shape
     ex_rank = lax.axis_index("ex")
     ex_count = lax.axis_size("ex")
@@ -167,51 +160,41 @@
 
 
 def right_kernel(row_count, cot_ref, sign_ref, col_ref, own_ref, out_ref):
-    rank = lax.axis_index("rows")
-
-    def store(half, columns, part):
-        out_ref[half, :, columns] = own_ref[half, :, columns] + part
-
-    right_block(cot_ref[...] * sign_ref[...], col_ref, rank, rank ^ 1, row_count, store)
+    values = cot_ref[...] * sign_ref[...]
+    near = lax.axis_index("rows") ^ 1
+    for flip in range(2):
+        first = 0
+        for part in right_block(values, quarter_index(col_ref, flip), near, row_count):
+            columns = slice(first, first + part.shape[1])
+            out_ref[flip, :, columns] = own_ref[flip, :, columns] + part
+            first += part.shape[1]
 
 
 def feature_kernel(flip, row_count, masks, hidden_refs, right_ref, row_ref, table_ref, member_ref, out_ref):
     rank = lax.axis_index("rows")
-    half = (lax.axis_index("ex") & 1) ^ flip
-    width = table_ref.shape[1]
-    lanes = row_ref.shape[1]
-    quarter_rows = row_ref.shape[0] // 4
-    first_row = ((rank & 1) * 2 + half) * quarter_rows
     row_bits = row_count.bit_length() - 1
-    blocks = []
-    for ref in hidden_refs:
-        for block in range(ref.shape[0]):
-            blocks.append(ref[block])
+    blocks = [ref[block] for ref in hidden_refs for block in range(ref.shape[0])]
+    base = table_ref[flip]
+    high = quarter_index(row_ref, flip) // base.shape[0]
+    left = None
+    for first in range(0, len(masks), 4):
+        table = [
+            base * parity_sign(high & (rank ^ mask), row_bits).astype(bf16)
+            for mask in masks[first : first + 4]
+        ]
+        piece = jnp.dot(
+            jnp.concatenate(blocks[first : first + 4], axis=1),
+            jnp.concatenate(table, axis=0),
+            preferred_element_type=f32,
+        )
+        left = piece if left is None else left + piece
+    product = left * right_ref[flip]
+    high_part = product.astype(bf16)
+    low_part = (product - high_part.astype(f32)).astype(bf16)
     member = member_ref[...]
-    group = min(4, quarter_rows)
-    for step in range(quarter_rows // group):
-        columns = slice(step * group * lanes, (step + 1) * group * lanes)
-        index = index_row(row_ref, first_row + step * group, group)
-        base = table_ref[half, :, columns]
-        high = index // width
-        left = None
-        for first in range(0, len(masks), 4):
-            table = [
-                base * parity_sign(high & (rank ^ mask), row_bits).astype(bf16)
-                for mask in masks[first : first + 4]
-            ]
-            piece = jnp.dot(
-                jnp.concatenate(blocks[first : first + 4], axis=1),
-                jnp.concatenate(table, axis=0),
-                preferred_element_type=f32,
-            )
-            left = piece if left is None else left + piece
-        product = left * right_ref[half, :, columns]
-        high_part = product.astype(bf16)
-        low_part = (product - high_part.astype(f32)).astype(bf16)
-        out_ref[:, columns] = jnp.dot(member, high_part, preferred_element_type=f32) + jnp.dot(
-            member, low_part, preferred_element_type=f32
-        )
+    total = jnp.dot(member, high_part, preferred_element_type=f32)
+    total = total + jnp.dot(member, low_part, preferred_element_type=f32)
+    out_ref[...] = total.astype(out_ref.dtype)
 
 
 def load_kernel(chunk, matrix_ref, after_ref, out_ref, token_ref, sem):
@@ -221,14 +204,18 @@
     copy.wait()
 
 
-def add_kernel(scale, kept_ref, received_ref, *refs):
+def add_kernel(kept_ref, received_ref, *refs):
     total = kept_ref[...] + received_ref[...].astype(f32)
-    if scale is not None:
-        refs[-1][...] = (total * scale).astype(bf16)
-    else:
-        send_ref, total_ref = refs[-2:]
-        send_ref[...] = total[: send_ref.shape[0]].astype(bf16)
-        total_ref[...] = total[total.shape[0] - total_ref.shape[0] :]
+    send_ref, total_ref = refs[-2:]
+    send_ref[...] = total[: send_ref.shape[0]].astype(bf16)
+    total_ref[...] = total[total.shape[0] - total_ref.shape[0] :]
+
+
+def low_kernel(scale, count, *refs):
+    total = refs[0][...].astype(f32)
+    for ref in refs[1:count]:
+        total = total + ref[...].astype(f32)
+    refs[-1][...] = (total * scale).astype(bf16)
 
 
 def own_score_kernel(low_ref, lower_ref, upper_ref, matrix_ref, out_ref, held_ref, sem):
@@ -293,8 +280,8 @@
         compiler_params=params,
     )(in_hbm(hidden_acts), in_hbm(row_signs.reshape(1, -1)))
     group = min(row_count, 4)
-    hidden_parts = [signed] + [swap(signed, "rows", mask) for mask in range(1, group)]
-    masks = list(range(group))
+    masks = [0] + list(range(1, group))[::-1]
+    hidden_parts = [signed] + [swap(signed, "rows", mask) for mask in masks[1:]]
     step = group
     while step < row_count:
         held = jnp.concatenate(hidden_parts, axis=0)
@@ -348,7 +335,7 @@
 
         return pl.pallas_call(
             kernel,
-            out_shape=jax.ShapeDtypeStruct((example_count, quarter), f32),
+            out_shape=pltpu.VMEM((example_count, quarter), bf16 if flip else f32),
             in_specs=[whole] * (parts + 4),
             out_specs=whole,
             compiler_params=params,
@@ -364,36 +351,45 @@
             compiler_params=params,
         )(in_hbm(inverse_rows), after)
 
-    def add_up(kept, received, send_count, token, scale=None):
+    def add_up(kept, received, send_count, token):
         count = received.shape[0]
-        out_shape = [pltpu.VMEM((send_count, quarter), bf16)]
-        if scale is None:
-            out_shape.append(pltpu.VMEM((count - send_count % count, quarter), f32))
         return pl.pallas_call(
-            functools.partial(add_kernel, scale),
-            out_shape=out_shape,
+            add_kernel,
+            out_shape=(
+                pltpu.VMEM((send_count, quarter), bf16),
+                pltpu.VMEM((count - send_count % count, quarter), f32),
+            ),
             in_specs=[whole] * (2 + (token is not None)),
-            out_specs=[whole] * len(out_shape),
+            out_specs=(whole, whole),
             compiler_params=params,
         )(kept, received, *([] if token is None else [token]))
 
+    def features_low(terms, token):
+        return pl.pallas_call(
+            functools.partial(low_kernel, norm_scale, len(terms)),
+            out_shape=pltpu.VMEM(terms[0].shape, bf16),
+            in_specs=[whole] * (len(terms) + (token is not None)),
+            out_specs=whole,
+            compiler_params=params,
+        )(*terms, *([] if token is None else [token]))
+
     ex_masks = [1 << bit for bit in range(1, ex_count.bit_length() - 1)][::-1]
-    row_masks = [1 << bit for bit in range(1, row_count.bit_length() - 1)]
+    row_masks = [1 << bit for bit in range(2, row_count.bit_length() - 1)]
     received = swap(features(1), "ex", 1)
     total = features(0)
-    matrices, token = [], None
-    hops = [("ex", mask) for mask in ex_masks] + [("rows", mask) for mask in row_masks]
-    for axis, mask in hops:
+    matrix_1, token = None, None
+    for axis, mask in [("ex", mask) for mask in ex_masks] + [("rows", mask) for mask in row_masks]:
         count = received.shape[0]
         send, total = add_up(total, received, count // 2 if axis == "ex" else count, token)
         token = None
-        if len(matrices) < 2:
-            matrix, token = load(1 + len(matrices), send)
-            matrices.append(matrix)
+        if matrix_1 is None:
+            matrix_1, token = load(1, send)
         received = swap(send, axis, mask)
-    matrix_1, matrix_2 = matrices
-    (low,) = add_up(total, received, received.shape[0], token, norm_scale)
-    near_low = swap(low, "rows", 1)
+    send, total = add_up(total, received, received.shape[0], token)
+    matrix_2, token = load(2, send)
+    others = [swap(send, "rows", mask) for mask in range(1, group)]
+    low = features_low([total] + others[1:2], token)
+    near_low = features_low(others[0::2][::-1], None)
 
     part, matrix_3 = pl.pallas_call(
         own_score_kernel,

time: 35 us -> 33.4 us (0.954)
  waiting for transfers between devices: 6.3 us -> 3.57 us
  starting transfers between devices: 11.3 us -> 13.1 us
  Pallas kernels: 16.4 us -> 15.7 us
    ppermute x9 -> x10, waiting for transfers between devices: 6.3 us -> 3.57 us  [swap(): lax.ppermute(values, axis, [(rank, rank ^ mask) for rank in range(size)])]
    ppermute x9 -> x10, starting transfers between devices: 11.3 us -> 13.1 us  [swap(): lax.ppermute(values, axis, [(rank, rank ^ mask) for rank in range(size)])]
    pallas_call x5 -> x6, Pallas kernels: 2.52 us -> 1.63 us  [the longest x2 1.53 us: features(): pl.pallas_call(kernel, out_shape=pltpu.VMEM((example_count, quarter), bf1...]
  transfers between devices with their start and end apart: 9 -> 10, of which waited for: 6 -> 5; matrix products, arithmetic and copies ran while one was open for 0% -> 0% of each run, Pallas kernels for 37% -> 38%
where the time goes in v4:
time: 33.4 us; the launch traced here: 33.1 us
  Pallas kernels  15.7 us (47%)
  starting transfers between devices  13.1 us (39%)
  waiting for transfers between devices  3.57 us (11%)
  other arithmetic  0.62 us (2%)
    ppermute x10, starting transfers between devices, swap(): lax.ppermute(values, axis, [(rank, rank ^ mask) for rank in range(size)])  13.1 us
    pallas_call x2, Pallas kernels, load(): pl.pallas_call(functools.partial(load_kernel, chunk_id), out_shape=(pltpu...  4.39 us
    ppermute x10, waiting for transfers between devices, swap(): lax.ppermute(values, axis, [(rank, rank ^ mask) for rank in range(size)])  3.57 us
    pallas_call x1, Pallas kernels, local(): pl.pallas_call(functools.partial(own_kernel, row_count), out_shape=(right...  2.84 us
    pallas_call x1, Pallas kernels, local(): pl.pallas_call(own_score_kernel, out_shape=(pltpu.VMEM((2 * own_examples,...  2.3 us
    pallas_call x1, Pallas kernels, local(): pl.pallas_call(near_score_kernel, out_shape=(own_shape, own_shape), in_sp...  2.27 us
    pallas_call x2, Pallas kernels, features(): pl.pallas_call(kernel, out_shape=pltpu.VMEM((example_count, quarter), bf1...  1.53 us
    pallas_call x1, Pallas kernels, local(): pl.pallas_call(functools.partial(right_kernel, row_count), out_shape=righ...  1.44 us
  transfers between devices with their start and end apart: 10, of which 5 were waited for; matrix products, arithmetic and copies ran while one was open for 0% of the time, Pallas kernels for 38%

profile of v4, /device:TPU:0, one launch (start us, length us, event | category | flops | bytes accessed | tf_op | source)
XLA Modules:
  0.0 33.1 jit_solution(11534005294482362806)
XLA Ops:
  0.0 3.0 %collective-permute-start.3 = (bf16[128,1024]{1,0:T(8,128)(2,1)}, bf16[128,1024]{1,0:T(8,128)(2,1)S(1)}, u32[]{:S(2)}, u32[]{:S(2)}) collective-permute-start(bf16[128,1024]{1,0:T(8,128)(2,1)} %refs_0_.1), channel_id=1, source_target_pairs={{0,4},{4,0},{8,12},{12,8},{1,5},{5,1},{9,13},{13,9},{2,6},{6,2},{1... | collective-permute-start | bytes 786440 | tf_op jit(solution)/shard_map/ppermute | solution.py:23
  3.0 0.8 %shard_map.82.refs_0_ = bf16[1,128,128]{2,1,0:T(8,128)(2,1)S(1)} custom-call(bf16[128,128]{1,0:T(8,128)(2,1)} %hidden_in.1, s32[1,128]{1,0:T(1,128)} %bitcast.8), custom_call_target="tpu_custom_call" | custom-call | tf_op jit(solution)/shard_map/pallas_call | solution.py:270
  3.8 2.5 %collective-permute-start = (bf16[1,128,128]{2,1,0:T(8,128)(2,1)S(1)}, bf16[1,128,128]{2,1,0:T(8,128)(2,1)S(1)}, u32[]{:S(2)}, u32[]{:S(2)}) collective-permute-start(bf16[1,128,128]{2,1,0:T(8,128)(2,1)S(1)} %shard_map.82.refs_0_), channel_id=1, source_target_pairs={{0,12},{4,8},{8,4},{12,0},{1,13},{5,9},{9,5},{13,1},{2,14},{6,10},... | collective-permute-start | bytes 98312 | tf_op jit(solution)/shard_map/ppermute | solution.py:23
  6.4 0.2 collective-permute-start.1
  6.6 1.7 %collective-permute-start.2 = (bf16[1,128,128]{2,1,0:T(8,128)(2,1)S(1)}, bf16[1,128,128]{2,1,0:T(8,128)(2,1)S(1)}, u32[]{:S(2)}, u32[]{:S(2)}) collective-permute-start(bf16[1,128,128]{2,1,0:T(8,128)(2,1)S(1)} %shard_map.82.refs_0_), channel_id=1, source_target_pairs={{0,4},{4,0},{8,12},{12,8},{1,5},{5,1},{9,13},{13,9},{2,6},{6,2},{1... | collective-permute-start | bytes 98312 | tf_op jit(solution)/shard_map/ppermute | solution.py:23
  8.3 2.8 %shard_map.83 = (f32[2,128,2048]{2,1,0:T(8,128)S(1)}, bf16[1,1024]{1,0:T(2,128)(2,1)S(1)}, bf16[2,128,2048]{2,1,0:T(8,128)(2,1)S(1)}, bf16[32,128]{1,0:T(8,128)(...) custom-call(bf16[128,1024]{1,0:T(8,128)(2,1)} %refs_0_.1, ...), custom_call_target="tpu_custom_call" | custom-call | tf_op jit(solution)/shard_map/pallas_call | solution.py:296
  11.1 0.0 collective-permute-done.3.cot_ref
  11.1 1.4 %shard_map.84.refs_4_ = f32[2,128,2048]{2,1,0:T(8,128)S(1)} custom-call(bf16[128,1024]{1,0:T(8,128)(2,1)S(1)} %collective-permute-done.3.cot_ref, bf16[1,1024]{1,0:T(2,128)(2,1)S(1)} %get-tuple-element.24.sign_ref, s32[64,128]{1,0:T(8,128)S(1)} %get-tuple-element.25.col_ref, f32[2,128,2048]{2,1,0:T(8,128)S(1)} %get-tuple-element.26.own_ref), custom_call_target="tpu_custom_call" | custom-call | tf_op jit(solution)/shard_map/pallas_call | solution.py:324
  12.6 0.5 %collective-permute-done.refs_1_ = bf16[1,128,128]{2,1,0:T(8,128)(2,1)S(1)} collective-permute-done((bf16[1,128,128]{2,1,0:T(8,128)(2,1)S(1)}, bf16[1,128,128]{2,1,0:T(8,128)(2,1)S(1)}, u32[]{:S(2)}, u32[]{:S(2)}) %collective-permute-start) | collective-permute-done | bytes 32800 | tf_op jit(solution)/shard_map/ppermute | solution.py:23
  13.1 0.0 collective-permute-done.1.refs_2_
  13.1 0.0 collective-permute-done.2.refs_3_
  13.1 0.8 %shard_map.86 = bf16[32,2048]{1,0:T(8,128)(2,1)S(1)} custom-call(bf16[1,128,128]{2,1,0:T(8,128)(2,1)S(1)} %shard_map.82.refs_0_, bf16[1,128,128]{2,1,0:T(8,128)(2,1)S(1)} %collective-permute-done.refs_1_, bf16[1,128,128]{2,1,0:T(8,128)(2,1)S(1)} %collective-permute-done.1.refs_2_, bf16[1,128,128]{2,1,0:T(8,128)(2,1)S(1)} %collective-permute-done.2.refs_3_, ...), custom_call_target="tpu_custom_call" | custom-call | tf_op jit(solution)/shard_map/pallas_call | solution.py:336
  13.9 0.1 collective-permute-start.4
  14.0 0.8 %shard_map.85.kept_ref = f32[32,2048]{1,0:T(8,128)S(1)} custom-call(bf16[1,128,128]{2,1,0:T(8,128)(2,1)S(1)} %shard_map.82.refs_0_, bf16[1,128,128]{2,1,0:T(8,128)(2,1)S(1)} %collective-permute-done.refs_1_, bf16[1,128,128]{2,1,0:T(8,128)(2,1)S(1)} %collective-permute-done.1.refs_2_, bf16[1,128,128]{2,1,0:T(8,128)(2,1)S(1)} %collective-permute-done.2.refs_3_, ...), custom_call_target="tpu_custom_call" | custom-call | tf_op jit(solution)/shard_map/pallas_call | solution.py:336
  14.8 0.6 %collective-permute-done.4.received_ref = bf16[32,2048]{1,0:T(8,128)(2,1)S(1)} collective-permute-done((bf16[32,2048]{1,0:T(8,128)(2,1)S(1)}, bf16[32,2048]{1,0:T(8,128)(2,1)S(1)}, u32[]{:S(2)}, u32[]{:S(2)}) %collective-permute-start.4) | collective-permute-done | bytes 131104 | tf_op jit(solution)/shard_map/ppermute | solution.py:23
  15.4 1.6 %collective-permute-start.5 = (bf16[16,2048]{1,0:T(8,128)(2,1)S(1)}, bf16[16,2048]{1,0:T(8,128)(2,1)S(1)}, u32[]{:S(2)}, u32[]{:S(2)}) collective-permute-start(bf16[16,2048]{1,0:T(8,128)(2,1)S(1)} %get-tuple-element.31.after_ref), channel_id=1, source_target_pairs={{0,2},{1,3},{2,0},{3,1},{4,6},{5,7},{6,4},{7,5},{8,10},{9,11},{10,... | collective-permute-start | bytes 196616 | tf_op jit(solution)/shard_map/ppermute | solution.py:23
  16.9 2.2 %shard_map.88 = (bf16[1024,2048]{1,0:T(8,128)(2,1)S(1)}, f32[8,128]{1,0:T(8,128)S(1)}) custom-call(bf16[2048,8192]{1,0:T(8,128)(2,1)} %matrix_ref.5, bf16[16,2048]{1,0:T(8,128)(2,1)S(1)} %get-tuple-element.31.after_ref), custom_call_target="tpu_custom_call" | custom-call | tf_op jit(solution)/shard_map/pallas_call | solution.py:345
  19.1 0.6 %collective-permute-done.5.received_ref = bf16[16,2048]{1,0:T(8,128)(2,1)S(1)} collective-permute-done((bf16[16,2048]{1,0:T(8,128)(2,1)S(1)}, bf16[16,2048]{1,0:T(8,128)(2,1)S(1)}, u32[]{:S(2)}, u32[]{:S(2)}) %collective-permute-start.5) | collective-permute-done | bytes 65568 | tf_op jit(solution)/shard_map/ppermute | solution.py:23
  19.7 1.7 %collective-permute-start.8 = (bf16[16,2048]{1,0:T(8,128)(2,1)S(1)}, bf16[16,2048]{1,0:T(8,128)(2,1)S(1)}, u32[]{:S(2)}, u32[]{:S(2)}) collective-permute-start(bf16[16,2048]{1,0:T(8,128)(2,1)S(1)} %get-tuple-element.33.after_ref), channel_id=1, source_target_pairs={{0,8},{4,12},{8,0},{12,4},{1,9},{5,13},{9,1},{13,5},{2,10},{6,14},... | collective-permute-start | bytes 196616 | tf_op jit(solution)/shard_map/ppermute | solution.py:23
  21.5 1.8 %collective-permute-start.6 = (bf16[16,2048]{1,0:T(8,128)(2,1)S(1)}, bf16[16,2048]{1,0:T(8,128)(2,1)S(1)}, u32[]{:S(2)}, u32[]{:S(2)}) collective-permute-start(bf16[16,2048]{1,0:T(8,128)(2,1)S(1)} %get-tuple-element.33.after_ref), channel_id=1, source_target_pairs={{0,12},{4,8},{8,4},{12,0},{1,13},{5,9},{9,5},{13,1},{2,14},{6,10},... | collective-permute-start | bytes 196616 | tf_op jit(solution)/shard_map/ppermute | solution.py:23
  23.3 0.5 %collective-permute-start.7 = (bf16[16,2048]{1,0:T(8,128)(2,1)S(1)}, bf16[16,2048]{1,0:T(8,128)(2,1)S(1)}, u32[]{:S(2)}, u32[]{:S(2)}) collective-permute-start(bf16[16,2048]{1,0:T(8,128)(2,1)S(1)} %get-tuple-element.33.after_ref), channel_id=1, source_target_pairs={{0,4},{4,0},{8,12},{12,8},{1,5},{5,1},{9,13},{13,9},{2,6},{6,2},{1... | collective-permute-start | bytes 196616 | tf_op jit(solution)/shard_map/ppermute | solution.py:23
  23.8 2.2 %shard_map.91 = (bf16[1024,2048]{1,0:T(8,128)(2,1)S(1)}, f32[8,128]{1,0:T(8,128)S(1)}) custom-call(bf16[2048,8192]{1,0:T(8,128)(2,1)} %matrix_ref.5, bf16[16,2048]{1,0:T(8,128)(2,1)S(1)} %get-tuple-element.33.after_ref), custom_call_target="tpu_custom_call" | custom-call | tf_op jit(solution)/shard_map/pallas_call | solution.py:345
  26.0 0.6 %collective-permute-done.8.refs_1_ = bf16[16,2048]{1,0:T(8,128)(2,1)S(1)} collective-permute-done((bf16[16,2048]{1,0:T(8,128)(2,1)S(1)}, bf16[16,2048]{1,0:T(8,128)(2,1)S(1)}, u32[]{:S(2)}, u32[]{:S(2)}) %collective-permute-start.8) | collective-permute-done | bytes 65568 | tf_op jit(solution)/shard_map/ppermute | solution.py:23
  26.6 2.3 %shard_map.93 = (f32[16,2048]{1,0:T(8,128)S(1)}, bf16[1024,2048]{1,0:T(8,128)(2,1)S(1)}) custom-call(bf16[16,2048]{1,0:T(8,128)(2,1)S(1)} %shard_map.92.low_ref, bf16[1024,2048]{1,0:T(8,128)(2,1)S(1)} %get-tuple-element.37.lower_ref, bf16[1024,2048]{1,0:T(8,128)(2,1)S(1)} %get-tuple-element.38.upper_ref, bf16[2048,8192]{1,0:T(8,128)(2,1)} %matrix_ref.5), custom_call_target="tpu_custom_call" | custom-call | tf_op jit(solution)/shard_map/pallas_call | solution.py:394
  28.9 0.0 collective-permute-done.6.refs_0_
  28.9 0.0 collective-permute-done.7.refs_1_
  28.9 2.3 %shard_map.94 = (f32[8,2048]{1,0:T(8,128)S(1)}, f32[8,2048]{1,0:T(8,128)S(1)}) custom-call(bf16[16,2048]{1,0:T(8,128)(2,1)S(1)} %shard_map.90.low_ref, bf16[1024,2048]{1,0:T(8,128)(2,1)S(1)} %get-tuple-element.34.lower_ref, bf16[1024,2048]{1,0:T(8,128)(2,1)S(1)} %get-tuple-element.39.upper_ref, f32[16,2048]{1,0:T(8,128)S(1)} %get-tuple-element.40.sum_ref), custom_call_target="tpu_custom_call" | custom-call | tf_op jit(solution)/shard_map/pallas_call | solution.py:403
  31.2 0.0 collective-permute-start.9
  31.2 1.3 %collective-permute-done.9 = f32[8,2048]{1,0:T(8,128)S(1)} collective-permute-done((f32[8,2048]{1,0:T(8,128)S(1)}, f32[8,2048]{1,0:T(8,128)S(1)}, u32[]{:S(2)}, u32[]{:S(2)}) %collective-permute-start.9) | collective-permute-done | bytes 65568 | tf_op jit(solution)/shard_map/ppermute | solution.py:23
  32.5 0.6 %add_convert_fusion = bf16[8,2048]{1,0:T(8,128)(2,1)} fusion(f32[8,2048]{1,0:T(8,128)S(1)} %get-tuple-element.41, f32[8,2048]{1,0:T(8,128)S(1)} %collective-permute-done.9), kind=kLoop, calls=%fused_computation | loop fusion | flops 32768 | bytes 163840 | tf_op jit(solution)/shard_map/convert_element_type | solution.py:410
  (4 shorter events, 0.1 us)
Async XLA Ops:
  0.0 11.1 %collective-permute-start.3 = (bf16[128,1024]{1,0:T(8,128)(2,1)}, bf16[128,1024]{1,0:T(8,128)(2,1)S(1)}, u32[]{:S(2)}, u32[]{:S(2)}) collective-permute-start(bf16[128,1024]{1,0:T(8,128)(2,1)} %refs_0_.1), channel_id=1, source_target_pairs={{0,4},{4,0},{8,12},{12,8},{1,5},{5,1},{9,13},{13,9},{2,6},{6,2},{1... | collective-permute-start | bytes 786440 | tf_op jit(solution)/shard_map/ppermute | solution.py:23
  3.8 9.3 %collective-permute-start = (bf16[1,128,128]{2,1,0:T(8,128)(2,1)S(1)}, bf16[1,128,128]{2,1,0:T(8,128)(2,1)S(1)}, u32[]{:S(2)}, u32[]{:S(2)}) collective-permute-start(bf16[1,128,128]{2,1,0:T(8,128)(2,1)S(1)} %shard_map.82.refs_0_), channel_id=1, source_target_pairs={{0,12},{4,8},{8,4},{12,0},{1,13},{5,9},{9,5},{13,1},{2,14},{6,10},... | collective-permute-start | bytes 98312 | tf_op jit(solution)/shard_map/ppermute | solution.py:23
  6.4 6.8 %collective-permute-start.1 = (bf16[1,128,128]{2,1,0:T(8,128)(2,1)S(1)}, bf16[1,128,128]{2,1,0:T(8,128)(2,1)S(1)}, u32[]{:S(2)}, u32[]{:S(2)}) collective-permute-start(bf16[1,128,128]{2,1,0:T(8,128)(2,1)S(1)} %shard_map.82.refs_0_), channel_id=1, source_target_pairs={{0,8},{4,12},{8,0},{12,4},{1,9},{5,13},{9,1},{13,5},{2,10},{6,14},... | collective-permute-start | bytes 98312 | tf_op jit(solution)/shard_map/ppermute | solution.py:23
  6.6 6.6 %collective-permute-start.2 = (bf16[1,128,128]{2,1,0:T(8,128)(2,1)S(1)}, bf16[1,128,128]{2,1,0:T(8,128)(2,1)S(1)}, u32[]{:S(2)}, u32[]{:S(2)}) collective-permute-start(bf16[1,128,128]{2,1,0:T(8,128)(2,1)S(1)} %shard_map.82.refs_0_), channel_id=1, source_target_pairs={{0,4},{4,0},{8,12},{12,8},{1,5},{5,1},{9,13},{13,9},{2,6},{6,2},{1... | collective-permute-start | bytes 98312 | tf_op jit(solution)/shard_map/ppermute | solution.py:23
  13.9 1.4 %collective-permute-start.4 = (bf16[32,2048]{1,0:T(8,128)(2,1)S(1)}, bf16[32,2048]{1,0:T(8,128)(2,1)S(1)}, u32[]{:S(2)}, u32[]{:S(2)}) collective-permute-start(bf16[32,2048]{1,0:T(8,128)(2,1)S(1)} %shard_map.86), channel_id=1, source_target_pairs={{0,1},{1,0},{2,3},{3,2},{4,5},{5,4},{6,7},{7,6},{8,9},{9,8},{10,11... | collective-permute-start | bytes 393224 | tf_op jit(solution)/shard_map/ppermute | solution.py:23
  15.4 4.3 %collective-permute-start.5 = (bf16[16,2048]{1,0:T(8,128)(2,1)S(1)}, bf16[16,2048]{1,0:T(8,128)(2,1)S(1)}, u32[]{:S(2)}, u32[]{:S(2)}) collective-permute-start(bf16[16,2048]{1,0:T(8,128)(2,1)S(1)} %get-tuple-element.31.after_ref), channel_id=1, source_target_pairs={{0,2},{1,3},{2,0},{3,1},{4,6},{5,7},{6,4},{7,5},{8,10},{9,11},{10,... | collective-permute-start | bytes 196616 | tf_op jit(solution)/shard_map/ppermute | solution.py:23
  19.7 6.8 %collective-permute-start.8 = (bf16[16,2048]{1,0:T(8,128)(2,1)S(1)}, bf16[16,2048]{1,0:T(8,128)(2,1)S(1)}, u32[]{:S(2)}, u32[]{:S(2)}) collective-permute-start(bf16[16,2048]{1,0:T(8,128)(2,1)S(1)} %get-tuple-element.33.after_ref), channel_id=1, source_target_pairs={{0,8},{4,12},{8,0},{12,4},{1,9},{5,13},{9,1},{13,5},{2,10},{6,14},... | collective-permute-start | bytes 196616 | tf_op jit(solution)/shard_map/ppermute | solution.py:23
  21.5 7.4 %collective-permute-start.6 = (bf16[16,2048]{1,0:T(8,128)(2,1)S(1)}, bf16[16,2048]{1,0:T(8,128)(2,1)S(1)}, u32[]{:S(2)}, u32[]{:S(2)}) collective-permute-start(bf16[16,2048]{1,0:T(8,128)(2,1)S(1)} %get-tuple-element.33.after_ref), channel_id=1, source_target_pairs={{0,12},{4,8},{8,4},{12,0},{1,13},{5,9},{9,5},{13,1},{2,14},{6,10},... | collective-permute-start | bytes 196616 | tf_op jit(solution)/shard_map/ppermute | solution.py:23
  23.3 5.6 %collective-permute-start.7 = (bf16[16,2048]{1,0:T(8,128)(2,1)S(1)}, bf16[16,2048]{1,0:T(8,128)(2,1)S(1)}, u32[]{:S(2)}, u32[]{:S(2)}) collective-permute-start(bf16[16,2048]{1,0:T(8,128)(2,1)S(1)} %get-tuple-element.33.after_ref), channel_id=1, source_target_pairs={{0,4},{4,0},{8,12},{12,8},{1,5},{5,1},{9,13},{13,9},{2,6},{6,2},{1... | collective-permute-start | bytes 196616 | tf_op jit(solution)/shard_map/ppermute | solution.py:23
  31.2 1.3 %collective-permute-start.9 = (f32[8,2048]{1,0:T(8,128)S(1)}, f32[8,2048]{1,0:T(8,128)S(1)}, u32[]{:S(2)}, u32[]{:S(2)}) collective-permute-start(f32[8,2048]{1,0:T(8,128)S(1)} %get-tuple-element.42), channel_id=1, source_target_pairs={{0,1},{1,0},{2,3},{3,2},{4,5},{5,4},{6,7},{7,6},{8,9},{9,8},{10,11... | collective-permute-start | bytes 196616 | tf_op jit(solution)/shard_map/ppermute | solution.py:23

commit v5 on v4

--- a/solution.py
+++ b/solution.py
@@ -67,10 +67,18 @@
     return total
 
 
-def quarter_index(ref, flip):
-    rows = ref.shape[0] // 4
+def run_count(row_count):
+    return 2 if row_count == 4 else 1
+
+
+def quarter_index(ref, flip, runs):
+    rank = lax.axis_index("rows")
     half = (lax.axis_index("ex") & 1) ^ flip
-    return index_row(ref, ((lax.axis_index("rows") & 1) * 2 + half) * rows, rows)
+    rows = ref.shape[0] // 4 // runs
+    if runs == 1:
+        return index_row(ref, ((rank & 1) * 2 + half) * rows, rows)
+    starts = [((rank ^ (2 * run)) * 2 + half) * rows for run in range(runs)]
+    return jnp.concatenate([index_row(ref, start, rows) for start in starts], axis=1)
 
 
 def right_block(values, index, block_id, row_count):
@@ -89,11 +97,27 @@
     return index_row(sign_ref, block_id * rows, rows).astype(bf16)
 
 
-def matrix_chunk(matrix_ref, chunk, shape):
+def chunk_shape(chunk, out_rows, quarter, runs):
+    if runs == 1:
+        return (out_rows // 2, quarter)
+    return (quarter // 2, out_rows) if chunk == 0 else (out_rows, quarter // 2)
+
+
+def matrix_chunk(matrix_ref, chunk, shape, runs):
+    rank = lax.axis_index("rows")
+    core = lax.axis_index("ex") & 1
     rows, depth = shape
-    half = (lax.axis_index("rows") & 1) ^ (chunk // 2)
-    first = pl.multiple_of((half * 2 + (lax.axis_index("ex") & 1)) * depth, depth)
-    return matrix_ref.at[pl.ds(chunk % 2 * rows, rows), pl.ds(first, depth)]
+    if runs == 1:
+        half = (rank & 1) ^ (chunk // 2)
+        first = pl.multiple_of((half * 2 + core) * depth, depth)
+        return matrix_ref.at[pl.ds(chunk % 2 * rows, rows), pl.ds(first, depth)]
+    if chunk == 0:
+        return matrix_ref.at[
+            pl.ds(pl.multiple_of(core * rows, rows), rows),
+            pl.ds(pl.multiple_of(rank * depth, depth), depth),
+        ]
+    block = rank ^ (0, 2, 1, 3)[chunk]
+    return matrix_ref.at[:, pl.ds(pl.multiple_of((block * 2 + core) * depth, depth), depth)]
 
 
 def sign_kernel(hidden_in, sign_in, out_ref, hidden_ref, sign_ref, sems):
@@ -118,7 +142,7 @@
         (col_in, col_ref),
         (row_in, row_ref),
         (len_in, len_ref),
-        (matrix_chunk(matrix_ref, 0, held_ref.shape), held_ref),
+        (matrix_chunk(matrix_ref, 0, held_ref.shape, run_count(row_count)), held_ref),
     )
     copies = [pltpu.make_async_copy(*pair, sems.at[at]) for at, pair in enumerate(pairs)]
     for copy in copies:
@@ -132,17 +156,17 @@
     values = cot_ref[...] * block_signs(sign_ref, rank, width)
     for flip in range(2):
         first = 0
-        for part in right_block(values, quarter_index(col_ref, flip), rank, row_count):
+        for part in right_block(values, quarter_index(col_ref, flip, run_count(row_count)), rank, row_count):
             right_ref[flip, :, first : first + part.shape[1]] = part
             first += part.shape[1]
-    tables(row_ref, len_ref, table_ref, member_ref)
+    tables(row_count, row_ref, len_ref, table_ref, member_ref)
     copies[-1].wait()
 
 
-def tables(row_ref, len_ref, table_ref, member_ref):
+def tables(row_count, row_ref, len_ref, table_ref, member_ref):
     width = table_ref.shape[1]
     for flip in range(2):
-        table_ref[flip] = sign_columns(quarter_index(row_ref, flip) % width, width)
+        table_ref[flip] = sign_columns(quarter_index(row_ref, flip, run_count(row_count)) % width, width)
     examples, tokens = member_ref.shape
     ex_rank = lax.axis_index("ex")
     ex_count = lax.axis_size("ex")
@@ -164,7 +188,7 @@
     near = lax.axis_index("rows") ^ 1
     for flip in range(2):
         first = 0
-        for part in right_block(values, quarter_index(col_ref, flip), near, row_count):
+        for part in right_block(values, quarter_index(col_ref, flip, run_count(row_count)), near, row_count):
             columns = slice(first, first + part.shape[1])
             out_ref[flip, :, columns] = own_ref[flip, :, columns] + part
             first += part.shape[1]
@@ -175,7 +199,7 @@
     row_bits = row_count.bit_length() - 1
     blocks = [ref[block] for ref in hidden_refs for block in range(ref.shape[0])]
     base = table_ref[flip]
-    high = quarter_index(row_ref, flip) // base.shape[0]
+    high = quarter_index(row_ref, flip, run_count(row_count)) // base.shape[0]
     left = None
     for first in range(0, len(masks), 4):
         table = [
@@ -197,11 +221,25 @@
     out_ref[...] = total.astype(out_ref.dtype)
 
 
-def load_kernel(chunk, matrix_ref, after_ref, out_ref, token_ref, sem):
-    copy = pltpu.make_async_copy(matrix_chunk(matrix_ref, chunk, out_ref.shape), out_ref, sem)
-    copy.start()
+def last_half(matrix_ref, half, shape, runs):
+    rows, depth = shape
+    return matrix_chunk(matrix_ref, 3, (2 * rows, depth), runs).at[pl.ds(half * rows, rows), :]
+
+
+def load_kernel(chunk, runs, matrix_ref, after_ref, *refs):
+    *out_refs, token_ref, sems = refs
+    sources = [matrix_chunk(matrix_ref, chunk, out_refs[0].shape, runs)]
+    if chunk == 2:
+        sources.append(last_half(matrix_ref, 0, out_refs[1].shape, runs))
+    copies = [
+        pltpu.make_async_copy(source, ref, sems.at[at])
+        for at, (source, ref) in enumerate(zip(sources, out_refs))
+    ]
+    for copy in copies:
+        copy.start()
     token_ref[...] = jnp.zeros_like(token_ref)
-    copy.wait()
+    for copy in copies:
+        copy.wait()
 
 
 def add_kernel(kept_ref, received_ref, *refs):
@@ -211,40 +249,54 @@
     total_ref[...] = total[total.shape[0] - total_ref.shape[0] :]
 
 
-def low_kernel(scale, count, *refs):
-    total = refs[0][...].astype(f32)
-    for ref in refs[1:count]:
-        total = total + ref[...].astype(f32)
+def low_kernel(scale, turns, *refs):
+    total = None
+    for turn, ref in zip(turns, refs):
+        term = ref[...].astype(f32)
+        if turn:
+            run = term.shape[1] // 2
+            term = jnp.concatenate([term[:, run:], term[:, :run]], axis=1)
+        total = term if total is None else total + term
     refs[-1][...] = (total * scale).astype(bf16)
 
 
-def own_score_kernel(low_ref, lower_ref, upper_ref, matrix_ref, out_ref, held_ref, sem):
-    copy = pltpu.make_async_copy(matrix_chunk(matrix_ref, 3, held_ref.shape), held_ref, sem)
+def times_transposed(low, refs):
+    parts = [
+        lax.dot_general(low, ref[...], contract_last, preferred_element_type=f32) for ref in refs
+    ]
+    return parts[0] if len(parts) == 1 else jnp.concatenate(parts, axis=1)
+
+
+def own_score_kernel(runs, low_ref, lower_ref, upper_ref, matrix_ref, out_ref, held_ref, sem):
+    copy = pltpu.make_async_copy(last_half(matrix_ref, 1, held_ref.shape, runs), held_ref, sem)
     copy.start()
 
     @pl.when(lax.axis_index("rows") >= 0)
     def _():
-        rows = held_ref.shape[0]
         low = low_ref[...]
-        for at, ref in enumerate((lower_ref, upper_ref)):
-            out_ref[:, at * rows : (at + 1) * rows] = lax.dot_general(
-                low, ref[...], contract_last, preferred_element_type=f32
-            )
+        if runs == 1:
+            out_ref[...] = times_transposed(low, (lower_ref, upper_ref))
+        else:
+            run = low.shape[1] // 2
+            straight = jnp.dot(low[:, :run], lower_ref[...], preferred_element_type=f32)
+            out_ref[...] = straight + times_transposed(low[:, run:], (upper_ref,))
 
     copy.wait()
 
 
-def near_score_kernel(low_ref, lower_ref, upper_ref, sum_ref, send_ref, keep_ref):
-    rows = lower_ref.shape[0]
+def near_score_kernel(runs, low_ref, lower_ref, *refs):
+    *upper_refs, sum_ref, send_ref, keep_ref = refs
     low = low_ref[...]
-    own = low.shape[0] // 2
+    if runs == 1:
+        part = times_transposed(low, (lower_ref, *upper_refs))
+    else:
+        run = low.shape[1] // 2
+        part = times_transposed(low[:, :run], (lower_ref,)) + times_transposed(low[:, run:], upper_refs)
+    part = part + sum_ref[...]
+    own = part.shape[0] // 2
     lower = (lax.axis_index("ex") & 1) == 0
-    for at, ref in enumerate((lower_ref, upper_ref)):
-        columns = slice(at * rows, (at + 1) * rows)
-        part = lax.dot_general(low, ref[...], contract_last, preferred_element_type=f32)
-        part = part + sum_ref[:, columns]
-        keep_ref[:, columns] = jnp.where(lower, part[:own], part[own:])
-        send_ref[:, columns] = jnp.where(lower, part[own:], part[:own])
+    keep_ref[...] = jnp.where(lower, part[:own], part[own:])
+    send_ref[...] = jnp.where(lower, part[own:], part[:own])
 
 
 def local(hidden_acts, cotangent, lengths, row_signs, col_signs, feat_row, feat_col, inverse_rows):
@@ -263,7 +315,10 @@
     anywhere = pl.BlockSpec(memory_space=pltpu.HBM)
     out_rows = inverse_rows.shape[0]
 
-    chunk = (out_rows // 2, quarter)
+    runs = run_count(row_count)
+    chunks = [pltpu.VMEM(chunk_shape(at, out_rows, quarter, runs), bf16) for at in range(4)]
+    last_rows, last_depth = chunks[3].shape
+    last_chunk = pltpu.VMEM((last_rows // 2, last_depth), bf16)
     table_shape = (feature_count // 128, 128)
 
     near_cot = swap(cotangent, "rows", 1)
@@ -300,7 +355,7 @@
             pltpu.VMEM((1, cot_width), bf16),
             pltpu.VMEM((2, width, quarter), bf16),
             pltpu.VMEM((example_count, tokens), bf16),
-            pltpu.VMEM(chunk, bf16),
+            chunks[0],
             pltpu.VMEM(table_shape, jnp.int32),
             pltpu.VMEM(table_shape, jnp.int32),
         ),
@@ -342,12 +397,13 @@
         )(*hidden_parts, right, row_index, hidden_table, member)
 
     def load(chunk_id, after):
+        loaded = [chunks[chunk_id]] + [last_chunk] * (chunk_id == 2)
         return pl.pallas_call(
-            functools.partial(load_kernel, chunk_id),
-            out_shape=(pltpu.VMEM(chunk, bf16), pltpu.VMEM((8, 128), f32)),
+            functools.partial(load_kernel, chunk_id, runs),
+            out_shape=(*loaded, pltpu.VMEM((8, 128), f32)),
             in_specs=[anywhere, whole],
-            out_specs=(whole, whole),
-            scratch_shapes=[pltpu.SemaphoreType.DMA],
+            out_specs=(whole,) * (len(loaded) + 1),
+            scratch_shapes=[pltpu.SemaphoreType.DMA((len(loaded),))],
             compiler_params=params,
         )(in_hbm(inverse_rows), after)
 
@@ -364,9 +420,9 @@
             compiler_params=params,
         )(kept, received, *([] if token is None else [token]))
 
-    def features_low(terms, token):
+    def features_low(terms, turns, token):
         return pl.pallas_call(
-            functools.partial(low_kernel, norm_scale, len(terms)),
+            functools.partial(low_kernel, norm_scale, turns[: len(terms)]),
             out_shape=pltpu.VMEM(terms[0].shape, bf16),
             in_specs=[whole] * (len(terms) + (token is not None)),
             out_specs=whole,
@@ -386,14 +442,15 @@
             matrix_1, token = load(1, send)
         received = swap(send, axis, mask)
     send, total = add_up(total, received, received.shape[0], token)
-    matrix_2, token = load(2, send)
+    matrix_2, matrix_3, token = load(2, send)
     others = [swap(send, "rows", mask) for mask in range(1, group)]
-    low = features_low([total] + others[1:2], token)
-    near_low = features_low(others[0::2][::-1], None)
-
-    part, matrix_3 = pl.pallas_call(
-        own_score_kernel,
-        out_shape=(pltpu.VMEM((2 * own_examples, out_rows), f32), pltpu.VMEM(chunk, bf16)),
+    turned = runs > 1
+    low = features_low([total] + others[1:2], [False, turned], token)
+    near_low = features_low(others[0::2][::-1], [turned, False], None)
+
+    part, matrix_4 = pl.pallas_call(
+        functools.partial(own_score_kernel, runs),
+        out_shape=(pltpu.VMEM((2 * own_examples, out_rows), f32), last_chunk),
         in_specs=[whole] * 3 + [anywhere],
         out_specs=(whole, whole),
         scratch_shapes=[pltpu.SemaphoreType.DMA],
@@ -401,12 +458,12 @@
     )(low, matrix_0, matrix_1, in_hbm(inverse_rows))
     own_shape = pltpu.VMEM((own_examples, out_rows), f32)
     send, keep = pl.pallas_call(
-        near_score_kernel,
+        functools.partial(near_score_kernel, runs),
         out_shape=(own_shape, own_shape),
-        in_specs=[whole] * 4,
+        in_specs=[whole] * 5,
         out_specs=(whole, whole),
         compiler_params=params,
-    )(near_low, matrix_2, matrix_3, part)
+    )(near_low, matrix_2, matrix_3, matrix_4, part)
     return (keep + swap(send, "ex", 1)).astype(bf16)
 
 

time: 33.4 us -> 32.9 us (0.985)
  waiting for transfers between devices: 3.57 us -> 2.99 us
    ppermute x10, waiting for transfers between devices: 3.57 us -> 2.99 us  [swap(): lax.ppermute(values, axis, [(rank, rank ^ mask) for rank in range(size)])]
  transfers between devices with their start and end apart: 10 -> 10, of which waited for: 5 -> 4; matrix products, arithmetic and copies ran while one was open for 0% -> 0% of each run, Pallas kernels for 38% -> 39%
where the time goes in v5:
time: 32.9 us; the launch traced here: 32.7 us
  Pallas kernels  15.8 us (48%)
  starting transfers between devices  13.1 us (40%)
  waiting for transfers between devices  2.99 us (9%)
  other arithmetic  0.62 us (2%)
    ppermute x10, starting transfers between devices, swap(): lax.ppermute(values, axis, [(rank, rank ^ mask) for rank in range(size)])  13.1 us
    pallas_call x2, Pallas kernels, load(): pl.pallas_call(functools.partial(load_kernel, chunk_id, runs), out_shape=...  5.1 us
    ppermute x10, waiting for transfers between devices, swap(): lax.ppermute(values, axis, [(rank, rank ^ mask) for rank in range(size)])  2.99 us
    pallas_call x1, Pallas kernels, local(): pl.pallas_call(functools.partial(own_kernel, row_count), out_shape=(right...  2.82 us
    pallas_call x1, Pallas kernels, local(): pl.pallas_call(functools.partial(near_score_kernel, runs), out_shape=(own...  2.27 us
    pallas_call x1, Pallas kernels, local(): pl.pallas_call(functools.partial(own_score_kernel, runs), out_shape=(pltp...  1.76 us
    pallas_call x2, Pallas kernels, features(): pl.pallas_call(kernel, out_shape=pltpu.VMEM((example_count, quarter), bf1...  1.52 us
    pallas_call x1, Pallas kernels, local(): pl.pallas_call(functools.partial(right_kernel, row_count), out_shape=righ...  1.44 us
  transfers between devices with their start and end apart: 10, of which 4 were waited for; matrix products, arithmetic and copies ran while one was open for 0% of the time, Pallas kernels for 39%

profile of v5, /device:TPU:0, one launch (start us, length us, event | category | flops | bytes accessed | tf_op | source)
XLA Modules:
  0.0 32.7 jit_solution(3437533244440597461)
XLA Ops:
  0.0 3.0 %collective-permute-start.3 = (bf16[128,1024]{1,0:T(8,128)(2,1)}, bf16[128,1024]{1,0:T(8,128)(2,1)S(1)}, u32[]{:S(2)}, u32[]{:S(2)}) collective-permute-start(bf16[128,1024]{1,0:T(8,128)(2,1)} %refs_0_.1), channel_id=1, source_target_pairs={{0,4},{4,0},{8,12},{12,8},{1,5},{5,1},{9,13},{13,9},{2,6},{6,2},{1... | collective-permute-start | bytes 786440 | tf_op jit(solution)/shard_map/ppermute | solution.py:23
  3.0 0.8 %shard_map.82.refs_0_ = bf16[1,128,128]{2,1,0:T(8,128)(2,1)S(1)} custom-call(bf16[128,128]{1,0:T(8,128)(2,1)} %hidden_in.1, s32[1,128]{1,0:T(1,128)} %bitcast.8), custom_call_target="tpu_custom_call" | custom-call | tf_op jit(solution)/shard_map/pallas_call | solution.py:325
  3.8 2.5 %collective-permute-start = (bf16[1,128,128]{2,1,0:T(8,128)(2,1)S(1)}, bf16[1,128,128]{2,1,0:T(8,128)(2,1)S(1)}, u32[]{:S(2)}, u32[]{:S(2)}) collective-permute-start(bf16[1,128,128]{2,1,0:T(8,128)(2,1)S(1)} %shard_map.82.refs_0_), channel_id=1, source_target_pairs={{0,12},{4,8},{8,4},{12,0},{1,13},{5,9},{9,5},{13,1},{2,14},{6,10},... | collective-permute-start | bytes 98312 | tf_op jit(solution)/shard_map/ppermute | solution.py:23
  6.4 0.2 collective-permute-start.1
  6.6 1.7 %collective-permute-start.2 = (bf16[1,128,128]{2,1,0:T(8,128)(2,1)S(1)}, bf16[1,128,128]{2,1,0:T(8,128)(2,1)S(1)}, u32[]{:S(2)}, u32[]{:S(2)}) collective-permute-start(bf16[1,128,128]{2,1,0:T(8,128)(2,1)S(1)} %shard_map.82.refs_0_), channel_id=1, source_target_pairs={{0,4},{4,0},{8,12},{12,8},{1,5},{5,1},{9,13},{13,9},{2,6},{6,2},{1... | collective-permute-start | bytes 98312 | tf_op jit(solution)/shard_map/ppermute | solution.py:23
  8.3 2.8 %shard_map.83 = (f32[2,128,2048]{2,1,0:T(8,128)S(1)}, bf16[1,1024]{1,0:T(2,128)(2,1)S(1)}, bf16[2,128,2048]{2,1,0:T(8,128)(2,1)S(1)}, bf16[32,128]{1,0:T(8,128)(...) custom-call(bf16[128,1024]{1,0:T(8,128)(2,1)} %refs_0_.1, ...), custom_call_target="tpu_custom_call" | custom-call | tf_op jit(solution)/shard_map/pallas_call | solution.py:351
  11.1 0.0 collective-permute-done.3.cot_ref
  11.1 1.4 %shard_map.84.refs_4_ = f32[2,128,2048]{2,1,0:T(8,128)S(1)} custom-call(bf16[128,1024]{1,0:T(8,128)(2,1)S(1)} %collective-permute-done.3.cot_ref, bf16[1,1024]{1,0:T(2,128)(2,1)S(1)} %get-tuple-element.25.sign_ref, s32[64,128]{1,0:T(8,128)S(1)} %get-tuple-element.26.col_ref, f32[2,128,2048]{2,1,0:T(8,128)S(1)} %get-tuple-element.27.own_ref), custom_call_target="tpu_custom_call" | custom-call | tf_op jit(solution)/shard_map/pallas_call | solution.py:379
  12.6 0.6 %collective-permute-done.refs_1_ = bf16[1,128,128]{2,1,0:T(8,128)(2,1)S(1)} collective-permute-done((bf16[1,128,128]{2,1,0:T(8,128)(2,1)S(1)}, bf16[1,128,128]{2,1,0:T(8,128)(2,1)S(1)}, u32[]{:S(2)}, u32[]{:S(2)}) %collective-permute-start) | collective-permute-done | bytes 32800 | tf_op jit(solution)/shard_map/ppermute | solution.py:23
  13.1 0.0 collective-permute-done.1.refs_2_
  13.1 0.0 collective-permute-done.2.refs_3_
  13.1 0.8 %shard_map.86 = bf16[32,2048]{1,0:T(8,128)(2,1)S(1)} custom-call(bf16[1,128,128]{2,1,0:T(8,128)(2,1)S(1)} %shard_map.82.refs_0_, bf16[1,128,128]{2,1,0:T(8,128)(2,1)S(1)} %collective-permute-done.refs_1_, bf16[1,128,128]{2,1,0:T(8,128)(2,1)S(1)} %collective-permute-done.1.refs_2_, bf16[1,128,128]{2,1,0:T(8,128)(2,1)S(1)} %collective-permute-done.2.refs_3_, ...), custom_call_target="tpu_custom_call" | custom-call | tf_op jit(solution)/shard_map/pallas_call | solution.py:391
  13.9 0.1 collective-permute-start.4
  14.0 0.8 %shard_map.85.kept_ref = f32[32,2048]{1,0:T(8,128)S(1)} custom-call(bf16[1,128,128]{2,1,0:T(8,128)(2,1)S(1)} %shard_map.82.refs_0_, bf16[1,128,128]{2,1,0:T(8,128)(2,1)S(1)} %collective-permute-done.refs_1_, bf16[1,128,128]{2,1,0:T(8,128)(2,1)S(1)} %collective-permute-done.1.refs_2_, bf16[1,128,128]{2,1,0:T(8,128)(2,1)S(1)} %collective-permute-done.2.refs_3_, ...), custom_call_target="tpu_custom_call" | custom-call | tf_op jit(solution)/shard_map/pallas_call | solution.py:391
  14.7 0.6 %collective-permute-done.4.received_ref = bf16[32,2048]{1,0:T(8,128)(2,1)S(1)} collective-permute-done((bf16[32,2048]{1,0:T(8,128)(2,1)S(1)}, bf16[32,2048]{1,0:T(8,128)(2,1)S(1)}, u32[]{:S(2)}, u32[]{:S(2)}) %collective-permute-start.4) | collective-permute-done | bytes 131104 | tf_op jit(solution)/shard_map/ppermute | solution.py:23
  15.3 1.6 %collective-permute-start.5 = (bf16[16,2048]{1,0:T(8,128)(2,1)S(1)}, bf16[16,2048]{1,0:T(8,128)(2,1)S(1)}, u32[]{:S(2)}, u32[]{:S(2)}) collective-permute-start(bf16[16,2048]{1,0:T(8,128)(2,1)S(1)} %get-tuple-element.32.after_ref), channel_id=1, source_target_pairs={{0,2},{1,3},{2,0},{3,1},{4,6},{5,7},{6,4},{7,5},{8,10},{9,11},{10,... | collective-permute-start | bytes 196616 | tf_op jit(solution)/shard_map/ppermute | solution.py:23
  16.9 2.2 %shard_map.88 = (bf16[2048,1024]{1,0:T(8,128)(2,1)S(1)}, f32[8,128]{1,0:T(8,128)S(1)}) custom-call(bf16[2048,8192]{1,0:T(8,128)(2,1)} %matrix_ref.5, bf16[16,2048]{1,0:T(8,128)(2,1)S(1)} %get-tuple-element.32.after_ref), custom_call_target="tpu_custom_call" | custom-call | tf_op jit(solution)/shard_map/pallas_call | solution.py:401
  19.1 0.6 %collective-permute-done.5.received_ref = bf16[16,2048]{1,0:T(8,128)(2,1)S(1)} collective-permute-done((bf16[16,2048]{1,0:T(8,128)(2,1)S(1)}, bf16[16,2048]{1,0:T(8,128)(2,1)S(1)}, u32[]{:S(2)}, u32[]{:S(2)}) %collective-permute-start.5) | collective-permute-done | bytes 65568 | tf_op jit(solution)/shard_map/ppermute | solution.py:23
  19.7 1.7 %collective-permute-start.8 = (bf16[16,2048]{1,0:T(8,128)(2,1)S(1)}, bf16[16,2048]{1,0:T(8,128)(2,1)S(1)}, u32[]{:S(2)}, u32[]{:S(2)}) collective-permute-start(bf16[16,2048]{1,0:T(8,128)(2,1)S(1)} %get-tuple-element.34.after_ref), channel_id=1, source_target_pairs={{0,8},{4,12},{8,0},{12,4},{1,9},{5,13},{9,1},{13,5},{2,10},{6,14},... | collective-permute-start | bytes 196616 | tf_op jit(solution)/shard_map/ppermute | solution.py:23
  21.5 1.8 %collective-permute-start.6 = (bf16[16,2048]{1,0:T(8,128)(2,1)S(1)}, bf16[16,2048]{1,0:T(8,128)(2,1)S(1)}, u32[]{:S(2)}, u32[]{:S(2)}) collective-permute-start(bf16[16,2048]{1,0:T(8,128)(2,1)S(1)} %get-tuple-element.34.after_ref), channel_id=1, source_target_pairs={{0,12},{4,8},{8,4},{12,0},{1,13},{5,9},{9,5},{13,1},{2,14},{6,10},... | collective-permute-start | bytes 196616 | tf_op jit(solution)/shard_map/ppermute | solution.py:23
  23.2 0.5 %collective-permute-start.7 = (bf16[16,2048]{1,0:T(8,128)(2,1)S(1)}, bf16[16,2048]{1,0:T(8,128)(2,1)S(1)}, u32[]{:S(2)}, u32[]{:S(2)}) collective-permute-start(bf16[16,2048]{1,0:T(8,128)(2,1)S(1)} %get-tuple-element.34.after_ref), channel_id=1, source_target_pairs={{0,4},{4,0},{8,12},{12,8},{1,5},{5,1},{9,13},{13,9},{2,6},{6,2},{1... | collective-permute-start | bytes 196616 | tf_op jit(solution)/shard_map/ppermute | solution.py:23
  23.7 2.9 %shard_map.91 = (bf16[2048,1024]{1,0:T(8,128)(2,1)S(1)}, bf16[1024,1024]{1,0:T(8,128)(2,1)S(1)}, f32[8,128]{1,0:T(8,128)S(1)}) custom-call(bf16[2048,8192]{1,0:T(8,128)(2,1)} %matrix_ref.5, bf16[16,2048]{1,0:T(8,128)(2,1)S(1)} %get-tuple-element.34.after_ref), custom_call_target="tpu_custom_call" | custom-call | tf_op jit(solution)/shard_map/pallas_call | solution.py:401
  26.6 0.0 collective-permute-done.8.refs_1_
  26.7 1.8 %shard_map.93 = (f32[16,2048]{1,0:T(8,128)S(1)}, bf16[1024,1024]{1,0:T(8,128)(2,1)S(1)}) custom-call(bf16[16,2048]{1,0:T(8,128)(2,1)S(1)} %shard_map.92.low_ref, bf16[1024,2048]{1,0:T(8,128)(2,1)S(1)} %get-tuple-element.39.lower_ref, bf16[2048,1024]{1,0:T(8,128)(2,1)S(1)} %get-tuple-element.40.upper_ref, bf16[2048,8192]{1,0:T(8,128)(2,1)} %matrix_ref.5), custom_call_target="tpu_custom_call" | custom-call | tf_op jit(solution)/shard_map/pallas_call | solution.py:451
  28.5 0.0 collective-permute-done.6.refs_0_
  28.5 0.0 collective-permute-done.7.refs_1_
  28.5 2.3 %shard_map.94 = (f32[8,2048]{1,0:T(8,128)S(1)}, f32[8,2048]{1,0:T(8,128)S(1)}) custom-call(bf16[16,2048]{1,0:T(8,128)(2,1)S(1)} %shard_map.90.low_ref, bf16[2048,1024]{1,0:T(8,128)(2,1)S(1)} %get-tuple-element.35.lower_ref, bf16[1024,1024]{1,0:T(8,128)(2,1)S(1)} %get-tuple-element.36.refs_0_, bf16[1024,1024]{1,0:T(8,128)(2,1)S(1)} %get-tuple-element.41.refs_1_, ...), custom_call_target="tpu_custom_call" | custom-call | tf_op jit(solution)/shard_map/pallas_call | solution.py:460
  30.8 0.0 collective-permute-start.9
  30.8 1.3 %collective-permute-done.9 = f32[8,2048]{1,0:T(8,128)S(1)} collective-permute-done((f32[8,2048]{1,0:T(8,128)S(1)}, f32[8,2048]{1,0:T(8,128)S(1)}, u32[]{:S(2)}, u32[]{:S(2)}) %collective-permute-start.9) | collective-permute-done | bytes 65568 | tf_op jit(solution)/shard_map/ppermute | solution.py:23
  32.0 0.6 %add_convert_fusion = bf16[8,2048]{1,0:T(8,128)(2,1)} fusion(f32[8,2048]{1,0:T(8,128)S(1)} %get-tuple-element.43, f32[8,2048]{1,0:T(8,128)S(1)} %collective-permute-done.9), kind=kLoop, calls=%fused_computation | loop fusion | flops 32768 | bytes 163840 | tf_op jit(solution)/shard_map/convert_element_type | solution.py:467
  (4 shorter events, 0.1 us)
Async XLA Ops:
  0.0 11.1 %collective-permute-start.3 = (bf16[128,1024]{1,0:T(8,128)(2,1)}, bf16[128,1024]{1,0:T(8,128)(2,1)S(1)}, u32[]{:S(2)}, u32[]{:S(2)}) collective-permute-start(bf16[128,1024]{1,0:T(8,128)(2,1)} %refs_0_.1), channel_id=1, source_target_pairs={{0,4},{4,0},{8,12},{12,8},{1,5},{5,1},{9,13},{13,9},{2,6},{6,2},{1... | collective-permute-start | bytes 786440 | tf_op jit(solution)/shard_map/ppermute | solution.py:23
  3.8 9.3 %collective-permute-start = (bf16[1,128,128]{2,1,0:T(8,128)(2,1)S(1)}, bf16[1,128,128]{2,1,0:T(8,128)(2,1)S(1)}, u32[]{:S(2)}, u32[]{:S(2)}) collective-permute-start(bf16[1,128,128]{2,1,0:T(8,128)(2,1)S(1)} %shard_map.82.refs_0_), channel_id=1, source_target_pairs={{0,12},{4,8},{8,4},{12,0},{1,13},{5,9},{9,5},{13,1},{2,14},{6,10},... | collective-permute-start | bytes 98312 | tf_op jit(solution)/shard_map/ppermute | solution.py:23
  6.4 6.8 %collective-permute-start.1 = (bf16[1,128,128]{2,1,0:T(8,128)(2,1)S(1)}, bf16[1,128,128]{2,1,0:T(8,128)(2,1)S(1)}, u32[]{:S(2)}, u32[]{:S(2)}) collective-permute-start(bf16[1,128,128]{2,1,0:T(8,128)(2,1)S(1)} %shard_map.82.refs_0_), channel_id=1, source_target_pairs={{0,8},{4,12},{8,0},{12,4},{1,9},{5,13},{9,1},{13,5},{2,10},{6,14},... | collective-permute-start | bytes 98312 | tf_op jit(solution)/shard_map/ppermute | solution.py:23
  6.6 6.6 %collective-permute-start.2 = (bf16[1,128,128]{2,1,0:T(8,128)(2,1)S(1)}, bf16[1,128,128]{2,1,0:T(8,128)(2,1)S(1)}, u32[]{:S(2)}, u32[]{:S(2)}) collective-permute-start(bf16[1,128,128]{2,1,0:T(8,128)(2,1)S(1)} %shard_map.82.refs_0_), channel_id=1, source_target_pairs={{0,4},{4,0},{8,12},{12,8},{1,5},{5,1},{9,13},{13,9},{2,6},{6,2},{1... | collective-permute-start | bytes 98312 | tf_op jit(solution)/shard_map/ppermute | solution.py:23
  13.9 1.4 %collective-permute-start.4 = (bf16[32,2048]{1,0:T(8,128)(2,1)S(1)}, bf16[32,2048]{1,0:T(8,128)(2,1)S(1)}, u32[]{:S(2)}, u32[]{:S(2)}) collective-permute-start(bf16[32,2048]{1,0:T(8,128)(2,1)S(1)} %shard_map.86), channel_id=1, source_target_pairs={{0,1},{1,0},{2,3},{3,2},{4,5},{5,4},{6,7},{7,6},{8,9},{9,8},{10,11... | collective-permute-start | bytes 393224 | tf_op jit(solution)/shard_map/ppermute | solution.py:23
  15.3 4.3 %collective-permute-start.5 = (bf16[16,2048]{1,0:T(8,128)(2,1)S(1)}, bf16[16,2048]{1,0:T(8,128)(2,1)S(1)}, u32[]{:S(2)}, u32[]{:S(2)}) collective-permute-start(bf16[16,2048]{1,0:T(8,128)(2,1)S(1)} %get-tuple-element.32.after_ref), channel_id=1, source_target_pairs={{0,2},{1,3},{2,0},{3,1},{4,6},{5,7},{6,4},{7,5},{8,10},{9,11},{10,... | collective-permute-start | bytes 196616 | tf_op jit(solution)/shard_map/ppermute | solution.py:23
  19.7 6.9 %collective-permute-start.8 = (bf16[16,2048]{1,0:T(8,128)(2,1)S(1)}, bf16[16,2048]{1,0:T(8,128)(2,1)S(1)}, u32[]{:S(2)}, u32[]{:S(2)}) collective-permute-start(bf16[16,2048]{1,0:T(8,128)(2,1)S(1)} %get-tuple-element.34.after_ref), channel_id=1, source_target_pairs={{0,8},{4,12},{8,0},{12,4},{1,9},{5,13},{9,1},{13,5},{2,10},{6,14},... | collective-permute-start | bytes 196616 | tf_op jit(solution)/shard_map/ppermute | solution.py:23
  21.5 7.0 %collective-permute-start.6 = (bf16[16,2048]{1,0:T(8,128)(2,1)S(1)}, bf16[16,2048]{1,0:T(8,128)(2,1)S(1)}, u32[]{:S(2)}, u32[]{:S(2)}) collective-permute-start(bf16[16,2048]{1,0:T(8,128)(2,1)S(1)} %get-tuple-element.34.after_ref), channel_id=1, source_target_pairs={{0,12},{4,8},{8,4},{12,0},{1,13},{5,9},{9,5},{13,1},{2,14},{6,10},... | collective-permute-start | bytes 196616 | tf_op jit(solution)/shard_map/ppermute | solution.py:23
  23.2 5.2 %collective-permute-start.7 = (bf16[16,2048]{1,0:T(8,128)(2,1)S(1)}, bf16[16,2048]{1,0:T(8,128)(2,1)S(1)}, u32[]{:S(2)}, u32[]{:S(2)}) collective-permute-start(bf16[16,2048]{1,0:T(8,128)(2,1)S(1)} %get-tuple-element.34.after_ref), channel_id=1, source_target_pairs={{0,4},{4,0},{8,12},{12,8},{1,5},{5,1},{9,13},{13,9},{2,6},{6,2},{1... | collective-permute-start | bytes 196616 | tf_op jit(solution)/shard_map/ppermute | solution.py:23
  30.8 1.3 %collective-permute-start.9 = (f32[8,2048]{1,0:T(8,128)S(1)}, f32[8,2048]{1,0:T(8,128)S(1)}, u32[]{:S(2)}, u32[]{:S(2)}) collective-permute-start(f32[8,2048]{1,0:T(8,128)S(1)} %get-tuple-element.44), channel_id=1, source_target_pairs={{0,1},{1,0},{2,3},{3,2},{4,5},{5,4},{6,7},{7,6},{8,9},{9,8},{10,11... | collective-permute-start | bytes 196616 | tf_op jit(solution)/shard_map/ppermute | solution.py:23

commit v6 on v5

--- a/solution.py
+++ b/solution.py
@@ -134,20 +134,22 @@
 
 def own_kernel(row_count, *refs):
     (cot_in, sign_in, col_in, row_in, len_in, matrix_ref), refs = refs[:6], refs[6:]
-    right_ref, near_sign_ref, table_ref, member_ref, held_ref, col_ref, row_ref = refs[:7]
-    cot_ref, sign_ref, len_ref, sems = refs[7:]
+    right_ref, near_sign_ref, table_ref, member_ref, held_ref, last_ref, col_ref, row_ref = refs[:8]
+    cot_ref, sign_ref, len_ref, sems = refs[8:]
+    runs = run_count(row_count)
     pairs = (
         (cot_in, cot_ref),
         (sign_in, sign_ref),
         (col_in, col_ref),
         (row_in, row_ref),
         (len_in, len_ref),
-        (matrix_chunk(matrix_ref, 0, held_ref.shape, run_count(row_count)), held_ref),
+        (matrix_chunk(matrix_ref, 2, held_ref.shape, runs), held_ref),
+        (last_half(matrix_ref, 1, last_ref.shape, runs), last_ref),
     )
     copies = [pltpu.make_async_copy(*pair, sems.at[at]) for at, pair in enumerate(pairs)]
     for copy in copies:
         copy.start()
-    for copy in copies[:-1]:
+    for copy in copies[:-2]:
         copy.wait()
     rank = lax.axis_index("rows")
     width = cot_ref.shape[1]
@@ -160,7 +162,8 @@
             right_ref[flip, :, first : first + part.shape[1]] = part
             first += part.shape[1]
     tables(row_count, row_ref, len_ref, table_ref, member_ref)
-    copies[-1].wait()
+    for copy in copies[-2:]:
+        copy.wait()
 
 
 def tables(row_count, row_ref, len_ref, table_ref, member_ref):
@@ -183,15 +186,23 @@
     member_ref[...] = inside.astype(f32).astype(bf16)
 
 
-def right_kernel(row_count, cot_ref, sign_ref, col_ref, own_ref, out_ref):
-    values = cot_ref[...] * sign_ref[...]
-    near = lax.axis_index("rows") ^ 1
-    for flip in range(2):
-        first = 0
-        for part in right_block(values, quarter_index(col_ref, flip, run_count(row_count)), near, row_count):
-            columns = slice(first, first + part.shape[1])
-            out_ref[flip, :, columns] = own_ref[flip, :, columns] + part
-            first += part.shape[1]
+def right_kernel(row_count, cot_ref, sign_ref, col_ref, own_ref, matrix_ref, out_ref, last_ref, sem):
+    runs = run_count(row_count)
+    copy = pltpu.make_async_copy(last_half(matrix_ref, 0, last_ref.shape, runs), last_ref, sem)
+    copy.start()
+    rank = lax.axis_index("rows")
+
+    @pl.when(rank >= 0)
+    def _():
+        values = cot_ref[...] * sign_ref[...]
+        for flip in range(2):
+            first = 0
+            for part in right_block(values, quarter_index(col_ref, flip, runs), rank ^ 1, row_count):
+                columns = slice(first, first + part.shape[1])
+                out_ref[flip, :, columns] = own_ref[flip, :, columns] + part
+                first += part.shape[1]
+
+    copy.wait()
 
 
 def feature_kernel(flip, row_count, masks, hidden_refs, right_ref, row_ref, table_ref, member_ref, out_ref):
@@ -226,20 +237,29 @@
     return matrix_chunk(matrix_ref, 3, (2 * rows, depth), runs).at[pl.ds(half * rows, rows), :]
 
 
-def load_kernel(chunk, runs, matrix_ref, after_ref, *refs):
-    *out_refs, token_ref, sems = refs
-    sources = [matrix_chunk(matrix_ref, chunk, out_refs[0].shape, runs)]
-    if chunk == 2:
-        sources.append(last_half(matrix_ref, 0, out_refs[1].shape, runs))
-    copies = [
-        pltpu.make_async_copy(source, ref, sems.at[at])
-        for at, (source, ref) in enumerate(zip(sources, out_refs))
-    ]
-    for copy in copies:
-        copy.start()
+def turn_kernel(chunk, runs, given, matrix_ref, after_ref, *refs):
+    given_refs, (out_ref, *turned_refs, token_ref, sem) = refs[:given], refs[given:]
+    copy = pltpu.make_async_copy(matrix_chunk(matrix_ref, chunk, out_ref.shape, runs), out_ref, sem)
+    copy.start()
     token_ref[...] = jnp.zeros_like(token_ref)
-    for copy in copies:
-        copy.wait()
+
+    @pl.when(lax.axis_index("rows") >= 0)
+    def _():
+        for given_ref, turned_ref in zip(given_refs, turned_refs):
+            depth = turned_ref.shape[0]
+            block = math.gcd(depth, 256)
+            shape = (block, block)
+            same = lax.broadcasted_iota(jnp.int32, shape, 0) == lax.broadcasted_iota(jnp.int32, shape, 1)
+            identity = same.astype(f32).astype(bf16)
+            for first in range(0, depth, block):
+                turned_ref[first : first + block, :] = lax.dot_general(
+                    identity,
+                    given_ref[:, first : first + block],
+                    contract_last,
+                    preferred_element_type=f32,
+                ).astype(bf16)
+
+    copy.wait()
 
 
 def add_kernel(kept_ref, received_ref, *refs):
@@ -267,31 +287,27 @@
     return parts[0] if len(parts) == 1 else jnp.concatenate(parts, axis=1)
 
 
-def own_score_kernel(runs, low_ref, lower_ref, upper_ref, matrix_ref, out_ref, held_ref, sem):
-    copy = pltpu.make_async_copy(last_half(matrix_ref, 1, held_ref.shape, runs), held_ref, sem)
-    copy.start()
-
-    @pl.when(lax.axis_index("rows") >= 0)
-    def _():
-        low = low_ref[...]
-        if runs == 1:
-            out_ref[...] = times_transposed(low, (lower_ref, upper_ref))
-        else:
-            run = low.shape[1] // 2
-            straight = jnp.dot(low[:, :run], lower_ref[...], preferred_element_type=f32)
-            out_ref[...] = straight + times_transposed(low[:, run:], (upper_ref,))
-
-    copy.wait()
-
-
-def near_score_kernel(runs, low_ref, lower_ref, *refs):
-    *upper_refs, sum_ref, send_ref, keep_ref = refs
+def own_score_kernel(runs, low_ref, lower_ref, upper_ref, out_ref):
     low = low_ref[...]
     if runs == 1:
-        part = times_transposed(low, (lower_ref, *upper_refs))
+        out_ref[...] = times_transposed(low, (lower_ref, upper_ref))
     else:
         run = low.shape[1] // 2
-        part = times_transposed(low[:, :run], (lower_ref,)) + times_transposed(low[:, run:], upper_refs)
+        part = jnp.dot(low[:, :run], lower_ref[...], preferred_element_type=f32)
+        out_ref[...] = part + jnp.dot(low[:, run:], upper_ref[...], preferred_element_type=f32)
+
+
+def near_score_kernel(runs, low_ref, lower_ref, upper_ref, last_ref, sum_ref, send_ref, keep_ref):
+    low = low_ref[...]
+    if runs == 1:
+        part = times_transposed(low, (lower_ref, upper_ref, last_ref))
+    else:
+        run = low.shape[1] // 2
+        part = jnp.dot(low[:, :run], lower_ref[...], preferred_element_type=f32)
+        halves = [
+            jnp.dot(low[:, run:], ref[...], preferred_element_type=f32) for ref in (upper_ref, last_ref)
+        ]
+        part = part + jnp.concatenate(halves, axis=1)
     part = part + sum_ref[...]
     own = part.shape[0] // 2
     lower = (lax.axis_index("ex") & 1) == 0
@@ -348,24 +364,25 @@
     cot_width = cotangent.shape[1]
     lanes = min(128, cot_width)
     right_shape = pltpu.VMEM((2, tokens, quarter), f32)
-    right, near_signs, hidden_table, member, matrix_0, col_index, row_index = pl.pallas_call(
+    right, near_signs, hidden_table, member, matrix_2, matrix_4, col_index, row_index = pl.pallas_call(
         functools.partial(own_kernel, row_count),
         out_shape=(
             right_shape,
             pltpu.VMEM((1, cot_width), bf16),
             pltpu.VMEM((2, width, quarter), bf16),
             pltpu.VMEM((example_count, tokens), bf16),
-            chunks[0],
+            chunks[2],
+            last_chunk,
             pltpu.VMEM(table_shape, jnp.int32),
             pltpu.VMEM(table_shape, jnp.int32),
         ),
         in_specs=[anywhere] * 6,
-        out_specs=(whole,) * 7,
+        out_specs=(whole,) * 8,
         scratch_shapes=[
             pltpu.VMEM(cotangent.shape, bf16),
             pltpu.VMEM((model_width // lanes, lanes), jnp.int32),
             pltpu.VMEM((1, example_count), jnp.int32),
-            pltpu.SemaphoreType.DMA((6,)),
+            pltpu.SemaphoreType.DMA((7,)),
         ],
         compiler_params=params,
     )(
@@ -376,13 +393,14 @@
         in_hbm(lengths.reshape(1, -1)),
         in_hbm(inverse_rows),
     )
-    right = pl.pallas_call(
+    right, matrix_3 = pl.pallas_call(
         functools.partial(right_kernel, row_count),
-        out_shape=right_shape,
-        in_specs=[whole] * 4,
-        out_specs=whole,
+        out_shape=(right_shape, last_chunk),
+        in_specs=[whole] * 4 + [anywhere],
+        out_specs=(whole, whole),
+        scratch_shapes=[pltpu.SemaphoreType.DMA],
         compiler_params=params,
-    )(near_cot, near_signs, col_index, right)
+    )(near_cot, near_signs, col_index, right, in_hbm(inverse_rows))
 
     def features(flip):
         def kernel(*refs):
@@ -396,16 +414,19 @@
             compiler_params=params,
         )(*hidden_parts, right, row_index, hidden_table, member)
 
-    def load(chunk_id, after):
-        loaded = [chunks[chunk_id]] + [last_chunk] * (chunk_id == 2)
-        return pl.pallas_call(
-            functools.partial(load_kernel, chunk_id, runs),
-            out_shape=(*loaded, pltpu.VMEM((8, 128), f32)),
-            in_specs=[anywhere, whole],
-            out_specs=(whole,) * (len(loaded) + 1),
-            scratch_shapes=[pltpu.SemaphoreType.DMA((len(loaded),))],
+    token_shape = pltpu.VMEM((8, 128), f32)
+
+    def load_and_turn(chunk, after, given):
+        turned = [pltpu.VMEM(values.shape[::-1], bf16) for values in given] if runs > 1 else []
+        loaded, *outs, token = pl.pallas_call(
+            functools.partial(turn_kernel, chunk, runs, len(given)),
+            out_shape=(chunks[chunk], *turned, token_shape),
+            in_specs=[anywhere] + [whole] * (1 + len(given)),
+            out_specs=(whole,) * (len(turned) + 2),
+            scratch_shapes=[pltpu.SemaphoreType.DMA],
             compiler_params=params,
-        )(in_hbm(inverse_rows), after)
+        )(in_hbm(inverse_rows), after, *given)
+        return loaded, outs if turned else given, token
 
     def add_up(kept, received, send_count, token):
         count = received.shape[0]
@@ -439,23 +460,22 @@
         send, total = add_up(total, received, count // 2 if axis == "ex" else count, token)
         token = None
         if matrix_1 is None:
-            matrix_1, token = load(1, send)
+            matrix_1, (matrix_2, matrix_4), token = load_and_turn(1, send, [matrix_2, matrix_4])
         received = swap(send, axis, mask)
     send, total = add_up(total, received, received.shape[0], token)
-    matrix_2, matrix_3, token = load(2, send)
+    matrix_0, (matrix_1, matrix_3), token = load_and_turn(0, send, [matrix_1, matrix_3])
     others = [swap(send, "rows", mask) for mask in range(1, group)]
     turned = runs > 1
     low = features_low([total] + others[1:2], [False, turned], token)
     near_low = features_low(others[0::2][::-1], [turned, False], None)
 
-    part, matrix_4 = pl.pallas_call(
+    part = pl.pallas_call(
         functools.partial(own_score_kernel, runs),
-        out_shape=(pltpu.VMEM((2 * own_examples, out_rows), f32), last_chunk),
-        in_specs=[whole] * 3 + [anywhere],
-        out_specs=(whole, whole),
-        scratch_shapes=[pltpu.SemaphoreType.DMA],
+        out_shape=pltpu.VMEM((2 * own_examples, out_rows), f32),
+        in_specs=[whole] * 3,
+        out_specs=whole,
         compiler_params=params,
-    )(low, matrix_0, matrix_1, in_hbm(inverse_rows))
+    )(low, matrix_0, matrix_1)
     own_shape = pltpu.VMEM((own_examples, out_rows), f32)
     send, keep = pl.pallas_call(
         functools.partial(near_score_kernel, runs),

time: 32.9 us -> 31.8 us (0.967)
  Pallas kernels: 15.8 us -> 13.9 us
  waiting for transfers between devices: 2.99 us -> 3.56 us
    pallas_call x4, Pallas kernels: 8.3 us -> 7.2 us  [the longest x2 4.4 us: load_and_turn(): pl.pallas_call(functools.partial(turn_kernel, chunk, runs, len(given)), o...]
    pallas_call x1, Pallas kernels: 2.27 us -> 1.2 us  [local(): pl.pallas_call(functools.partial(near_score_kernel, runs), out_shape=(own...]
    ppermute x10, waiting for transfers between devices: 2.99 us -> 3.56 us  [swap(): lax.ppermute(values, axis, [(rank, rank ^ mask) for rank in range(size)])]
  transfers between devices with their start and end apart: 10 -> 10, of which waited for: 4 -> 6; matrix products, arithmetic and copies ran while one was open for 0% -> 0% of each run, Pallas kernels for 39% -> 38%
where the time goes in v6:
time: 31.8 us; the launch traced here: 31.5 us
  Pallas kernels  13.9 us (44%)
  starting transfers between devices  13.3 us (42%)
  waiting for transfers between devices  3.56 us (11%)
  other arithmetic  0.62 us (2%)
    ppermute x10, starting transfers between devices, swap(): lax.ppermute(values, axis, [(rank, rank ^ mask) for rank in range(size)])  13.3 us
    pallas_call x2, Pallas kernels, load_and_turn(): pl.pallas_call(functools.partial(turn_kernel, chunk, runs, len(given)), o...  4.4 us
    ppermute x10, waiting for transfers between devices, swap(): lax.ppermute(values, axis, [(rank, rank ^ mask) for rank in range(size)])  3.56 us
    pallas_call x1, Pallas kernels, local(): pl.pallas_call(functools.partial(own_kernel, row_count), out_shape=(right...  3.1 us
    pallas_call x1, Pallas kernels, local(): pl.pallas_call(functools.partial(right_kernel, row_count), out_shape=(rig...  1.61 us
    pallas_call x2, Pallas kernels, features(): pl.pallas_call(kernel, out_shape=pltpu.VMEM((example_count, quarter), bf1...  1.52 us
    pallas_call x1, Pallas kernels, local(): pl.pallas_call(functools.partial(near_score_kernel, runs), out_shape=(own...  1.2 us
    pallas_call x1, Pallas kernels, local(): pl.pallas_call(functools.partial(own_score_kernel, runs), out_shape=pltpu...  1.19 us
  transfers between devices with their start and end apart: 10, of which 6 were waited for; matrix products, arithmetic and copies ran while one was open for 0% of the time, Pallas kernels for 38%

profile of v6, /device:TPU:0, one launch (start us, length us, event | category | flops | bytes accessed | tf_op | source)
XLA Modules:
  0.0 31.5 jit_solution(14327381437787336040)
XLA Ops:
  0.0 3.0 %collective-permute-start.3 = (bf16[128,1024]{1,0:T(8,128)(2,1)}, bf16[128,1024]{1,0:T(8,128)(2,1)S(1)}, u32[]{:S(2)}, u32[]{:S(2)}) collective-permute-start(bf16[128,1024]{1,0:T(8,128)(2,1)} %refs_0_.1), channel_id=1, source_target_pairs={{0,4},{4,0},{8,12},{12,8},{1,5},{5,1},{9,13},{13,9},{2,6},{6,2},{1... | collective-permute-start | bytes 786440 | tf_op jit(solution)/shard_map/ppermute | solution.py:23
  3.0 0.8 %shard_map.82.refs_0_ = bf16[1,128,128]{2,1,0:T(8,128)(2,1)S(1)} custom-call(bf16[128,128]{1,0:T(8,128)(2,1)} %hidden_in.1, s32[1,128]{1,0:T(1,128)} %bitcast.8), custom_call_target="tpu_custom_call" | custom-call | tf_op jit(solution)/shard_map/pallas_call | solution.py:341
  3.8 2.5 %collective-permute-start = (bf16[1,128,128]{2,1,0:T(8,128)(2,1)S(1)}, bf16[1,128,128]{2,1,0:T(8,128)(2,1)S(1)}, u32[]{:S(2)}, u32[]{:S(2)}) collective-permute-start(bf16[1,128,128]{2,1,0:T(8,128)(2,1)S(1)} %shard_map.82.refs_0_), channel_id=1, source_target_pairs={{0,12},{4,8},{8,4},{12,0},{1,13},{5,9},{9,5},{13,1},{2,14},{6,10},... | collective-permute-start | bytes 98312 | tf_op jit(solution)/shard_map/ppermute | solution.py:23
  6.4 0.2 collective-permute-start.1
  6.6 1.7 %collective-permute-start.2 = (bf16[1,128,128]{2,1,0:T(8,128)(2,1)S(1)}, bf16[1,128,128]{2,1,0:T(8,128)(2,1)S(1)}, u32[]{:S(2)}, u32[]{:S(2)}) collective-permute-start(bf16[1,128,128]{2,1,0:T(8,128)(2,1)S(1)} %shard_map.82.refs_0_), channel_id=1, source_target_pairs={{0,4},{4,0},{8,12},{12,8},{1,5},{5,1},{9,13},{13,9},{2,6},{6,2},{1... | collective-permute-start | bytes 98312 | tf_op jit(solution)/shard_map/ppermute | solution.py:23
  8.3 3.1 %shard_map.83 = (f32[2,128,2048]{2,1,0:T(8,128)S(1)}, bf16[1,1024]{1,0:T(2,128)(2,1)S(1)}, bf16[2,128,2048]{2,1,0:T(8,128)(2,1)S(1)}, bf16[32,128]{1,0:T(8,128)(...) custom-call(bf16[128,1024]{1,0:T(8,128)(2,1)} %refs_0_.1, ...), custom_call_target="tpu_custom_call" | custom-call | tf_op jit(solution)/shard_map/pallas_call | solution.py:367
  11.4 0.0 collective-permute-done.3.cot_ref
  11.4 1.6 %shard_map.84 = (f32[2,128,2048]{2,1,0:T(8,128)S(1)}, bf16[1024,1024]{1,0:T(8,128)(2,1)S(1)}) custom-call(bf16[128,1024]{1,0:T(8,128)(2,1)S(1)} %collective-permute-done.3.cot_ref, bf16[1,1024]{1,0:T(2,128)(2,1)S(1)} %get-tuple-element.29.sign_ref, s32[64,128]{1,0:T(8,128)S(1)} %get-tuple-element.30.col_ref, f32[2,128,2048]{2,1,0:T(8,128)S(1)} %get-tuple-element.31.own_ref, ...), custom_call_target="tpu_custom_call" | custom-call | tf_op jit(solution)/shard_map/pallas_call | solution.py:396
  13.0 0.1 collective-permute-done.refs_1_
  13.1 0.0 collective-permute-done.1.refs_2_
  13.1 0.0 collective-permute-done.2.refs_3_
  13.1 0.8 %shard_map.86 = bf16[32,2048]{1,0:T(8,128)(2,1)S(1)} custom-call(bf16[1,128,128]{2,1,0:T(8,128)(2,1)S(1)} %shard_map.82.refs_0_, bf16[1,128,128]{2,1,0:T(8,128)(2,1)S(1)} %collective-permute-done.refs_1_, bf16[1,128,128]{2,1,0:T(8,128)(2,1)S(1)} %collective-permute-done.1.refs_2_, bf16[1,128,128]{2,1,0:T(8,128)(2,1)S(1)} %collective-permute-done.2.refs_3_, ...), custom_call_target="tpu_custom_call" | custom-call | tf_op jit(solution)/shard_map/pallas_call | solution.py:409
  13.9 0.1 collective-permute-start.4
  14.0 0.8 %shard_map.85.kept_ref = f32[32,2048]{1,0:T(8,128)S(1)} custom-call(bf16[1,128,128]{2,1,0:T(8,128)(2,1)S(1)} %shard_map.82.refs_0_, bf16[1,128,128]{2,1,0:T(8,128)(2,1)S(1)} %collective-permute-done.refs_1_, bf16[1,128,128]{2,1,0:T(8,128)(2,1)S(1)} %collective-permute-done.1.refs_2_, bf16[1,128,128]{2,1,0:T(8,128)(2,1)S(1)} %collective-permute-done.2.refs_3_, ...), custom_call_target="tpu_custom_call" | custom-call | tf_op jit(solution)/shard_map/pallas_call | solution.py:409
  14.8 0.6 %collective-permute-done.4.received_ref = bf16[32,2048]{1,0:T(8,128)(2,1)S(1)} collective-permute-done((bf16[32,2048]{1,0:T(8,128)(2,1)S(1)}, bf16[32,2048]{1,0:T(8,128)(2,1)S(1)}, u32[]{:S(2)}, u32[]{:S(2)}) %collective-permute-start.4) | collective-permute-done | bytes 131104 | tf_op jit(solution)/shard_map/ppermute | solution.py:23
  15.4 1.6 %collective-permute-start.5 = (bf16[16,2048]{1,0:T(8,128)(2,1)S(1)}, bf16[16,2048]{1,0:T(8,128)(2,1)S(1)}, u32[]{:S(2)}, u32[]{:S(2)}) collective-permute-start(bf16[16,2048]{1,0:T(8,128)(2,1)S(1)} %get-tuple-element.37.after_ref), channel_id=1, source_target_pairs={{0,2},{1,3},{2,0},{3,1},{4,6},{5,7},{6,4},{7,5},{8,10},{9,11},{10,... | collective-permute-start | bytes 196616 | tf_op jit(solution)/shard_map/ppermute | solution.py:23
  16.9 2.2 %shard_map.88 = (bf16[2048,1024]{1,0:T(8,128)(2,1)S(1)}, bf16[1024,2048]{1,0:T(8,128)(2,1)S(1)}, bf16[1024,1024]{1,0:T(8,128)(2,1)S(1)}, f32[8,128]{1,0:T(8,128)S(1)}) custom-call(bf16[2048,8192]{1,0:T(8,128)(2,1)} %matrix_ref.5, bf16[16,2048]{1,0:T(8,128)(2,1)S(1)} %get-tuple-element.37.after_ref, bf16[2048,1024]{1,0:T(8,128)(2,1)S(1)} %get-tuple-element.38.refs_0_, ...), custom_call_target="tpu_custom_call" | custom-call | tf_op jit(solution)/shard_map/pallas_call | solution.py:421
  19.1 0.6 %collective-permute-done.5.received_ref = bf16[16,2048]{1,0:T(8,128)(2,1)S(1)} collective-permute-done((bf16[16,2048]{1,0:T(8,128)(2,1)S(1)}, bf16[16,2048]{1,0:T(8,128)(2,1)S(1)}, u32[]{:S(2)}, u32[]{:S(2)}) %collective-permute-start.5) | collective-permute-done | bytes 65568 | tf_op jit(solution)/shard_map/ppermute | solution.py:23
  19.7 1.9 %collective-permute-start.8 = (bf16[16,2048]{1,0:T(8,128)(2,1)S(1)}, bf16[16,2048]{1,0:T(8,128)(2,1)S(1)}, u32[]{:S(2)}, u32[]{:S(2)}) collective-permute-start(bf16[16,2048]{1,0:T(8,128)(2,1)S(1)} %get-tuple-element.41.after_ref), channel_id=1, source_target_pairs={{0,8},{4,12},{8,0},{12,4},{1,9},{5,13},{9,1},{13,5},{2,10},{6,14},... | collective-permute-start | bytes 196616 | tf_op jit(solution)/shard_map/ppermute | solution.py:23
  21.6 1.8 %collective-permute-start.6 = (bf16[16,2048]{1,0:T(8,128)(2,1)S(1)}, bf16[16,2048]{1,0:T(8,128)(2,1)S(1)}, u32[]{:S(2)}, u32[]{:S(2)}) collective-permute-start(bf16[16,2048]{1,0:T(8,128)(2,1)S(1)} %get-tuple-element.41.after_ref), channel_id=1, source_target_pairs={{0,12},{4,8},{8,4},{12,0},{1,13},{5,9},{9,5},{13,1},{2,14},{6,10},... | collective-permute-start | bytes 196616 | tf_op jit(solution)/shard_map/ppermute | solution.py:23
  23.4 0.5 %collective-permute-start.7 = (bf16[16,2048]{1,0:T(8,128)(2,1)S(1)}, bf16[16,2048]{1,0:T(8,128)(2,1)S(1)}, u32[]{:S(2)}, u32[]{:S(2)}) collective-permute-start(bf16[16,2048]{1,0:T(8,128)(2,1)S(1)} %get-tuple-element.41.after_ref), channel_id=1, source_target_pairs={{0,4},{4,0},{8,12},{12,8},{1,5},{5,1},{9,13},{13,9},{2,6},{6,2},{1... | collective-permute-start | bytes 196616 | tf_op jit(solution)/shard_map/ppermute | solution.py:23
  23.9 2.2 %shard_map.91 = (bf16[1024,2048]{1,0:T(8,128)(2,1)S(1)}, bf16[1024,2048]{1,0:T(8,128)(2,1)S(1)}, bf16[1024,1024]{1,0:T(8,128)(2,1)S(1)}, f32[8,128]{1,0:T(8,128)S(1)}) custom-call(bf16[2048,8192]{1,0:T(8,128)(2,1)} %matrix_ref.5, bf16[16,2048]{1,0:T(8,128)(2,1)S(1)} %get-tuple-element.41.after_ref, bf16[2048,1024]{1,0:T(8,128)(2,1)S(1)} %get-tuple-element.43.refs_0_, ...), custom_call_target="tpu_custom_call" | custom-call | tf_op jit(solution)/shard_map/pallas_call | solution.py:421
  26.1 0.0 collective-permute-done.8.refs_1_
  26.2 1.2 %shard_map.93.sum_ref = f32[16,2048]{1,0:T(8,128)S(1)} custom-call(bf16[16,2048]{1,0:T(8,128)(2,1)S(1)} %shard_map.92.low_ref, bf16[1024,2048]{1,0:T(8,128)(2,1)S(1)} %get-tuple-element.49.lower_ref, bf16[1024,2048]{1,0:T(8,128)(2,1)S(1)} %get-tuple-element.50.upper_ref), custom_call_target="tpu_custom_call" | custom-call | tf_op jit(solution)/shard_map/pallas_call | solution.py:472
  27.3 0.5 %collective-permute-done.6.refs_0_ = bf16[16,2048]{1,0:T(8,128)(2,1)S(1)} collective-permute-done((bf16[16,2048]{1,0:T(8,128)(2,1)S(1)}, bf16[16,2048]{1,0:T(8,128)(2,1)S(1)}, u32[]{:S(2)}, u32[]{:S(2)}) %collective-permute-start.6) | collective-permute-done | bytes 65568 | tf_op jit(solution)/shard_map/ppermute | solution.py:23
  27.9 0.5 %collective-permute-done.7.refs_1_ = bf16[16,2048]{1,0:T(8,128)(2,1)S(1)} collective-permute-done((bf16[16,2048]{1,0:T(8,128)(2,1)S(1)}, bf16[16,2048]{1,0:T(8,128)(2,1)S(1)}, u32[]{:S(2)}, u32[]{:S(2)}) %collective-permute-start.7) | collective-permute-done | bytes 65568 | tf_op jit(solution)/shard_map/ppermute | solution.py:23
  28.4 1.2 %shard_map.94 = (f32[8,2048]{1,0:T(8,128)S(1)}, f32[8,2048]{1,0:T(8,128)S(1)}) custom-call(bf16[16,2048]{1,0:T(8,128)(2,1)S(1)} %shard_map.90.low_ref, bf16[1024,2048]{1,0:T(8,128)(2,1)S(1)} %get-tuple-element.42.lower_ref, bf16[1024,1024]{1,0:T(8,128)(2,1)S(1)} %get-tuple-element.45.upper_ref, bf16[1024,1024]{1,0:T(8,128)(2,1)S(1)} %get-tuple-element.46.last_ref, ...), custom_call_target="tpu_custom_call" | custom-call | tf_op jit(solution)/shard_map/pallas_call | solution.py:480
  29.6 0.0 collective-permute-start.9
  29.6 1.3 %collective-permute-done.9 = f32[8,2048]{1,0:T(8,128)S(1)} collective-permute-done((f32[8,2048]{1,0:T(8,128)S(1)}, f32[8,2048]{1,0:T(8,128)S(1)}, u32[]{:S(2)}, u32[]{:S(2)}) %collective-permute-start.9) | collective-permute-done | bytes 65568 | tf_op jit(solution)/shard_map/ppermute | solution.py:23
  30.9 0.6 %add_convert_fusion = bf16[8,2048]{1,0:T(8,128)(2,1)} fusion(f32[8,2048]{1,0:T(8,128)S(1)} %get-tuple-element.51, f32[8,2048]{1,0:T(8,128)S(1)} %collective-permute-done.9), kind=kLoop, calls=%fused_computation | loop fusion | flops 32768 | bytes 163840 | tf_op jit(solution)/shard_map/convert_element_type | solution.py:487
  (4 shorter events, 0.1 us)
Async XLA Ops:
  0.0 11.4 %collective-permute-start.3 = (bf16[128,1024]{1,0:T(8,128)(2,1)}, bf16[128,1024]{1,0:T(8,128)(2,1)S(1)}, u32[]{:S(2)}, u32[]{:S(2)}) collective-permute-start(bf16[128,1024]{1,0:T(8,128)(2,1)} %refs_0_.1), channel_id=1, source_target_pairs={{0,4},{4,0},{8,12},{12,8},{1,5},{5,1},{9,13},{13,9},{2,6},{6,2},{1... | collective-permute-start | bytes 786440 | tf_op jit(solution)/shard_map/ppermute | solution.py:23
  3.8 9.3 %collective-permute-start = (bf16[1,128,128]{2,1,0:T(8,128)(2,1)S(1)}, bf16[1,128,128]{2,1,0:T(8,128)(2,1)S(1)}, u32[]{:S(2)}, u32[]{:S(2)}) collective-permute-start(bf16[1,128,128]{2,1,0:T(8,128)(2,1)S(1)} %shard_map.82.refs_0_), channel_id=1, source_target_pairs={{0,12},{4,8},{8,4},{12,0},{1,13},{5,9},{9,5},{13,1},{2,14},{6,10},... | collective-permute-start | bytes 98312 | tf_op jit(solution)/shard_map/ppermute | solution.py:23
  6.4 6.8 %collective-permute-start.1 = (bf16[1,128,128]{2,1,0:T(8,128)(2,1)S(1)}, bf16[1,128,128]{2,1,0:T(8,128)(2,1)S(1)}, u32[]{:S(2)}, u32[]{:S(2)}) collective-permute-start(bf16[1,128,128]{2,1,0:T(8,128)(2,1)S(1)} %shard_map.82.refs_0_), channel_id=1, source_target_pairs={{0,8},{4,12},{8,0},{12,4},{1,9},{5,13},{9,1},{13,5},{2,10},{6,14},... | collective-permute-start | bytes 98312 | tf_op jit(solution)/shard_map/ppermute | solution.py:23
  6.6 6.6 %collective-permute-start.2 = (bf16[1,128,128]{2,1,0:T(8,128)(2,1)S(1)}, bf16[1,128,128]{2,1,0:T(8,128)(2,1)S(1)}, u32[]{:S(2)}, u32[]{:S(2)}) collective-permute-start(bf16[1,128,128]{2,1,0:T(8,128)(2,1)S(1)} %shard_map.82.refs_0_), channel_id=1, source_target_pairs={{0,4},{4,0},{8,12},{12,8},{1,5},{5,1},{9,13},{13,9},{2,6},{6,2},{1... | collective-permute-start | bytes 98312 | tf_op jit(solution)/shard_map/ppermute | solution.py:23
  13.9 1.4 %collective-permute-start.4 = (bf16[32,2048]{1,0:T(8,128)(2,1)S(1)}, bf16[32,2048]{1,0:T(8,128)(2,1)S(1)}, u32[]{:S(2)}, u32[]{:S(2)}) collective-permute-start(bf16[32,2048]{1,0:T(8,128)(2,1)S(1)} %shard_map.86), channel_id=1, source_target_pairs={{0,1},{1,0},{2,3},{3,2},{4,5},{5,4},{6,7},{7,6},{8,9},{9,8},{10,11... | collective-permute-start | bytes 393224 | tf_op jit(solution)/shard_map/ppermute | solution.py:23
  15.4 4.3 %collective-permute-start.5 = (bf16[16,2048]{1,0:T(8,128)(2,1)S(1)}, bf16[16,2048]{1,0:T(8,128)(2,1)S(1)}, u32[]{:S(2)}, u32[]{:S(2)}) collective-permute-start(bf16[16,2048]{1,0:T(8,128)(2,1)S(1)} %get-tuple-element.37.after_ref), channel_id=1, source_target_pairs={{0,2},{1,3},{2,0},{3,1},{4,6},{5,7},{6,4},{7,5},{8,10},{9,11},{10,... | collective-permute-start | bytes 196616 | tf_op jit(solution)/shard_map/ppermute | solution.py:23
  19.7 6.4 %collective-permute-start.8 = (bf16[16,2048]{1,0:T(8,128)(2,1)S(1)}, bf16[16,2048]{1,0:T(8,128)(2,1)S(1)}, u32[]{:S(2)}, u32[]{:S(2)}) collective-permute-start(bf16[16,2048]{1,0:T(8,128)(2,1)S(1)} %get-tuple-element.41.after_ref), channel_id=1, source_target_pairs={{0,8},{4,12},{8,0},{12,4},{1,9},{5,13},{9,1},{13,5},{2,10},{6,14},... | collective-permute-start | bytes 196616 | tf_op jit(solution)/shard_map/ppermute | solution.py:23
  21.6 6.3 %collective-permute-start.6 = (bf16[16,2048]{1,0:T(8,128)(2,1)S(1)}, bf16[16,2048]{1,0:T(8,128)(2,1)S(1)}, u32[]{:S(2)}, u32[]{:S(2)}) collective-permute-start(bf16[16,2048]{1,0:T(8,128)(2,1)S(1)} %get-tuple-element.41.after_ref), channel_id=1, source_target_pairs={{0,12},{4,8},{8,4},{12,0},{1,13},{5,9},{9,5},{13,1},{2,14},{6,10},... | collective-permute-start | bytes 196616 | tf_op jit(solution)/shard_map/ppermute | solution.py:23
  23.4 5.0 %collective-permute-start.7 = (bf16[16,2048]{1,0:T(8,128)(2,1)S(1)}, bf16[16,2048]{1,0:T(8,128)(2,1)S(1)}, u32[]{:S(2)}, u32[]{:S(2)}) collective-permute-start(bf16[16,2048]{1,0:T(8,128)(2,1)S(1)} %get-tuple-element.41.after_ref), channel_id=1, source_target_pairs={{0,4},{4,0},{8,12},{12,8},{1,5},{5,1},{9,13},{13,9},{2,6},{6,2},{1... | collective-permute-start | bytes 196616 | tf_op jit(solution)/shard_map/ppermute | solution.py:23
  29.6 1.3 %collective-permute-start.9 = (f32[8,2048]{1,0:T(8,128)S(1)}, f32[8,2048]{1,0:T(8,128)S(1)}, u32[]{:S(2)}, u32[]{:S(2)}) collective-permute-start(f32[8,2048]{1,0:T(8,128)S(1)} %get-tuple-element.52), channel_id=1, source_target_pairs={{0,1},{1,0},{2,3},{3,2},{4,5},{5,4},{6,7},{7,6},{8,9},{9,8},{10,11... | collective-permute-start | bytes 196616 | tf_op jit(solution)/shard_map/ppermute | solution.py:23

commit v7 on v6

--- a/solution.py
+++ b/solution.py
@@ -144,7 +144,7 @@
         (row_in, row_ref),
         (len_in, len_ref),
         (matrix_chunk(matrix_ref, 2, held_ref.shape, runs), held_ref),
-        (last_half(matrix_ref, 1, last_ref.shape, runs), last_ref),
+        (matrix_chunk(matrix_ref, 3, last_ref.shape, runs), last_ref),
     )
     copies = [pltpu.make_async_copy(*pair, sems.at[at]) for at, pair in enumerate(pairs)]
     for copy in copies:
@@ -186,23 +186,15 @@
     member_ref[...] = inside.astype(f32).astype(bf16)
 
 
-def right_kernel(row_count, cot_ref, sign_ref, col_ref, own_ref, matrix_ref, out_ref, last_ref, sem):
-    runs = run_count(row_count)
-    copy = pltpu.make_async_copy(last_half(matrix_ref, 0, last_ref.shape, runs), last_ref, sem)
-    copy.start()
-    rank = lax.axis_index("rows")
-
-    @pl.when(rank >= 0)
-    def _():
-        values = cot_ref[...] * sign_ref[...]
-        for flip in range(2):
-            first = 0
-            for part in right_block(values, quarter_index(col_ref, flip, runs), rank ^ 1, row_count):
-                columns = slice(first, first + part.shape[1])
-                out_ref[flip, :, columns] = own_ref[flip, :, columns] + part
-                first += part.shape[1]
-
-    copy.wait()
+def right_kernel(row_count, cot_ref, sign_ref, col_ref, own_ref, out_ref):
+    values = cot_ref[...] * sign_ref[...]
+    near = lax.axis_index("rows") ^ 1
+    for flip in range(2):
+        first = 0
+        for part in right_block(values, quarter_index(col_ref, flip, run_count(row_count)), near, row_count):
+            columns = slice(first, first + part.shape[1])
+            out_ref[flip, :, columns] = own_ref[flip, :, columns] + part
+            first += part.shape[1]
 
 
 def feature_kernel(flip, row_count, masks, hidden_refs, right_ref, row_ref, table_ref, member_ref, out_ref):
@@ -232,11 +224,6 @@
     out_ref[...] = total.astype(out_ref.dtype)
 
 
-def last_half(matrix_ref, half, shape, runs):
-    rows, depth = shape
-    return matrix_chunk(matrix_ref, 3, (2 * rows, depth), runs).at[pl.ds(half * rows, rows), :]
-
-
 def turn_kernel(chunk, runs, given, matrix_ref, after_ref, *refs):
     given_refs, (out_ref, *turned_refs, token_ref, sem) = refs[:given], refs[given:]
     copy = pltpu.make_async_copy(matrix_chunk(matrix_ref, chunk, out_ref.shape, runs), out_ref, sem)
@@ -280,35 +267,24 @@
     refs[-1][...] = (total * scale).astype(bf16)
 
 
-def times_transposed(low, refs):
-    parts = [
-        lax.dot_general(low, ref[...], contract_last, preferred_element_type=f32) for ref in refs
-    ]
-    return parts[0] if len(parts) == 1 else jnp.concatenate(parts, axis=1)
+def products(low, lower_ref, upper_ref, runs):
+    if runs == 1:
+        parts = [
+            lax.dot_general(low, ref[...], contract_last, preferred_element_type=f32)
+            for ref in (lower_ref, upper_ref)
+        ]
+        return jnp.concatenate(parts, axis=1)
+    run = low.shape[1] // 2
+    part = jnp.dot(low[:, :run], lower_ref[...], preferred_element_type=f32)
+    return part + jnp.dot(low[:, run:], upper_ref[...], preferred_element_type=f32)
 
 
 def own_score_kernel(runs, low_ref, lower_ref, upper_ref, out_ref):
-    low = low_ref[...]
-    if runs == 1:
-        out_ref[...] = times_transposed(low, (lower_ref, upper_ref))
-    else:
-        run = low.shape[1] // 2
-        part = jnp.dot(low[:, :run], lower_ref[...], preferred_element_type=f32)
-        out_ref[...] = part + jnp.dot(low[:, run:], upper_ref[...], preferred_element_type=f32)
-
-
-def near_score_kernel(runs, low_ref, lower_ref, upper_ref, last_ref, sum_ref, send_ref, keep_ref):
-    low = low_ref[...]
-    if runs == 1:
-        part = times_transposed(low, (lower_ref, upper_ref, last_ref))
-    else:
-        run = low.shape[1] // 2
-        part = jnp.dot(low[:, :run], lower_ref[...], preferred_element_type=f32)
-        halves = [
-            jnp.dot(low[:, run:], ref[...], preferred_element_type=f32) for ref in (upper_ref, last_ref)
-        ]
-        part = part + jnp.concatenate(halves, axis=1)
-    part = part + sum_ref[...]
+    out_ref[...] = products(low_ref[...], lower_ref, upper_ref, runs)
+
+
+def near_score_kernel(runs, low_ref, lower_ref, upper_ref, sum_ref, send_ref, keep_ref):
+    part = sum_ref[...] + products(low_ref[...], lower_ref, upper_ref, runs)
     own = part.shape[0] // 2
     lower = (lax.axis_index("ex") & 1) == 0
     keep_ref[...] = jnp.where(lower, part[:own], part[own:])
@@ -333,8 +309,6 @@
 
     runs = run_count(row_count)
     chunks = [pltpu.VMEM(chunk_shape(at, out_rows, quarter, runs), bf16) for at in range(4)]
-    last_rows, last_depth = chunks[3].shape
-    last_chunk = pltpu.VMEM((last_rows // 2, last_depth), bf16)
     table_shape = (feature_count // 128, 128)
 
     near_cot = swap(cotangent, "rows", 1)
@@ -364,7 +338,7 @@
     cot_width = cotangent.shape[1]
     lanes = min(128, cot_width)
     right_shape = pltpu.VMEM((2, tokens, quarter), f32)
-    right, near_signs, hidden_table, member, matrix_2, matrix_4, col_index, row_index = pl.pallas_call(
+    right, near_signs, hidden_table, member, matrix_2, matrix_3, col_index, row_index = pl.pallas_call(
         functools.partial(own_kernel, row_count),
         out_shape=(
             right_shape,
@@ -372,7 +346,7 @@
             pltpu.VMEM((2, width, quarter), bf16),
             pltpu.VMEM((example_count, tokens), bf16),
             chunks[2],
-            last_chunk,
+            chunks[3],
             pltpu.VMEM(table_shape, jnp.int32),
             pltpu.VMEM(table_shape, jnp.int32),
         ),
@@ -393,14 +367,13 @@
         in_hbm(lengths.reshape(1, -1)),
         in_hbm(inverse_rows),
     )
-    right, matrix_3 = pl.pallas_call(
+    right = pl.pallas_call(
         functools.partial(right_kernel, row_count),
-        out_shape=(right_shape, last_chunk),
-        in_specs=[whole] * 4 + [anywhere],
-        out_specs=(whole, whole),
-        scratch_shapes=[pltpu.SemaphoreType.DMA],
+        out_shape=right_shape,
+        in_specs=[whole] * 4,
+        out_specs=whole,
         compiler_params=params,
-    )(near_cot, near_signs, col_index, right, in_hbm(inverse_rows))
+    )(near_cot, near_signs, col_index, right)
 
     def features(flip):
         def kernel(*refs):
@@ -460,7 +433,7 @@
         send, total = add_up(total, received, count // 2 if axis == "ex" else count, token)
         token = None
         if matrix_1 is None:
-            matrix_1, (matrix_2, matrix_4), token = load_and_turn(1, send, [matrix_2, matrix_4])
+            matrix_1, (matrix_2,), token = load_and_turn(1, send, [matrix_2])
         received = swap(send, axis, mask)
     send, total = add_up(total, received, received.shape[0], token)
     matrix_0, (matrix_1, matrix_3), token = load_and_turn(0, send, [matrix_1, matrix_3])
@@ -480,10 +453,10 @@
     send, keep = pl.pallas_call(
         functools.partial(near_score_kernel, runs),
         out_shape=(own_shape, own_shape),
-        in_specs=[whole] * 5,
+        in_specs=[whole] * 4,
         out_specs=(whole, whole),
         compiler_params=params,
-    )(near_low, matrix_2, matrix_3, matrix_4, part)
+    )(near_low, matrix_2, matrix_3, part)
     return (keep + swap(send, "ex", 1)).astype(bf16)
 
 

time: 31.8 us -> 31.7 us (level)
  Pallas kernels: 13.9 us -> 14.6 us
  starting transfers between devices: 13.3 us -> 12.8 us
    pallas_call x1, Pallas kernels: 3.1 us -> 3.7 us  [local(): pl.pallas_call(functools.partial(own_kernel, row_count), out_shape=(right...]
    ppermute x10, starting transfers between devices: 13.3 us -> 12.8 us  [swap(): lax.ppermute(values, axis, [(rank, rank ^ mask) for rank in range(size)])]
  transfers between devices with their start and end apart: 10 -> 10, of which waited for: 6 -> 4; matrix products, arithmetic and copies ran while one was open for 0% -> 0% of each run, Pallas kernels for 38% -> 40%
where the time goes in v7:
time: 31.7 us; the launch traced here: 31.5 us
  Pallas kernels  14.6 us (46%)
  starting transfers between devices  12.8 us (40%)
  waiting for transfers between devices  3.41 us (11%)
  other arithmetic  0.62 us (2%)
    ppermute x10, starting transfers between devices, swap(): lax.ppermute(values, axis, [(rank, rank ^ mask) for rank in range(size)])  12.8 us
    pallas_call x2, Pallas kernels, load_and_turn(): pl.pallas_call(functools.partial(turn_kernel, chunk, runs, len(given)), o...  4.6 us
    pallas_call x1, Pallas kernels, local(): pl.pallas_call(functools.partial(own_kernel, row_count), out_shape=(right...  3.7 us
    ppermute x10, waiting for transfers between devices, swap(): lax.ppermute(values, axis, [(rank, rank ^ mask) for rank in range(size)])  3.41 us
    pallas_call x2, Pallas kernels, features(): pl.pallas_call(kernel, out_shape=pltpu.VMEM((example_count, quarter), bf1...  1.54 us
    pallas_call x1, Pallas kernels, local(): pl.pallas_call(functools.partial(right_kernel, row_count), out_shape=righ...  1.44 us
    pallas_call x1, Pallas kernels, local(): pl.pallas_call(functools.partial(near_score_kernel, runs), out_shape=(own...  1.2 us
    pallas_call x1, Pallas kernels, local(): pl.pallas_call(functools.partial(own_score_kernel, runs), out_shape=pltpu...  1.19 us
  transfers between devices with their start and end apart: 10, of which 4 were waited for; matrix products, arithmetic and copies ran while one was open for 0% of the time, Pallas kernels for 40%

profile of v7, /device:TPU:0, one launch (start us, length us, event | category | flops | bytes accessed | tf_op | source)
XLA Modules:
  0.0 31.5 jit_solution(962249187716600694)
XLA Ops:
  0.0 3.0 %collective-permute-start.3 = (bf16[128,1024]{1,0:T(8,128)(2,1)}, bf16[128,1024]{1,0:T(8,128)(2,1)S(1)}, u32[]{:S(2)}, u32[]{:S(2)}) collective-permute-start(bf16[128,1024]{1,0:T(8,128)(2,1)} %refs_0_.1), channel_id=1, source_target_pairs={{0,4},{4,0},{8,12},{12,8},{1,5},{5,1},{9,13},{13,9},{2,6},{6,2},{1... | collective-permute-start | bytes 786440 | tf_op jit(solution)/shard_map/ppermute | solution.py:23
  3.0 0.8 %shard_map.82.refs_0_ = bf16[1,128,128]{2,1,0:T(8,128)(2,1)S(1)} custom-call(bf16[128,128]{1,0:T(8,128)(2,1)} %hidden_in.1, s32[1,128]{1,0:T(1,128)} %bitcast.8), custom_call_target="tpu_custom_call" | custom-call | tf_op jit(solution)/shard_map/pallas_call | solution.py:315
  3.8 2.5 %collective-permute-start = (bf16[1,128,128]{2,1,0:T(8,128)(2,1)S(1)}, bf16[1,128,128]{2,1,0:T(8,128)(2,1)S(1)}, u32[]{:S(2)}, u32[]{:S(2)}) collective-permute-start(bf16[1,128,128]{2,1,0:T(8,128)(2,1)S(1)} %shard_map.82.refs_0_), channel_id=1, source_target_pairs={{0,12},{4,8},{8,4},{12,0},{1,13},{5,9},{9,5},{13,1},{2,14},{6,10},... | collective-permute-start | bytes 98312 | tf_op jit(solution)/shard_map/ppermute | solution.py:23
  6.4 0.2 collective-permute-start.1
  6.6 1.7 %collective-permute-start.2 = (bf16[1,128,128]{2,1,0:T(8,128)(2,1)S(1)}, bf16[1,128,128]{2,1,0:T(8,128)(2,1)S(1)}, u32[]{:S(2)}, u32[]{:S(2)}) collective-permute-start(bf16[1,128,128]{2,1,0:T(8,128)(2,1)S(1)} %shard_map.82.refs_0_), channel_id=1, source_target_pairs={{0,4},{4,0},{8,12},{12,8},{1,5},{5,1},{9,13},{13,9},{2,6},{6,2},{1... | collective-permute-start | bytes 98312 | tf_op jit(solution)/shard_map/ppermute | solution.py:23
  8.3 3.7 %shard_map.83 = (f32[2,128,2048]{2,1,0:T(8,128)S(1)}, bf16[1,1024]{1,0:T(2,128)(2,1)S(1)}, bf16[2,128,2048]{2,1,0:T(8,128)(2,1)S(1)}, bf16[32,128]{1,0:T(8,128)(...) custom-call(bf16[128,1024]{1,0:T(8,128)(2,1)} %refs_0_.1, ...), custom_call_target="tpu_custom_call" | custom-call | tf_op jit(solution)/shard_map/pallas_call | solution.py:341
  12.0 0.0 collective-permute-done.3.cot_ref
  12.0 1.4 %shard_map.84.refs_4_ = f32[2,128,2048]{2,1,0:T(8,128)S(1)} custom-call(bf16[128,1024]{1,0:T(8,128)(2,1)S(1)} %collective-permute-done.3.cot_ref, bf16[1,1024]{1,0:T(2,128)(2,1)S(1)} %get-tuple-element.26.sign_ref, s32[64,128]{1,0:T(8,128)S(1)} %get-tuple-element.27.col_ref, f32[2,128,2048]{2,1,0:T(8,128)S(1)} %get-tuple-element.28.own_ref), custom_call_target="tpu_custom_call" | custom-call | tf_op jit(solution)/shard_map/pallas_call | solution.py:370
  13.4 0.0 collective-permute-done.refs_1_
  13.4 0.0 collective-permute-done.1.refs_2_
  13.5 0.0 collective-permute-done.2.refs_3_
  13.5 0.8 %shard_map.86 = bf16[32,2048]{1,0:T(8,128)(2,1)S(1)} custom-call(bf16[1,128,128]{2,1,0:T(8,128)(2,1)S(1)} %shard_map.82.refs_0_, bf16[1,128,128]{2,1,0:T(8,128)(2,1)S(1)} %collective-permute-done.refs_1_, bf16[1,128,128]{2,1,0:T(8,128)(2,1)S(1)} %collective-permute-done.1.refs_2_, bf16[1,128,128]{2,1,0:T(8,128)(2,1)S(1)} %collective-permute-done.2.refs_3_, ...), custom_call_target="tpu_custom_call" | custom-call | tf_op jit(solution)/shard_map/pallas_call | solution.py:382
  14.2 0.1 collective-permute-start.4
  14.3 0.8 %shard_map.85.kept_ref = f32[32,2048]{1,0:T(8,128)S(1)} custom-call(bf16[1,128,128]{2,1,0:T(8,128)(2,1)S(1)} %shard_map.82.refs_0_, bf16[1,128,128]{2,1,0:T(8,128)(2,1)S(1)} %collective-permute-done.refs_1_, bf16[1,128,128]{2,1,0:T(8,128)(2,1)S(1)} %collective-permute-done.1.refs_2_, bf16[1,128,128]{2,1,0:T(8,128)(2,1)S(1)} %collective-permute-done.2.refs_3_, ...), custom_call_target="tpu_custom_call" | custom-call | tf_op jit(solution)/shard_map/pallas_call | solution.py:382
  15.1 0.6 %collective-permute-done.4.received_ref = bf16[32,2048]{1,0:T(8,128)(2,1)S(1)} collective-permute-done((bf16[32,2048]{1,0:T(8,128)(2,1)S(1)}, bf16[32,2048]{1,0:T(8,128)(2,1)S(1)}, u32[]{:S(2)}, u32[]{:S(2)}) %collective-permute-start.4) | collective-permute-done | bytes 131104 | tf_op jit(solution)/shard_map/ppermute | solution.py:23
  15.7 1.6 %collective-permute-start.5 = (bf16[16,2048]{1,0:T(8,128)(2,1)S(1)}, bf16[16,2048]{1,0:T(8,128)(2,1)S(1)}, u32[]{:S(2)}, u32[]{:S(2)}) collective-permute-start(bf16[16,2048]{1,0:T(8,128)(2,1)S(1)} %get-tuple-element.33.after_ref), channel_id=1, source_target_pairs={{0,2},{1,3},{2,0},{3,1},{4,6},{5,7},{6,4},{7,5},{8,10},{9,11},{10,... | collective-permute-start | bytes 196616 | tf_op jit(solution)/shard_map/ppermute | solution.py:23
  17.3 2.2 %shard_map.88 = (bf16[2048,1024]{1,0:T(8,128)(2,1)S(1)}, bf16[1024,2048]{1,0:T(8,128)(2,1)S(1)}, f32[8,128]{1,0:T(8,128)S(1)}) custom-call(bf16[2048,8192]{1,0:T(8,128)(2,1)} %matrix_ref.3, bf16[16,2048]{1,0:T(8,128)(2,1)S(1)} %get-tuple-element.33.after_ref, bf16[2048,1024]{1,0:T(8,128)(2,1)S(1)} %get-tuple-element.34.refs_0_), custom_call_target="tpu_custom_call" | custom-call | tf_op jit(solution)/shard_map/pallas_call | solution.py:394
  19.5 0.6 %collective-permute-done.5.received_ref = bf16[16,2048]{1,0:T(8,128)(2,1)S(1)} collective-permute-done((bf16[16,2048]{1,0:T(8,128)(2,1)S(1)}, bf16[16,2048]{1,0:T(8,128)(2,1)S(1)}, u32[]{:S(2)}, u32[]{:S(2)}) %collective-permute-start.5) | collective-permute-done | bytes 65568 | tf_op jit(solution)/shard_map/ppermute | solution.py:23
  20.0 1.8 %collective-permute-start.8 = (bf16[16,2048]{1,0:T(8,128)(2,1)S(1)}, bf16[16,2048]{1,0:T(8,128)(2,1)S(1)}, u32[]{:S(2)}, u32[]{:S(2)}) collective-permute-start(bf16[16,2048]{1,0:T(8,128)(2,1)S(1)} %get-tuple-element.36.after_ref), channel_id=1, source_target_pairs={{0,8},{4,12},{8,0},{12,4},{1,9},{5,13},{9,1},{13,5},{2,10},{6,14},... | collective-permute-start | bytes 196616 | tf_op jit(solution)/shard_map/ppermute | solution.py:23
  21.8 1.4 %collective-permute-start.6 = (bf16[16,2048]{1,0:T(8,128)(2,1)S(1)}, bf16[16,2048]{1,0:T(8,128)(2,1)S(1)}, u32[]{:S(2)}, u32[]{:S(2)}) collective-permute-start(bf16[16,2048]{1,0:T(8,128)(2,1)S(1)} %get-tuple-element.36.after_ref), channel_id=1, source_target_pairs={{0,12},{4,8},{8,4},{12,0},{1,13},{5,9},{9,5},{13,1},{2,14},{6,10},... | collective-permute-start | bytes 196616 | tf_op jit(solution)/shard_map/ppermute | solution.py:23
  23.3 0.5 %collective-permute-start.7 = (bf16[16,2048]{1,0:T(8,128)(2,1)S(1)}, bf16[16,2048]{1,0:T(8,128)(2,1)S(1)}, u32[]{:S(2)}, u32[]{:S(2)}) collective-permute-start(bf16[16,2048]{1,0:T(8,128)(2,1)S(1)} %get-tuple-element.36.after_ref), channel_id=1, source_target_pairs={{0,4},{4,0},{8,12},{12,8},{1,5},{5,1},{9,13},{13,9},{2,6},{6,2},{1... | collective-permute-start | bytes 196616 | tf_op jit(solution)/shard_map/ppermute | solution.py:23
  23.7 2.4 %shard_map.91 = (bf16[1024,2048]{1,0:T(8,128)(2,1)S(1)}, bf16[1024,2048]{1,0:T(8,128)(2,1)S(1)}, bf16[1024,2048]{1,0:T(8,128)(2,1)S(1)}, f32[8,128]{1,0:T(8,128)S(1)}) custom-call(bf16[2048,8192]{1,0:T(8,128)(2,1)} %matrix_ref.3, bf16[16,2048]{1,0:T(8,128)(2,1)S(1)} %get-tuple-element.36.after_ref, bf16[2048,1024]{1,0:T(8,128)(2,1)S(1)} %get-tuple-element.38.refs_0_, ...), custom_call_target="tpu_custom_call" | custom-call | tf_op jit(solution)/shard_map/pallas_call | solution.py:394
  26.1 1.0 %collective-permute-done.8.refs_1_ = bf16[16,2048]{1,0:T(8,128)(2,1)S(1)} collective-permute-done((bf16[16,2048]{1,0:T(8,128)(2,1)S(1)}, bf16[16,2048]{1,0:T(8,128)(2,1)S(1)}, u32[]{:S(2)}, u32[]{:S(2)}) %collective-permute-start.8) | collective-permute-done | bytes 65568 | tf_op jit(solution)/shard_map/ppermute | solution.py:23
  27.2 1.2 %shard_map.93.sum_ref = f32[16,2048]{1,0:T(8,128)S(1)} custom-call(bf16[16,2048]{1,0:T(8,128)(2,1)S(1)} %shard_map.92.low_ref, bf16[1024,2048]{1,0:T(8,128)(2,1)S(1)} %get-tuple-element.43.lower_ref, bf16[1024,2048]{1,0:T(8,128)(2,1)S(1)} %get-tuple-element.44.upper_ref), custom_call_target="tpu_custom_call" | custom-call | tf_op jit(solution)/shard_map/pallas_call | solution.py:445
  28.4 0.0 collective-permute-done.6.refs_0_
  28.4 0.0 collective-permute-done.7.refs_1_
  28.4 1.2 %shard_map.94 = (f32[8,2048]{1,0:T(8,128)S(1)}, f32[8,2048]{1,0:T(8,128)S(1)}) custom-call(bf16[16,2048]{1,0:T(8,128)(2,1)S(1)} %shard_map.90.low_ref, bf16[1024,2048]{1,0:T(8,128)(2,1)S(1)} %get-tuple-element.37.lower_ref, bf16[1024,2048]{1,0:T(8,128)(2,1)S(1)} %get-tuple-element.40.upper_ref, f32[16,2048]{1,0:T(8,128)S(1)} %shard_map.93.sum_ref), custom_call_target="tpu_custom_call" | custom-call | tf_op jit(solution)/shard_map/pallas_call | solution.py:453
  29.6 0.0 collective-permute-start.9
  29.6 1.3 %collective-permute-done.9 = f32[8,2048]{1,0:T(8,128)S(1)} collective-permute-done((f32[8,2048]{1,0:T(8,128)S(1)}, f32[8,2048]{1,0:T(8,128)S(1)}, u32[]{:S(2)}, u32[]{:S(2)}) %collective-permute-start.9) | collective-permute-done | bytes 65568 | tf_op jit(solution)/shard_map/ppermute | solution.py:23
  30.9 0.6 %add_convert_fusion = bf16[8,2048]{1,0:T(8,128)(2,1)} fusion(f32[8,2048]{1,0:T(8,128)S(1)} %get-tuple-element.45, f32[8,2048]{1,0:T(8,128)S(1)} %collective-permute-done.9), kind=kLoop, calls=%fused_computation | loop fusion | flops 32768 | bytes 163840 | tf_op jit(solution)/shard_map/convert_element_type | solution.py:460
  (4 shorter events, 0.1 us)
Async XLA Ops:
  0.0 12.0 %collective-permute-start.3 = (bf16[128,1024]{1,0:T(8,128)(2,1)}, bf16[128,1024]{1,0:T(8,128)(2,1)S(1)}, u32[]{:S(2)}, u32[]{:S(2)}) collective-permute-start(bf16[128,1024]{1,0:T(8,128)(2,1)} %refs_0_.1), channel_id=1, source_target_pairs={{0,4},{4,0},{8,12},{12,8},{1,5},{5,1},{9,13},{13,9},{2,6},{6,2},{1... | collective-permute-start | bytes 786440 | tf_op jit(solution)/shard_map/ppermute | solution.py:23
  3.8 9.6 %collective-permute-start = (bf16[1,128,128]{2,1,0:T(8,128)(2,1)S(1)}, bf16[1,128,128]{2,1,0:T(8,128)(2,1)S(1)}, u32[]{:S(2)}, u32[]{:S(2)}) collective-permute-start(bf16[1,128,128]{2,1,0:T(8,128)(2,1)S(1)} %shard_map.82.refs_0_), channel_id=1, source_target_pairs={{0,12},{4,8},{8,4},{12,0},{1,13},{5,9},{9,5},{13,1},{2,14},{6,10},... | collective-permute-start | bytes 98312 | tf_op jit(solution)/shard_map/ppermute | solution.py:23
  6.4 7.1 %collective-permute-start.1 = (bf16[1,128,128]{2,1,0:T(8,128)(2,1)S(1)}, bf16[1,128,128]{2,1,0:T(8,128)(2,1)S(1)}, u32[]{:S(2)}, u32[]{:S(2)}) collective-permute-start(bf16[1,128,128]{2,1,0:T(8,128)(2,1)S(1)} %shard_map.82.refs_0_), channel_id=1, source_target_pairs={{0,8},{4,12},{8,0},{12,4},{1,9},{5,13},{9,1},{13,5},{2,10},{6,14},... | collective-permute-start | bytes 98312 | tf_op jit(solution)/shard_map/ppermute | solution.py:23
  6.6 6.9 %collective-permute-start.2 = (bf16[1,128,128]{2,1,0:T(8,128)(2,1)S(1)}, bf16[1,128,128]{2,1,0:T(8,128)(2,1)S(1)}, u32[]{:S(2)}, u32[]{:S(2)}) collective-permute-start(bf16[1,128,128]{2,1,0:T(8,128)(2,1)S(1)} %shard_map.82.refs_0_), channel_id=1, source_target_pairs={{0,4},{4,0},{8,12},{12,8},{1,5},{5,1},{9,13},{13,9},{2,6},{6,2},{1... | collective-permute-start | bytes 98312 | tf_op jit(solution)/shard_map/ppermute | solution.py:23
  14.2 1.4 %collective-permute-start.4 = (bf16[32,2048]{1,0:T(8,128)(2,1)S(1)}, bf16[32,2048]{1,0:T(8,128)(2,1)S(1)}, u32[]{:S(2)}, u32[]{:S(2)}) collective-permute-start(bf16[32,2048]{1,0:T(8,128)(2,1)S(1)} %shard_map.86), channel_id=1, source_target_pairs={{0,1},{1,0},{2,3},{3,2},{4,5},{5,4},{6,7},{7,6},{8,9},{9,8},{10,11... | collective-permute-start | bytes 393224 | tf_op jit(solution)/shard_map/ppermute | solution.py:23
  15.7 4.3 %collective-permute-start.5 = (bf16[16,2048]{1,0:T(8,128)(2,1)S(1)}, bf16[16,2048]{1,0:T(8,128)(2,1)S(1)}, u32[]{:S(2)}, u32[]{:S(2)}) collective-permute-start(bf16[16,2048]{1,0:T(8,128)(2,1)S(1)} %get-tuple-element.33.after_ref), channel_id=1, source_target_pairs={{0,2},{1,3},{2,0},{3,1},{4,6},{5,7},{6,4},{7,5},{8,10},{9,11},{10,... | collective-permute-start | bytes 196616 | tf_op jit(solution)/shard_map/ppermute | solution.py:23
  20.0 7.1 %collective-permute-start.8 = (bf16[16,2048]{1,0:T(8,128)(2,1)S(1)}, bf16[16,2048]{1,0:T(8,128)(2,1)S(1)}, u32[]{:S(2)}, u32[]{:S(2)}) collective-permute-start(bf16[16,2048]{1,0:T(8,128)(2,1)S(1)} %get-tuple-element.36.after_ref), channel_id=1, source_target_pairs={{0,8},{4,12},{8,0},{12,4},{1,9},{5,13},{9,1},{13,5},{2,10},{6,14},... | collective-permute-start | bytes 196616 | tf_op jit(solution)/shard_map/ppermute | solution.py:23
  21.8 6.6 %collective-permute-start.6 = (bf16[16,2048]{1,0:T(8,128)(2,1)S(1)}, bf16[16,2048]{1,0:T(8,128)(2,1)S(1)}, u32[]{:S(2)}, u32[]{:S(2)}) collective-permute-start(bf16[16,2048]{1,0:T(8,128)(2,1)S(1)} %get-tuple-element.36.after_ref), channel_id=1, source_target_pairs={{0,12},{4,8},{8,4},{12,0},{1,13},{5,9},{9,5},{13,1},{2,14},{6,10},... | collective-permute-start | bytes 196616 | tf_op jit(solution)/shard_map/ppermute | solution.py:23
  23.3 5.1 %collective-permute-start.7 = (bf16[16,2048]{1,0:T(8,128)(2,1)S(1)}, bf16[16,2048]{1,0:T(8,128)(2,1)S(1)}, u32[]{:S(2)}, u32[]{:S(2)}) collective-permute-start(bf16[16,2048]{1,0:T(8,128)(2,1)S(1)} %get-tuple-element.36.after_ref), channel_id=1, source_target_pairs={{0,4},{4,0},{8,12},{12,8},{1,5},{5,1},{9,13},{13,9},{2,6},{6,2},{1... | collective-permute-start | bytes 196616 | tf_op jit(solution)/shard_map/ppermute | solution.py:23
  29.6 1.3 %collective-permute-start.9 = (f32[8,2048]{1,0:T(8,128)S(1)}, f32[8,2048]{1,0:T(8,128)S(1)}, u32[]{:S(2)}, u32[]{:S(2)}) collective-permute-start(f32[8,2048]{1,0:T(8,128)S(1)} %get-tuple-element.46), channel_id=1, source_target_pairs={{0,1},{1,0},{2,3},{3,2},{4,5},{5,4},{6,7},{7,6},{8,9},{9,8},{10,11... | collective-permute-start | bytes 196616 | tf_op jit(solution)/shard_map/ppermute | solution.py:23

commit v8 on v6

--- a/solution.py
+++ b/solution.py
@@ -144,7 +144,7 @@
         (row_in, row_ref),
         (len_in, len_ref),
         (matrix_chunk(matrix_ref, 2, held_ref.shape, runs), held_ref),
-        (last_half(matrix_ref, 1, last_ref.shape, runs), last_ref),
+        (half_chunk(matrix_ref, 3, 1, last_ref.shape, runs), last_ref),
     )
     copies = [pltpu.make_async_copy(*pair, sems.at[at]) for at, pair in enumerate(pairs)]
     for copy in copies:
@@ -188,7 +188,7 @@
 
 def right_kernel(row_count, cot_ref, sign_ref, col_ref, own_ref, matrix_ref, out_ref, last_ref, sem):
     runs = run_count(row_count)
-    copy = pltpu.make_async_copy(last_half(matrix_ref, 0, last_ref.shape, runs), last_ref, sem)
+    copy = pltpu.make_async_copy(half_chunk(matrix_ref, 3, 0, last_ref.shape, runs), last_ref, sem)
     copy.start()
     rank = lax.axis_index("rows")
 
@@ -232,15 +232,24 @@
     out_ref[...] = total.astype(out_ref.dtype)
 
 
-def last_half(matrix_ref, half, shape, runs):
+def half_chunk(matrix_ref, chunk, half, shape, runs):
     rows, depth = shape
-    return matrix_chunk(matrix_ref, 3, (2 * rows, depth), runs).at[pl.ds(half * rows, rows), :]
-
-
-def turn_kernel(chunk, runs, given, matrix_ref, after_ref, *refs):
-    given_refs, (out_ref, *turned_refs, token_ref, sem) = refs[:given], refs[given:]
-    copy = pltpu.make_async_copy(matrix_chunk(matrix_ref, chunk, out_ref.shape, runs), out_ref, sem)
-    copy.start()
+    return matrix_chunk(matrix_ref, chunk, (2 * rows, depth), runs).at[pl.ds(half * rows, rows), :]
+
+
+def turn_kernel(late, runs, given, matrix_ref, after_ref, *refs):
+    given_refs, refs = refs[:given], refs[given:]
+    loaded = 2 if late else 1
+    out_refs, (*turned_refs, token_ref, sems) = refs[:loaded], refs[loaded:]
+    sources = [half_chunk(matrix_ref, 1, loaded - 1, out_refs[0].shape, runs)]
+    if late:
+        sources.append(matrix_chunk(matrix_ref, 0, out_refs[1].shape, runs))
+    copies = [
+        pltpu.make_async_copy(source, ref, sems.at[at])
+        for at, (source, ref) in enumerate(zip(sources, out_refs))
+    ]
+    for copy in copies:
+        copy.start()
     token_ref[...] = jnp.zeros_like(token_ref)
 
     @pl.when(lax.axis_index("rows") >= 0)
@@ -259,7 +268,8 @@
                     preferred_element_type=f32,
                 ).astype(bf16)
 
-    copy.wait()
+    for copy in copies:
+        copy.wait()
 
 
 def add_kernel(kept_ref, received_ref, *refs):
@@ -287,14 +297,16 @@
     return parts[0] if len(parts) == 1 else jnp.concatenate(parts, axis=1)
 
 
-def own_score_kernel(runs, low_ref, lower_ref, upper_ref, out_ref):
+def own_score_kernel(runs, low_ref, lower_ref, upper_ref, last_ref, out_ref):
     low = low_ref[...]
     if runs == 1:
-        out_ref[...] = times_transposed(low, (lower_ref, upper_ref))
+        out_ref[...] = times_transposed(low, (lower_ref, upper_ref, last_ref))
     else:
         run = low.shape[1] // 2
         part = jnp.dot(low[:, :run], lower_ref[...], preferred_element_type=f32)
-        out_ref[...] = part + jnp.dot(low[:, run:], upper_ref[...], preferred_element_type=f32)
+        upper = jnp.dot(low[:, run:], upper_ref[...], preferred_element_type=f32)
+        last = times_transposed(low[:, run:], (last_ref,))
+        out_ref[...] = part + jnp.concatenate([upper, last], axis=1)
 
 
 def near_score_kernel(runs, low_ref, lower_ref, upper_ref, last_ref, sum_ref, send_ref, keep_ref):
@@ -416,17 +428,18 @@
 
     token_shape = pltpu.VMEM((8, 128), f32)
 
-    def load_and_turn(chunk, after, given):
+    def load_and_turn(late, after, given):
+        loaded = [last_chunk] + [chunks[0]] * late
         turned = [pltpu.VMEM(values.shape[::-1], bf16) for values in given] if runs > 1 else []
-        loaded, *outs, token = pl.pallas_call(
-            functools.partial(turn_kernel, chunk, runs, len(given)),
-            out_shape=(chunks[chunk], *turned, token_shape),
+        outs = pl.pallas_call(
+            functools.partial(turn_kernel, late, runs, len(given)),
+            out_shape=(*loaded, *turned, token_shape),
             in_specs=[anywhere] + [whole] * (1 + len(given)),
-            out_specs=(whole,) * (len(turned) + 2),
-            scratch_shapes=[pltpu.SemaphoreType.DMA],
+            out_specs=(whole,) * (len(loaded) + len(turned) + 1),
+            scratch_shapes=[pltpu.SemaphoreType.DMA((len(loaded),))],
             compiler_params=params,
         )(in_hbm(inverse_rows), after, *given)
-        return loaded, outs if turned else given, token
+        return outs[: len(loaded)], outs[len(loaded) : -1] if turned else given, outs[-1]
 
     def add_up(kept, received, send_count, token):
         count = received.shape[0]
@@ -460,10 +473,14 @@
         send, total = add_up(total, received, count // 2 if axis == "ex" else count, token)
         token = None
         if matrix_1 is None:
-            matrix_1, (matrix_2, matrix_4), token = load_and_turn(1, send, [matrix_2, matrix_4])
+            (matrix_1,), (matrix_2, matrix_4), token = load_and_turn(
+                False, send, [matrix_2, matrix_4]
+            )
         received = swap(send, axis, mask)
     send, total = add_up(total, received, received.shape[0], token)
-    matrix_0, (matrix_1, matrix_3), token = load_and_turn(0, send, [matrix_1, matrix_3])
+    (matrix_5, matrix_0), (matrix_1, matrix_3), token = load_and_turn(
+        True, send, [matrix_1, matrix_3]
+    )
     others = [swap(send, "rows", mask) for mask in range(1, group)]
     turned = runs > 1
     low = features_low([total] + others[1:2], [False, turned], token)
@@ -472,10 +489,10 @@
     part = pl.pallas_call(
         functools.partial(own_score_kernel, runs),
         out_shape=pltpu.VMEM((2 * own_examples, out_rows), f32),
-        in_specs=[whole] * 3,
+        in_specs=[whole] * 4,
         out_specs=whole,
         compiler_params=params,
-    )(low, matrix_0, matrix_1)
+    )(low, matrix_0, matrix_1, matrix_5)
     own_shape = pltpu.VMEM((own_examples, out_rows), f32)
     send, keep = pl.pallas_call(
         functools.partial(near_score_kernel, runs),

time: 31.8 us -> 31.7 us (level)
  Pallas kernels: 13.9 us -> 14.5 us
  waiting for transfers between devices: 3.56 us -> 2.99 us
    ppermute x10, waiting for transfers between devices: 3.56 us -> 2.99 us  [swap(): lax.ppermute(values, axis, [(rank, rank ^ mask) for rank in range(size)])]
  transfers between devices with their start and end apart: 10 -> 10, of which waited for: 6 -> 5; matrix products, arithmetic and copies ran while one was open for 0% -> 0% of each run, Pallas kernels for 38% -> 40%
where the time goes in v8:
time: 31.7 us; the launch traced here: 31.5 us
  Pallas kernels  14.5 us (46%)
  starting transfers between devices  13.3 us (42%)
  waiting for transfers between devices  2.99 us (9%)
  other arithmetic  0.62 us (2%)
    ppermute x10, starting transfers between devices, swap(): lax.ppermute(values, axis, [(rank, rank ^ mask) for rank in range(size)])  13.3 us
    pallas_call x2, Pallas kernels, load_and_turn(): pl.pallas_call(functools.partial(turn_kernel, late, runs, len(given)), ou...  4.7 us
    pallas_call x1, Pallas kernels, local(): pl.pallas_call(functools.partial(own_kernel, row_count), out_shape=(right...  3.1 us
    ppermute x10, waiting for transfers between devices, swap(): lax.ppermute(values, axis, [(rank, rank ^ mask) for rank in range(size)])  2.99 us
    pallas_call x1, Pallas kernels, local(): pl.pallas_call(functools.partial(right_kernel, row_count), out_shape=(rig...  1.61 us
    pallas_call x2, Pallas kernels, features(): pl.pallas_call(kernel, out_shape=pltpu.VMEM((example_count, quarter), bf1...  1.52 us
    pallas_call x1, Pallas kernels, local(): pl.pallas_call(functools.partial(own_score_kernel, runs), out_shape=pltpu...  1.46 us
    pallas_call x1, Pallas kernels, local(): pl.pallas_call(functools.partial(near_score_kernel, runs), out_shape=(own...  1.2 us
  transfers between devices with their start and end apart: 10, of which 5 were waited for; matrix products, arithmetic and copies ran while one was open for 0% of the time, Pallas kernels for 40%

profile of v8, /device:TPU:0, one launch (start us, length us, event | category | flops | bytes accessed | tf_op | source)
XLA Modules:
  0.0 31.5 jit_solution(4217644280482649750)
XLA Ops:
  0.0 3.0 %collective-permute-start.3 = (bf16[128,1024]{1,0:T(8,128)(2,1)}, bf16[128,1024]{1,0:T(8,128)(2,1)S(1)}, u32[]{:S(2)}, u32[]{:S(2)}) collective-permute-start(bf16[128,1024]{1,0:T(8,128)(2,1)} %refs_0_.1), channel_id=1, source_target_pairs={{0,4},{4,0},{8,12},{12,8},{1,5},{5,1},{9,13},{13,9},{2,6},{6,2},{1... | collective-permute-start | bytes 786440 | tf_op jit(solution)/shard_map/ppermute | solution.py:23
  3.0 0.8 %shard_map.82.refs_0_ = bf16[1,128,128]{2,1,0:T(8,128)(2,1)S(1)} custom-call(bf16[128,128]{1,0:T(8,128)(2,1)} %hidden_in.1, s32[1,128]{1,0:T(1,128)} %bitcast.8), custom_call_target="tpu_custom_call" | custom-call | tf_op jit(solution)/shard_map/pallas_call | solution.py:353
  3.8 2.5 %collective-permute-start = (bf16[1,128,128]{2,1,0:T(8,128)(2,1)S(1)}, bf16[1,128,128]{2,1,0:T(8,128)(2,1)S(1)}, u32[]{:S(2)}, u32[]{:S(2)}) collective-permute-start(bf16[1,128,128]{2,1,0:T(8,128)(2,1)S(1)} %shard_map.82.refs_0_), channel_id=1, source_target_pairs={{0,12},{4,8},{8,4},{12,0},{1,13},{5,9},{9,5},{13,1},{2,14},{6,10},... | collective-permute-start | bytes 98312 | tf_op jit(solution)/shard_map/ppermute | solution.py:23
  6.4 0.2 collective-permute-start.1
  6.6 1.7 %collective-permute-start.2 = (bf16[1,128,128]{2,1,0:T(8,128)(2,1)S(1)}, bf16[1,128,128]{2,1,0:T(8,128)(2,1)S(1)}, u32[]{:S(2)}, u32[]{:S(2)}) collective-permute-start(bf16[1,128,128]{2,1,0:T(8,128)(2,1)S(1)} %shard_map.82.refs_0_), channel_id=1, source_target_pairs={{0,4},{4,0},{8,12},{12,8},{1,5},{5,1},{9,13},{13,9},{2,6},{6,2},{1... | collective-permute-start | bytes 98312 | tf_op jit(solution)/shard_map/ppermute | solution.py:23
  8.3 3.1 %shard_map.83 = (f32[2,128,2048]{2,1,0:T(8,128)S(1)}, bf16[1,1024]{1,0:T(2,128)(2,1)S(1)}, bf16[2,128,2048]{2,1,0:T(8,128)(2,1)S(1)}, bf16[32,128]{1,0:T(8,128)(...) custom-call(bf16[128,1024]{1,0:T(8,128)(2,1)} %refs_0_.1, ...), custom_call_target="tpu_custom_call" | custom-call | tf_op jit(solution)/shard_map/pallas_call | solution.py:379
  11.4 0.0 collective-permute-done.3.cot_ref
  11.4 1.6 %shard_map.84 = (f32[2,128,2048]{2,1,0:T(8,128)S(1)}, bf16[1024,1024]{1,0:T(8,128)(2,1)S(1)}) custom-call(bf16[128,1024]{1,0:T(8,128)(2,1)S(1)} %collective-permute-done.3.cot_ref, bf16[1,1024]{1,0:T(2,128)(2,1)S(1)} %get-tuple-element.30.sign_ref, s32[64,128]{1,0:T(8,128)S(1)} %get-tuple-element.31.col_ref, f32[2,128,2048]{2,1,0:T(8,128)S(1)} %get-tuple-element.32.own_ref, ...), custom_call_target="tpu_custom_call" | custom-call | tf_op jit(solution)/shard_map/pallas_call | solution.py:408
  13.0 0.1 collective-permute-done.refs_1_
  13.1 0.0 collective-permute-done.1.refs_2_
  13.1 0.0 collective-permute-done.2.refs_3_
  13.1 0.8 %shard_map.86 = bf16[32,2048]{1,0:T(8,128)(2,1)S(1)} custom-call(bf16[1,128,128]{2,1,0:T(8,128)(2,1)S(1)} %shard_map.82.refs_0_, bf16[1,128,128]{2,1,0:T(8,128)(2,1)S(1)} %collective-permute-done.refs_1_, bf16[1,128,128]{2,1,0:T(8,128)(2,1)S(1)} %collective-permute-done.1.refs_2_, bf16[1,128,128]{2,1,0:T(8,128)(2,1)S(1)} %collective-permute-done.2.refs_3_, ...), custom_call_target="tpu_custom_call" | custom-call | tf_op jit(solution)/shard_map/pallas_call | solution.py:421
  13.9 0.1 collective-permute-start.4
  14.0 0.8 %shard_map.85.kept_ref = f32[32,2048]{1,0:T(8,128)S(1)} custom-call(bf16[1,128,128]{2,1,0:T(8,128)(2,1)S(1)} %shard_map.82.refs_0_, bf16[1,128,128]{2,1,0:T(8,128)(2,1)S(1)} %collective-permute-done.refs_1_, bf16[1,128,128]{2,1,0:T(8,128)(2,1)S(1)} %collective-permute-done.1.refs_2_, bf16[1,128,128]{2,1,0:T(8,128)(2,1)S(1)} %collective-permute-done.2.refs_3_, ...), custom_call_target="tpu_custom_call" | custom-call | tf_op jit(solution)/shard_map/pallas_call | solution.py:421
  14.8 0.6 %collective-permute-done.4.received_ref = bf16[32,2048]{1,0:T(8,128)(2,1)S(1)} collective-permute-done((bf16[32,2048]{1,0:T(8,128)(2,1)S(1)}, bf16[32,2048]{1,0:T(8,128)(2,1)S(1)}, u32[]{:S(2)}, u32[]{:S(2)}) %collective-permute-start.4) | collective-permute-done | bytes 131104 | tf_op jit(solution)/shard_map/ppermute | solution.py:23
  15.4 1.6 %collective-permute-start.5 = (bf16[16,2048]{1,0:T(8,128)(2,1)S(1)}, bf16[16,2048]{1,0:T(8,128)(2,1)S(1)}, u32[]{:S(2)}, u32[]{:S(2)}) collective-permute-start(bf16[16,2048]{1,0:T(8,128)(2,1)S(1)} %get-tuple-element.38.after_ref), channel_id=1, source_target_pairs={{0,2},{1,3},{2,0},{3,1},{4,6},{5,7},{6,4},{7,5},{8,10},{9,11},{10,... | collective-permute-start | bytes 196616 | tf_op jit(solution)/shard_map/ppermute | solution.py:23
  16.9 1.8 %shard_map.88 = (bf16[1024,1024]{1,0:T(8,128)(2,1)S(1)}, bf16[1024,2048]{1,0:T(8,128)(2,1)S(1)}, bf16[1024,1024]{1,0:T(8,128)(2,1)S(1)}, f32[8,128]{1,0:T(8,128)S(1)}) custom-call(bf16[2048,8192]{1,0:T(8,128)(2,1)} %matrix_ref.5, bf16[16,2048]{1,0:T(8,128)(2,1)S(1)} %get-tuple-element.38.after_ref, bf16[2048,1024]{1,0:T(8,128)(2,1)S(1)} %get-tuple-element.39.refs_0_, ...), custom_call_target="tpu_custom_call" | custom-call | tf_op jit(solution)/shard_map/pallas_call | solution.py:434
  18.8 0.9 %collective-permute-done.5.received_ref = bf16[16,2048]{1,0:T(8,128)(2,1)S(1)} collective-permute-done((bf16[16,2048]{1,0:T(8,128)(2,1)S(1)}, bf16[16,2048]{1,0:T(8,128)(2,1)S(1)}, u32[]{:S(2)}, u32[]{:S(2)}) %collective-permute-start.5) | collective-permute-done | bytes 65568 | tf_op jit(solution)/shard_map/ppermute | solution.py:23
  19.7 1.9 %collective-permute-start.8 = (bf16[16,2048]{1,0:T(8,128)(2,1)S(1)}, bf16[16,2048]{1,0:T(8,128)(2,1)S(1)}, u32[]{:S(2)}, u32[]{:S(2)}) collective-permute-start(bf16[16,2048]{1,0:T(8,128)(2,1)S(1)} %get-tuple-element.42.after_ref), channel_id=1, source_target_pairs={{0,8},{4,12},{8,0},{12,4},{1,9},{5,13},{9,1},{13,5},{2,10},{6,14},... | collective-permute-start | bytes 196616 | tf_op jit(solution)/shard_map/ppermute | solution.py:23
  21.6 1.8 %collective-permute-start.6 = (bf16[16,2048]{1,0:T(8,128)(2,1)S(1)}, bf16[16,2048]{1,0:T(8,128)(2,1)S(1)}, u32[]{:S(2)}, u32[]{:S(2)}) collective-permute-start(bf16[16,2048]{1,0:T(8,128)(2,1)S(1)} %get-tuple-element.42.after_ref), channel_id=1, source_target_pairs={{0,12},{4,8},{8,4},{12,0},{1,13},{5,9},{9,5},{13,1},{2,14},{6,10},... | collective-permute-start | bytes 196616 | tf_op jit(solution)/shard_map/ppermute | solution.py:23
  23.4 0.5 %collective-permute-start.7 = (bf16[16,2048]{1,0:T(8,128)(2,1)S(1)}, bf16[16,2048]{1,0:T(8,128)(2,1)S(1)}, u32[]{:S(2)}, u32[]{:S(2)}) collective-permute-start(bf16[16,2048]{1,0:T(8,128)(2,1)S(1)} %get-tuple-element.42.after_ref), channel_id=1, source_target_pairs={{0,4},{4,0},{8,12},{12,8},{1,5},{5,1},{9,13},{13,9},{2,6},{6,2},{1... | collective-permute-start | bytes 196616 | tf_op jit(solution)/shard_map/ppermute | solution.py:23
  23.9 2.8 %shard_map.91 = (bf16[1024,1024]{1,0:T(8,128)(2,1)S(1)}, bf16[1024,2048]{1,0:T(8,128)(2,1)S(1)}, bf16[1024,1024]{1,0:T(8,128)(2,1)S(1)}, bf16[1024,1024]{1,0:T(8,128)(2,1)S(1)}, f32[8,128]{1,0:T(8,128)S(1)}) custom-call(bf16[2048,8192]{1,0:T(8,128)(2,1)} %matrix_ref.5, bf16[16,2048]{1,0:T(8,128)(2,1)S(1)} %get-tuple-element.42.after_ref, ...), custom_call_target="tpu_custom_call" | custom-call | tf_op jit(solution)/shard_map/pallas_call | solution.py:434
  26.8 0.0 collective-permute-done.8.refs_1_
  26.8 1.5 %shard_map.93.sum_ref = f32[16,2048]{1,0:T(8,128)S(1)} custom-call(bf16[16,2048]{1,0:T(8,128)(2,1)S(1)} %shard_map.92.low_ref, bf16[1024,2048]{1,0:T(8,128)(2,1)S(1)} %get-tuple-element.50.lower_ref, bf16[1024,1024]{1,0:T(8,128)(2,1)S(1)} %get-tuple-element.51.upper_ref, bf16[1024,1024]{1,0:T(8,128)(2,1)S(1)} %get-tuple-element.52.last_ref), custom_call_target="tpu_custom_call" | custom-call | tf_op jit(solution)/shard_map/pallas_call | solution.py:489
  28.3 0.0 collective-permute-done.6.refs_0_
  28.3 0.1 collective-permute-done.7.refs_1_
  28.4 1.2 %shard_map.94 = (f32[8,2048]{1,0:T(8,128)S(1)}, f32[8,2048]{1,0:T(8,128)S(1)}) custom-call(bf16[16,2048]{1,0:T(8,128)(2,1)S(1)} %shard_map.90.low_ref, bf16[1024,2048]{1,0:T(8,128)(2,1)S(1)} %get-tuple-element.43.lower_ref, bf16[1024,1024]{1,0:T(8,128)(2,1)S(1)} %get-tuple-element.46.upper_ref, bf16[1024,1024]{1,0:T(8,128)(2,1)S(1)} %get-tuple-element.47.last_ref, ...), custom_call_target="tpu_custom_call" | custom-call | tf_op jit(solution)/shard_map/pallas_call | solution.py:497
  29.6 0.0 collective-permute-start.9
  29.6 1.3 %collective-permute-done.9 = f32[8,2048]{1,0:T(8,128)S(1)} collective-permute-done((f32[8,2048]{1,0:T(8,128)S(1)}, f32[8,2048]{1,0:T(8,128)S(1)}, u32[]{:S(2)}, u32[]{:S(2)}) %collective-permute-start.9) | collective-permute-done | bytes 65568 | tf_op jit(solution)/shard_map/ppermute | solution.py:23
  30.9 0.6 %add_convert_fusion = bf16[8,2048]{1,0:T(8,128)(2,1)} fusion(f32[8,2048]{1,0:T(8,128)S(1)} %get-tuple-element.53, f32[8,2048]{1,0:T(8,128)S(1)} %collective-permute-done.9), kind=kLoop, calls=%fused_computation | loop fusion | flops 32768 | bytes 163840 | tf_op jit(solution)/shard_map/convert_element_type | solution.py:504
  (4 shorter events, 0.1 us)
Async XLA Ops:
  0.0 11.4 %collective-permute-start.3 = (bf16[128,1024]{1,0:T(8,128)(2,1)}, bf16[128,1024]{1,0:T(8,128)(2,1)S(1)}, u32[]{:S(2)}, u32[]{:S(2)}) collective-permute-start(bf16[128,1024]{1,0:T(8,128)(2,1)} %refs_0_.1), channel_id=1, source_target_pairs={{0,4},{4,0},{8,12},{12,8},{1,5},{5,1},{9,13},{13,9},{2,6},{6,2},{1... | collective-permute-start | bytes 786440 | tf_op jit(solution)/shard_map/ppermute | solution.py:23
  3.8 9.3 %collective-permute-start = (bf16[1,128,128]{2,1,0:T(8,128)(2,1)S(1)}, bf16[1,128,128]{2,1,0:T(8,128)(2,1)S(1)}, u32[]{:S(2)}, u32[]{:S(2)}) collective-permute-start(bf16[1,128,128]{2,1,0:T(8,128)(2,1)S(1)} %shard_map.82.refs_0_), channel_id=1, source_target_pairs={{0,12},{4,8},{8,4},{12,0},{1,13},{5,9},{9,5},{13,1},{2,14},{6,10},... | collective-permute-start | bytes 98312 | tf_op jit(solution)/shard_map/ppermute | solution.py:23
  6.4 6.8 %collective-permute-start.1 = (bf16[1,128,128]{2,1,0:T(8,128)(2,1)S(1)}, bf16[1,128,128]{2,1,0:T(8,128)(2,1)S(1)}, u32[]{:S(2)}, u32[]{:S(2)}) collective-permute-start(bf16[1,128,128]{2,1,0:T(8,128)(2,1)S(1)} %shard_map.82.refs_0_), channel_id=1, source_target_pairs={{0,8},{4,12},{8,0},{12,4},{1,9},{5,13},{9,1},{13,5},{2,10},{6,14},... | collective-permute-start | bytes 98312 | tf_op jit(solution)/shard_map/ppermute | solution.py:23
  6.6 6.6 %collective-permute-start.2 = (bf16[1,128,128]{2,1,0:T(8,128)(2,1)S(1)}, bf16[1,128,128]{2,1,0:T(8,128)(2,1)S(1)}, u32[]{:S(2)}, u32[]{:S(2)}) collective-permute-start(bf16[1,128,128]{2,1,0:T(8,128)(2,1)S(1)} %shard_map.82.refs_0_), channel_id=1, source_target_pairs={{0,4},{4,0},{8,12},{12,8},{1,5},{5,1},{9,13},{13,9},{2,6},{6,2},{1... | collective-permute-start | bytes 98312 | tf_op jit(solution)/shard_map/ppermute | solution.py:23
  13.9 1.4 %collective-permute-start.4 = (bf16[32,2048]{1,0:T(8,128)(2,1)S(1)}, bf16[32,2048]{1,0:T(8,128)(2,1)S(1)}, u32[]{:S(2)}, u32[]{:S(2)}) collective-permute-start(bf16[32,2048]{1,0:T(8,128)(2,1)S(1)} %shard_map.86), channel_id=1, source_target_pairs={{0,1},{1,0},{2,3},{3,2},{4,5},{5,4},{6,7},{7,6},{8,9},{9,8},{10,11... | collective-permute-start | bytes 393224 | tf_op jit(solution)/shard_map/ppermute | solution.py:23
  15.4 4.3 %collective-permute-start.5 = (bf16[16,2048]{1,0:T(8,128)(2,1)S(1)}, bf16[16,2048]{1,0:T(8,128)(2,1)S(1)}, u32[]{:S(2)}, u32[]{:S(2)}) collective-permute-start(bf16[16,2048]{1,0:T(8,128)(2,1)S(1)} %get-tuple-element.38.after_ref), channel_id=1, source_target_pairs={{0,2},{1,3},{2,0},{3,1},{4,6},{5,7},{6,4},{7,5},{8,10},{9,11},{10,... | collective-permute-start | bytes 196616 | tf_op jit(solution)/shard_map/ppermute | solution.py:23
  19.7 7.1 %collective-permute-start.8 = (bf16[16,2048]{1,0:T(8,128)(2,1)S(1)}, bf16[16,2048]{1,0:T(8,128)(2,1)S(1)}, u32[]{:S(2)}, u32[]{:S(2)}) collective-permute-start(bf16[16,2048]{1,0:T(8,128)(2,1)S(1)} %get-tuple-element.42.after_ref), channel_id=1, source_target_pairs={{0,8},{4,12},{8,0},{12,4},{1,9},{5,13},{9,1},{13,5},{2,10},{6,14},... | collective-permute-start | bytes 196616 | tf_op jit(solution)/shard_map/ppermute | solution.py:23
  21.6 6.6 %collective-permute-start.6 = (bf16[16,2048]{1,0:T(8,128)(2,1)S(1)}, bf16[16,2048]{1,0:T(8,128)(2,1)S(1)}, u32[]{:S(2)}, u32[]{:S(2)}) collective-permute-start(bf16[16,2048]{1,0:T(8,128)(2,1)S(1)} %get-tuple-element.42.after_ref), channel_id=1, source_target_pairs={{0,12},{4,8},{8,4},{12,0},{1,13},{5,9},{9,5},{13,1},{2,14},{6,10},... | collective-permute-start | bytes 196616 | tf_op jit(solution)/shard_map/ppermute | solution.py:23
  23.4 5.0 %collective-permute-start.7 = (bf16[16,2048]{1,0:T(8,128)(2,1)S(1)}, bf16[16,2048]{1,0:T(8,128)(2,1)S(1)}, u32[]{:S(2)}, u32[]{:S(2)}) collective-permute-start(bf16[16,2048]{1,0:T(8,128)(2,1)S(1)} %get-tuple-element.42.after_ref), channel_id=1, source_target_pairs={{0,4},{4,0},{8,12},{12,8},{1,5},{5,1},{9,13},{13,9},{2,6},{6,2},{1... | collective-permute-start | bytes 196616 | tf_op jit(solution)/shard_map/ppermute | solution.py:23
  29.6 1.3 %collective-permute-start.9 = (f32[8,2048]{1,0:T(8,128)S(1)}, f32[8,2048]{1,0:T(8,128)S(1)}, u32[]{:S(2)}, u32[]{:S(2)}) collective-permute-start(f32[8,2048]{1,0:T(8,128)S(1)} %get-tuple-element.54), channel_id=1, source_target_pairs={{0,1},{1,0},{2,3},{3,2},{4,5},{5,4},{6,7},{7,6},{8,9},{9,8},{10,11... | collective-permute-start | bytes 196616 | tf_op jit(solution)/shard_map/ppermute | solution.py:23
